TPU v7x, 32 devices: a whole 2x2x4 slice. The times are simulated.
32 devices in a mesh: groups: 2 (over y), sec: 4 (over z), tile: 2 (over x), row: 2 (over core).
Axes of the slice: x: 2, y: 2, z: 4, core: 2. Of those that a mesh axis runs over, the one named last changes fastest.
Arguments:
- section_pixels: float32 [8, 512, 4096], P(('groups', 'sec'), ('tile', 'row')), parts along dimension 0, may hold values from -40 to 40
- jitter_index: int32 [8, 512], P(('groups', 'sec'), ('tile', 'row')), parts along dimension 0, may hold values from 0 to 7
- drift_list: int32 [8, 4, 8, 3], P(('groups', 'sec')), parts along dimension 0, may hold values from 0 to 31, as said below
- blend_weight: float32 [8, 4, 8], P(('groups', 'sec')), parts along dimension 0, may hold values from 0.5 to 2
- patch_col: int32 [4, 8], P(('tile', 'row'), 'groups'), parts along dimension 1, may hold values from 0 to 896
Outputs:
- jitter_phase: float32 [8, 512], P(('groups', 'sec'), ('tile', 'row')), parts along dimension 0
- surfaces: float32 [6, 4, 4, 128, 128], P('groups', ('tile', 'row'), 'sec'), parts along dimension 0
There are 2 independent parts, one for each index of `groups`. A program takes and returns all parts, laid end to end along the dimension named above; each array names one. Nothing has to cross between parts.
Inputs may be any that keep to these rules, and one draw needn't show every extreme that they name: `drift_list`: entry [s, j, k] names a block of band j (distinct over k), the band that owns its target, and the target block. No band sends more than 2 blocks to one owner, and in every section one owner receives exactly 2 blocks from every band.
All inputs are finite; a program needn't handle non-finite values.
Results may differ from a plain program's by a relative error of at most 0.0065.
Values may be sent and summed in bfloat16 or wider, within the bound.
No kernel may reach another device: no remote copies, remote signals or barrier semaphores. Data moves between devices by JAX's collectives and lax.ppermute only.
A program may use at most 64 MiB of HBM per device.

v0:
```python
import math

import jax
import jax.numpy as jnp
from jax import lax
from jax.sharding import PartitionSpec as P

SEG = 512
PATCH = 128
BLOCK = 128
JMAX = 8
OV = 8
CAP = 2


def shifted(block, axis, distance):
    devices = range(lax.axis_size(axis))
    route = [(i - distance, i) for i in devices if i - distance in devices]
    return lax.ppermute(block, axis, route)


def dft_tables(length):
    indices = jnp.arange(length, dtype=jnp.int32)
    products = indices[:, None] * indices[None, :] % length
    angles = products.astype(jnp.float32) * (2.0 * math.pi / length)
    return (jnp.cos(angles), jnp.sin(angles))


def align_rows(pixels, delays):
    row_width = pixels.shape[1]
    padded = jnp.pad(pixels, ((0, 0), (0, JMAX)))
    aligned = jnp.zeros_like(pixels)
    for shift_by in range(JMAX):
        aligned = aligned + jnp.where(
            delays[:, None] == shift_by, padded[:, shift_by : shift_by + row_width], 0.0
        )
    return aligned


def row_spectra(rows):
    row_count, row_width = rows.shape
    cosine_table, sine_table = dft_tables(SEG)
    dft_table = jnp.concatenate([cosine_table, -sine_table], 1)
    spectra = jnp.dot(
        rows.reshape(row_count * (row_width // SEG), SEG),
        dft_table,
        precision=lax.Precision.HIGHEST,
        preferred_element_type=jnp.float32,
    )
    spectra = spectra.reshape(row_count, row_width // SEG, 2 * SEG)
    return (spectra[..., :SEG], spectra[..., SEG:])


def jitter_estimate(now_real, now_imag, before_real, before_imag):
    indices = jnp.arange(SEG, dtype=jnp.int32)
    weights = jnp.sin(indices.astype(jnp.float32) * (2.0 * math.pi / SEG))
    cross_term = now_imag * before_real - now_real * before_imag
    numerator = jnp.mean(weights * cross_term, axis=(1, 2))
    power_sum = 0.5 * (
        now_real * now_real
        + now_imag * now_imag
        + before_real * before_real
        + before_imag * before_imag
    )
    return numerator / (jnp.mean(power_sum, axis=(1, 2)) + 1e-05)


def correct_rows(aligned, jitter):
    padded = jnp.pad(aligned, ((0, 0), (1, 1)))
    slopes = 0.5 * (padded[:, 2:] - padded[:, :-2])
    return (aligned - jitter[:, None] * slopes).astype(jnp.bfloat16)


def left_mul(matrix, batch):
    return jnp.einsum("ij,...jk->...ik", matrix, batch, precision=lax.Precision.HIGHEST)


def right_mul(batch, matrix):
    return jnp.einsum("...ij,jk->...ik", batch, matrix, precision=lax.Precision.HIGHEST)


def correlate(patches):
    side = patches.shape[-1]
    cosine_table, sine_table = dft_tables(side)
    values = patches.astype(jnp.float32)
    first_cos = right_mul(values, cosine_table)
    first_sin = right_mul(values, sine_table)
    freq_real = left_mul(cosine_table, first_cos) - left_mul(sine_table, first_sin)
    freq_imag = -(left_mul(sine_table, first_cos) + left_mul(cosine_table, first_sin))
    cross_real = freq_real[:-1] * freq_real[1:] + freq_imag[:-1] * freq_imag[1:]
    cross_imag = freq_imag[:-1] * freq_real[1:] - freq_real[:-1] * freq_imag[1:]
    magnitude = jnp.sqrt(cross_real * cross_real + cross_imag * cross_imag)
    damping = 0.5 * jnp.mean(magnitude, axis=(-2, -1), keepdims=True) + 1e-06
    scaled = 1.0 / (magnitude + damping)
    damped_real = cross_real * scaled
    damped_imag = cross_imag * scaled
    back_real = right_mul(damped_real, cosine_table) - right_mul(damped_imag, sine_table)
    back_imag = right_mul(damped_real, sine_table) + right_mul(damped_imag, cosine_table)
    return (left_mul(cosine_table, back_real) - left_mul(sine_table, back_imag)) / side


def per_device(section_pixels, jitter_index, drift_list, blend_weight, patch_col):
    pixels = section_pixels[0]
    row_count, row_width = pixels.shape
    aligned = align_rows(pixels, jitter_index[0])
    above_row = shifted(aligned[row_count - 1 :], ("tile", "row"), 1)
    now_real, now_imag = row_spectra(aligned)
    top_real, top_imag = row_spectra(above_row)
    before_real = jnp.concatenate([top_real, now_real[:-1]], 0)
    before_imag = jnp.concatenate([top_imag, now_imag[:-1]], 0)
    jitter = jitter_estimate(now_real, now_imag, before_real, before_imag)
    corrected = correct_rows(aligned, jitter)
    owners = lax.axis_size("tile") * lax.axis_size("row")
    owner_id = lax.axis_index("tile") * lax.axis_size("row") + lax.axis_index("row")
    blocks_across = row_width // BLOCK
    band_rows = row_count // BLOCK
    total_blocks = band_rows * blocks_across
    drifts = drift_list[0]
    weights = blend_weight[0]
    positions = jnp.arange(OV, dtype=jnp.int32)
    earlier = positions[None, :] < positions[:, None]
    same_owner = drifts[:, :, 1][:, :, None] == drifts[:, :, 1][:, None, :]
    slot_ids = jnp.sum((same_owner & earlier[None]).astype(jnp.int32), axis=2)
    my_list = lax.dynamic_index_in_dim(drifts, owner_id, 0, keepdims=False)
    my_slots = lax.dynamic_index_in_dim(slot_ids, owner_id, 0, keepdims=False)

    def cut_block(block_id):
        return lax.dynamic_slice(
            corrected,
            (block_id // blocks_across * BLOCK, block_id % blocks_across * BLOCK),
            (BLOCK, BLOCK),
        )

    sources = jax.vmap(cut_block)(my_list[:, 0])
    outgoing = (
        jnp.zeros((owners * CAP, BLOCK, BLOCK), jnp.bfloat16)
        .at[my_list[:, 1] * CAP + my_slots]
        .set(sources)
    )
    arrived = lax.all_to_all(
        outgoing.reshape(owners, CAP, BLOCK, BLOCK),
        ("tile", "row"),
        split_axis=0,
        concat_axis=0,
        tiled=True,
    )
    arrived = arrived.reshape(owners * CAP, BLOCK, BLOCK)
    to_me = (drifts[:, :, 1] == owner_id).astype(jnp.float32) * weights
    slot_index = (jnp.arange(owners, dtype=jnp.int32)[:, None] * CAP + slot_ids).reshape(-1)
    slot_onehot = (
        slot_index[:, None] == jnp.arange(owners * CAP, dtype=jnp.int32)[None, :]
    ).astype(jnp.float32)
    block_onehot = (
        jnp.arange(total_blocks, dtype=jnp.int32)[:, None] == drifts[:, :, 2].reshape(-1)[None, :]
    ).astype(jnp.float32)
    block_onehot = block_onehot * to_me.reshape(-1)[None, :]
    mixing = jnp.dot(
        block_onehot,
        slot_onehot,
        precision=lax.Precision.HIGHEST,
        preferred_element_type=jnp.float32,
    )
    incoming = jnp.einsum(
        "nm,mxy->nxy", mixing, arrived.astype(jnp.float32), precision=lax.Precision.HIGHEST
    )
    incoming = (
        incoming.reshape(band_rows, blocks_across, BLOCK, BLOCK)
        .transpose(0, 2, 1, 3)
        .reshape(row_count, row_width)
    )
    denominator = (1.0 + jnp.sum(block_onehot, axis=1)).reshape(band_rows, blocks_across)
    denominator = jnp.repeat(jnp.repeat(denominator, BLOCK, 0), BLOCK, 1)
    montage = ((corrected.astype(jnp.float32) + incoming) / denominator).astype(jnp.bfloat16)
    patch_rows = row_count // PATCH
    offsets = patch_col[0]
    slab_count = lax.axis_size("sec")
    slab_width = row_width // slab_count
    band_grid = montage.reshape(patch_rows, PATCH, slab_count, slab_width)
    picked = jax.vmap(
        lambda column_piece, start_col: lax.dynamic_slice_in_dim(column_piece, start_col, PATCH, 2),
        in_axes=(2, 0),
        out_axes=2,
    )(band_grid, offsets)
    outbound = picked.reshape(1, patch_rows, PATCH, slab_count * PATCH)
    surfaces = correlate(lax.all_to_all(outbound, "sec", split_axis=3, concat_axis=0, tiled=True))
    return (jitter[None, :], surfaces[:, :, None])


def solution(mesh):
    in_specs = (
        P(("groups", "sec"), ("tile", "row"), None),
        P(("groups", "sec"), ("tile", "row")),
        P(("groups", "sec"), None, None, None),
        P(("groups", "sec"), None, None),
        P(("tile", "row"), "groups"),
    )
    out_specs = (
        P(("groups", "sec"), ("tile", "row")),
        P("groups", ("tile", "row"), "sec", None, None),
    )
    return jax.shard_map(
        per_device, mesh=mesh, in_specs=in_specs, out_specs=out_specs, check_vma=False
    )
```

profile of v0, /device:TPU:0, one launch (start us, length us, event | category | flops | bytes accessed | tf_op | source)
XLA Modules:
  0.0 104.6 jit_solution(3331705832865443064)
XLA Ops:
  1.3 2.9 %copy.89 = f32[1,128,4096]{1,2,0:T(8,128)} copy(f32[1,128,4096]{2,1,0:T(8,128)} %param.5) | data formatting | bytes 4194304 | tf_op args[0]
  4.2 9.1 %select_add_fusion = f32[128,4096]{0,1:T(8,128)S(1)} fusion(f32[128,4096]{0,1:T(8,128)} %bitcast.149, pred[128]{0:T(512)(128)(4,1)S(1)} %get-tuple-element.72, pred[128]{0:T(512)(128)(4,1)S(1)} %get-tuple-element.73, pred[128]{0:T(512)(128)(4,1)S(1)} %get-tuple-element.67, pred[128]{0:T(512)(128)(4,1)S(1)} %get-tuple-element.68, ...), kind=kLoop, calls=%fused_computation.17 | loop fusion | flops 7864320 | bytes 4195328 | tf_op jit(solution)/shard_map/add | solution.py:34
  13.3 2.0 %slice.124 = f32[1,4096]{0,1:T(8,128)} slice(f32[128,4096]{0,1:T(8,128)S(1)} %select_add_fusion), slice={[127:128], [0:4096]} | slice | bytes 32768 | tf_op jit(solution)/shard_map/slice | solution.py:106
  15.3 2.2 %copy.91 = f32[1,4096]{1,0:T(1,128)S(1)} copy(f32[1,4096]{0,1:T(8,128)} %slice.124) | data formatting | bytes 32768 | tf_op jit(solution)/shard_map/slice | solution.py:106
  17.5 2.4 %collective-permute-start = (f32[1,4096]{1,0:T(1,128)S(1)}, f32[1,4096]{1,0:T(1,128)S(1)}, u32[]{:S(2)}, u32[]{:S(2)}) collective-permute-start(f32[1,4096]{1,0:T(1,128)S(1)} %copy.91), channel_id=1, source_target_pairs={{0,1},{1,2},{2,3},{4,5},{5,6},{6,7},{8,9},{9,10},{10,11},{12,13},{... | collective-permute-start | bytes 49160 | tf_op jit(solution)/shard_map/ppermute | solution.py:19
  20.0 5.3 %sine_negate_fusion = (f32[512,512]{1,0:T(8,128)S(1)}, f32[512,512]{1,0:T(8,128)}) fusion(), kind=kLoop, calls=%fused_computation.37 | loop fusion | flops 3932160 | bytes 2097152 | tf_op jit(solution)/shard_map/neg | solution.py:43
  26.4 8.0 %fusion.2 = f32[128,8,1024]{2,0,1:T(8,128)S(1)} fusion(f32[128,8,512]{0,2,1:T(8,128)S(1)} %bitcast.148, f32[512,512]{1,0:T(8,128)S(1)} %get-tuple-element.74, f32[512,512]{1,0:T(8,128)} %get-tuple-element.75), kind=kOutput, calls=%fused_computation.11 | convolution fusion | flops 6442975232 | bytes 8388608 | tf_op jit(solution)/shard_map/dot_general | solution.py:44
  34.4 3.0 %fusion.129 = (f32[127,8,512]{2,0,1:T(8,128)}, f32[127,8,512]{2,0,1:T(8,128)}) fusion(f32[128,8,1024]{2,0,1:T(8,128)S(1)} %fusion.2), kind=kLoop, calls=%fused_computation.186 | loop fusion | bytes 8323072 | tf_op jit(solution)/shard_map/slice | solution.py:109
  37.4 0.8 copy-done
  39.5 2.5 %fusion.4 = f32[8,1024]{1,0:T(8,128)S(1)} fusion(f32[8,512]{1,0:T(8,128)S(1)} %reshape.280, f32[512,512]{1,0:T(8,128)S(1)} %get-tuple-element.74, f32[512,512]{1,0:T(8,128)} %get-tuple-element.75), kind=kOutput, calls=%fused_computation.18 | convolution fusion | flops 50855936 | bytes 2146304 | tf_op jit(solution)/shard_map/dot_general | solution.py:44
  42.0 4.4 %multiply_reduce_fusion.1 = (f32[128]{0:T(128)S(1)}, f32[128]{0:T(128)S(1)}) fusion(f32[128,8,1024]{2,0,1:T(8,128)} %copy-done, f32[127,8,512]{2,0,1:T(8,128)} %get-tuple-element.60, f32[1,8,512]{2,0,1:T(1,128)S(1)} %get-tuple-element.62, f32[127,8,512]{2,0,1:T(8,128)S(1)} %copy-done.1, f32[1,8,512]{2,0,1:T(1,128)S(1)} %get-tuple-element.61, ...), kind=kLoop, calls=%fused_computation.16 | loop fusion | flops 8388352 | bytes 8391680 | tf_op jit(solution)/shard_map/reduce_sum | solution.py:58
  47.5 12.3 %while.1 = (s32[]{:T(128)}, bf16[128,4096]{0,1:T(8,128)(2,1)S(1)}, s32[8,2]{0,1:T(2,128)S(1)}, bf16[8,128,128]{2,1,0:T(8,128)(2,1)S(1)}, s32[]{:T(128)}) while((s32[]{:T(128)}, bf16[128,4096]{0,1:T(8,128)(2,1)S(1)}, s32[8,2]{0,1:T(2,128)S(1)}, bf16[8,128,128]{2,1,0:T(8,128)(2,1)S(1)}, s32[]{:T(128)}) %tuple.48), condition=%wide.while_cond, body=%wide.while_body.sunk | while | flops 2 | bytes 196713 | solution.py:128
  48.1 0.7 constant_dynamic-slice_fusion.6
  49.7 0.7 constant_dynamic-slice_fusion.6
  51.2 0.7 constant_dynamic-slice_fusion.6
  54.3 0.7 constant_dynamic-slice_fusion.6
  59.8 1.0 scatter_fusion
  60.8 1.0 copy.93
  61.7 3.9 %all-to-all-start = ((bf16[4,2,128,128]{3,1,2,0:T(2,128)(2,1)}), bf16[4,2,128,128]{3,1,2,0:T(2,128)(2,1)S(1)}, u32[]{:S(2)}, u32[]{:S(2)}) async-start(bf16[4,2,128,128]{3,1,2,0:T(2,128)(2,1)} %copy.93), calls=%async_computation | async-start | bytes 524288 | tf_op jit(solution)/shard_map/all_to_all | solution.py:140
  65.6 6.0 %all-to-all-done = bf16[4,2,128,128]{3,1,2,0:T(2,128)(2,1)S(1)} async-done(((bf16[4,2,128,128]{3,1,2,0:T(2,128)(2,1)}), bf16[4,2,128,128]{3,1,2,0:T(2,128)(2,1)S(1)}, u32[]{:S(2)}, u32[]{:S(2)}) %all-to-all-start) | async-done | bytes 262176 | tf_op jit(solution)/shard_map/all_to_all | solution.py:140
  71.8 2.4 %convolution_bitcast_fusion = f32[1,128,32,128]{3,2,1,0:T(8,128)} fusion(f32[32,8,1]{0,1,2:T(8,128)S(1)} %convolution_bitcast_fusion.1, bf16[8,128,128]{2,0,1:T(8,128)(2,1)S(1)} %bitcast.153), kind=kOutput, calls=%fused_computation.19 | convolution fusion | flops 50331648 | bytes 2360320 | tf_op jit(solution)/shard_map/nm,mxy->nxy/dot_general | solution.py:163
  74.2 3.0 %copy.120 = f32[1,128,32,128]{1,3,2,0:T(8,128)} copy(f32[1,128,32,128]{3,2,1,0:T(8,128)} %convolution_bitcast_fusion) | data formatting | bytes 4194304 | tf_op jit(solution)/shard_map/reshape | solution.py:169
  77.2 2.1 %fusion.1 = bf16[128,4096]{0,1:T(8,128)(2,1)S(1)} fusion(f32[1,128,32,128]{1,3,2,0:T(8,128)} %copy.120, f32[4096]{0:T(1024)S(1)} %broadcast_bitcast_fusion, f32[128,4096]{0,1:T(8,128)S(1)} %select_add_fusion, f32[128]{0:T(128)S(1)} %get-tuple-element.57), kind=kLoop, calls=%fused_computation.10 | loop fusion | flops 4194304 | bytes 5259776 | tf_op jit(solution)/shard_map/convert_element_type | solution.py:173
  79.3 1.6 %copy.127 = bf16[1,128,4,1024]{1,0,2,3:T(2,128)(2,1)S(1)} copy(bf16[1,128,4,1024]{1,3,2,0:T(8,128)(2,1)S(1)} %bitcast.151) | data formatting | bytes 2097152 | tf_op jit(solution)/shard_map/reshape | solution.py:178
  80.9 1.2 %gather_fusion = bf16[4,128,128]{1,0,2:T(4,128)(2,1)S(1)} fusion(bf16[4,1,128,1024]{2,1,0,3:T(2,128)(2,1)S(1)} %bitcast.150, s32[4]{0:T(128)S(1)} %fusion.77), kind=kCustom, calls=%fused_computation | custom fusion | bytes 262208 | tf_op jit(solution)/shard_map/vmap()/gather | solution.py:180
  82.8 1.4 %reduce.5 = bf16[512,128]{1,0:T(8,128)(2,1)S(1)} reduce(bf16[512,1,1,128]{3,2,1,0:T(2,128)(2,1)S(1)} %bitcast.154, bf16[]{:T(256)} %broadcast.413), dimensions={1,2}, to_apply=%bitcast.142.reduce_sub_computation | reduce | bytes 262146
  84.3 11.1 %all_to_all.20 = bf16[4,2,8192]{2,1,0:T(2,128)(2,1)S(1)} all-to-all(bf16[4,2,8192]{2,1,0:T(2,128)(2,1)S(1)} %reshape.338), channel_id=1, replica_groups=mesh['groups'=2,'sec'=4,'tile'=2,'row'=2] {'sec'}, dimensions={0} | all-to-all | bytes 262144 | tf_op jit(solution)/shard_map/all_to_all | solution.py:185
  99.5 0.8 fusion.19
  100.2 0.7 fusion.21
  101.0 0.7 convolution_add_fusion.1
  101.7 0.8 convolution_subtract_fusion.2
  103.8 0.8 copy.110
  (96 shorter events, 19.7 us)
Async XLA Ops:
  15.3 10.0 %copy-start.2 = (s32[1,4,8,3]{2,1,3,0:T(4,128)S(1)}, s32[1,4,8,3]{2,1,3,0:T(4,128)}, u32[]{:S(2)}) copy-start(s32[1,4,8,3]{2,1,3,0:T(4,128)} %param.7) | copy-start | bytes 1156
  15.3 10.1 %copy-start.3 = (f32[1,4,8]{2,1,0:T(4,128)S(1)}, f32[1,4,8]{2,1,0:T(4,128)}, u32[]{:S(2)}) copy-start(f32[1,4,8]{2,1,0:T(4,128)} %param.8) | copy-start | bytes 388
  17.5 20.7 %collective-permute-start = (f32[1,4096]{1,0:T(1,128)S(1)}, f32[1,4096]{1,0:T(1,128)S(1)}, u32[]{:S(2)}, u32[]{:S(2)}) collective-permute-start(f32[1,4096]{1,0:T(1,128)S(1)} %copy.91), channel_id=1, source_target_pairs={{0,1},{1,2},{2,3},{4,5},{5,6},{6,7},{8,9},{9,10},{10,11},{12,13},{... | collective-permute-start | bytes 49160 | tf_op jit(solution)/shard_map/ppermute | solution.py:19
  34.4 3.8 %copy-start = (f32[128,8,1024]{2,0,1:T(8,128)}, f32[128,8,1024]{2,0,1:T(8,128)S(1)}, u32[]{:S(2)}) copy-start(f32[128,8,1024]{2,0,1:T(8,128)S(1)} %fusion.2) | copy-start | bytes 12582916
  39.4 2.5 %copy-start.1 = (f32[127,8,512]{2,0,1:T(8,128)S(1)}, f32[127,8,512]{2,0,1:T(8,128)}, u32[]{:S(2)}) copy-start(f32[127,8,512]{2,0,1:T(8,128)} %get-tuple-element.59) | copy-start | bytes 6242308
  47.4 18.2 %copy-start.4 = (s32[1,4]{1,0:T(1,128)S(1)}, s32[1,4]{1,0:T(1,128)}, u32[]{:S(2)}) copy-start(s32[1,4]{1,0:T(1,128)} %param.9) | copy-start | bytes 52
  61.7 9.9 %all-to-all-start = ((bf16[4,2,128,128]{3,1,2,0:T(2,128)(2,1)}), bf16[4,2,128,128]{3,1,2,0:T(2,128)(2,1)S(1)}, u32[]{:S(2)}, u32[]{:S(2)}) async-start(bf16[4,2,128,128]{3,1,2,0:T(2,128)(2,1)} %copy.93), calls=%async_computation | async-start | bytes 524288 | tf_op jit(solution)/shard_map/all_to_all | solution.py:140
where the time goes:
time: 105 us
  local copies, waits for them, and re-layouts  33.7 us (32%)
  other arithmetic  25.4 us (24%)
  matrix products  20.9 us (20%)
  blocking collectives  11.1 us (11%)
  starting transfers between devices  6.23 us (6%)
  waiting for transfers between devices  6.03 us (6%)
    gather x40, local copies, waits for them, and re-layouts  12 us
    all_to_all x1, blocking collectives, per_device(): lax.all_to_all(outbound, 'sec', split_axis=3, concat_axis=0, tiled=True)  11.1 us
    dot_general x2, matrix products, row_spectra(): jnp.dot(rows.reshape(row_count * (row_width // SEG), SEG), dft_table, pre...  10.5 us
    add x1, other arithmetic, align_rows(): aligned + jnp.where(delays[:, None] == shift_by, padded[:, shift_by:shift...  9.08 us
    all_to_all x1, waiting for transfers between devices, per_device(): lax.all_to_all(outgoing.reshape(owners, CAP, BLOCK, BLOCK), ('tile', 'row...  6.03 us
    unnamed x17, local copies, waits for them, and re-layouts  5.3 us
    neg x1, other arithmetic, row_spectra(): dft_table = jnp.concatenate([cosine_table, -sine_table], 1)  5.29 us
    reduce_sum x1, other arithmetic, jitter_estimate(): numerator = jnp.mean(weights * cross_term, axis=(1, 2))  4.36 us
  transfers between devices with their start and end apart: 2, of which 1 were waited for; matrix products, arithmetic and copies ran while one was open for 17% of the time, Pallas kernels for 0%

commit v1 on v0

v1 whole, which is shorter than its diff:
```python
import functools
import math

import jax
import jax.numpy as jnp
import numpy as np
from jax import lax
from jax.experimental import pallas as pl
from jax.experimental.pallas import tpu as pltpu
from jax.sharding import PartitionSpec as P

SEG = 512
PATCH = 128
BLOCK = 128
CAP = 2
SUB = 8
BANDS = ("tile", "row")


def is_pow2(n):
    return n & (n - 1) == 0


def target(me, k, n):
    return me ^ k if is_pow2(n) else (me + k) % n


def origin(me, k, n):
    return me ^ k if is_pow2(n) else (me + n - k) % n


def send(x, axis, k, n):
    return lax.ppermute(x, axis, [(i, target(i, k, n)) for i in range(n)])


def has_tail(k, n):
    return any(target(i, k, n) == (i + 1) % n for i in range(n))


def find_slots(drift, band, owner, count):
    place = [jnp.int32(0)] * CAP
    found = jnp.int32(0)
    for p in range(count):
        hit = drift[0, band, p, 1] == owner
        for c in range(CAP):
            place[c] = jnp.where(hit & (found == c), p, place[c])
        found = found + jnp.where(hit, 1, 0)
    return place, found


def window_place(pcol, q, slab):
    start = q * slab + pcol[0, q]
    return start >> 7, start & (BLOCK - 1)


def split(x):
    high = x.astype(jnp.bfloat16)
    return high, (x - high.astype(jnp.float32)).astype(jnp.bfloat16)


def front_kernel(owners, secs, chunks, delay, drift, pcol, pixels, *refs):
    jitter_out, strips, first_out = refs[:3]
    messages = refs[3 : 3 + owners]
    raw, shifted, slope, wide, sums, loaded = refs[3 + owners :]
    rows, width = pixels.shape
    blocks = width // BLOCK
    per = rows // chunks
    band = lax.axis_index(BANDS)
    sec = lax.axis_index("sec")

    def load(i):
        at = pl.ds(i * per, per)
        return pltpu.make_async_copy(pixels.at[at, :], raw.at[at, :], loaded.at[i])

    for i in range(chunks):
        load(i).start()
    wide[...] = jnp.broadcast_to(delay[...], (rows, rows)).T
    shifted[:, 0:SUB, :] = jnp.zeros((blocks, SUB, BLOCK), jnp.float32)
    lane = lax.broadcasted_iota(jnp.int32, (SUB, BLOCK), 1)
    sub = lax.broadcasted_iota(jnp.int32, (SUB, BLOCK), 0)
    first_lane = lane == 0
    last_lane = lane == BLOCK - 1
    first_sub = sub == 0
    seg = SEG // BLOCK

    def eight_rows(g, _):
        at = pl.multiple_of(g * SUB, SUB)
        delays = wide[pl.ds(at, SUB), :]
        moved = lane + delays
        index = moved & (BLOCK - 1)
        near = moved < BLOCK
        picked = [
            jnp.take_along_axis(
                raw[pl.ds(at, SUB), v * BLOCK : (v + 1) * BLOCK],
                index,
                axis=1,
                mode="promise_in_bounds",
            )
            for v in range(blocks)
        ]
        picked.append(jnp.zeros((SUB, BLOCK), jnp.float32))
        x = [jnp.where(near, picked[v], picked[v + 1]) for v in range(blocks)]
        ahead = [pltpu.roll(t, BLOCK - 1, 1) for t in x]
        behind = [pltpu.roll(t, 1, 1) for t in x]
        zero = jnp.zeros((SUB, BLOCK), jnp.float32)
        cross = zero
        power = zero
        for v in range(blocks):
            nxt = ahead[v + 1] if v + 1 < blocks else zero
            prv = behind[v - 1] if v > 0 else zero
            up = jnp.where(last_lane, nxt, ahead[v])
            down = jnp.where(first_lane, prv, behind[v])
            line = up - down
            ring = line
            if v % seg == seg - 1:
                ring = jnp.where(last_lane, ahead[v + 1 - seg], ahead[v]) - down
            if v % seg == 0:
                ring = up - jnp.where(first_lane, behind[v - 1 + seg], behind[v])
            before = jnp.where(
                first_sub, shifted[v, pl.ds(at + SUB - 1, 1), :], pltpu.roll(x[v], 1, 0)
            )
            cross = cross + before * ring
            power = power + x[v] * x[v]
            shifted[v, pl.ds(at + SUB, SUB), :] = x[v]
            slope[v, pl.ds(at, SUB), :] = line
        sums[0, pl.ds(at + SUB, SUB), :] = cross
        sums[1, pl.ds(at + SUB, SUB), :] = power
        return 0

    steps = per // SUB
    for i in range(chunks):
        load(i).wait()
        lax.fori_loop(i * steps, (i + 1) * steps, eight_rows, 0)

    total_cross = jnp.sum(sums[0, SUB:, :], axis=1, keepdims=True)
    total_power = jnp.sum(sums[1, SUB:, :], axis=1, keepdims=True)
    row_index = lax.broadcasted_iota(jnp.int32, (rows, 1), 0)
    above_power = jnp.where(row_index == 0, 0.0, pltpu.roll(
        jnp.broadcast_to(total_power, (rows, BLOCK)), 1, 0))
    numerator = -jnp.where(row_index == 0, 0.0, total_cross)
    jitter = numerator / (total_power + above_power + 1e-5 * 2 * (blocks // seg))
    wide_jitter = jnp.broadcast_to(jitter, (rows, BLOCK))
    half = 0.5 * wide_jitter
    jitter_out[...] = wide_jitter.T[0:1, :]

    def corrected(n):
        return (shifted[n, SUB:, :] - half * slope[n]).astype(jnp.bfloat16)

    for v in range(blocks):
        first_out[v : v + 1, :] = shifted[v, SUB : SUB + 1, :]
        sums[0, v : v + 1, :] = shifted[v, SUB + rows - 1 : SUB + rows, :]
    first = first_out[...].astype(jnp.bfloat16)
    last, rest = split(sums[0, :blocks, :])
    count = drift.shape[2]
    for k in range(owners):
        place, _ = find_slots(drift, band, target(band, k, owners), count)
        for c in range(CAP):
            messages[k][c * BLOCK : (c + 1) * BLOCK, :] = corrected(drift[0, band, place[c], 0])
        base = CAP * BLOCK
        messages[k][base : base + blocks, :] = first
        messages[k][base + blocks : base + 2 * blocks, :] = last
        if messages[k].shape[0] > base + 2 * blocks:
            messages[k][base + 2 * blocks : base + 3 * blocks, :] = rest
    slab = width // secs
    for k in range(secs):
        n, _ = window_place(pcol, target(sec, k, secs), slab)
        strips[k, 0] = corrected(n)
        strips[k, 1] = corrected(jnp.minimum(n + 1, blocks - 1))


def row_differences(x, segmented):
    blocks = x.shape[0]
    seg = SEG // BLOCK
    lane = lax.broadcasted_iota(jnp.int32, x.shape, 1)
    block = lax.broadcasted_iota(jnp.int32, x.shape, 0)
    ahead = pltpu.roll(x, BLOCK - 1, 1)
    behind = pltpu.roll(x, 1, 1)
    last_lane = lane == BLOCK - 1
    first_lane = lane == 0
    nxt = pltpu.roll(ahead, blocks - 1, 0)
    prv = pltpu.roll(behind, 1, 0)
    line = jnp.where(last_lane, jnp.where(block == blocks - 1, 0.0, nxt), ahead) - jnp.where(
        first_lane, jnp.where(block == 0, 0.0, prv), behind
    )
    if not segmented:
        return line, None
    nxt = jnp.where(block % seg == seg - 1, pltpu.roll(ahead, seg - 1, 0), nxt)
    prv = jnp.where(block % seg == 0, pltpu.roll(behind, blocks - seg + 1, 0), prv)
    ring = jnp.where(last_lane, nxt, ahead) - jnp.where(first_lane, prv, behind)
    return line, ring


def total(x):
    return jnp.sum(jnp.sum(x, axis=1, keepdims=True), axis=0, keepdims=True)


def blend_kernel(owners, secs, drift, weight, pcol, jitter_in, strips, first, *refs):
    messages = refs[:owners]
    jitter_out = refs[owners]
    windows = refs[owners + 1 : owners + 1 + secs]
    firsts, lasts, tails, fixed, acc, den = refs[owners + 1 + secs :]
    blocks = first.shape[0]
    width = blocks * BLOCK
    seg = SEG // BLOCK
    band = lax.axis_index(BANDS)
    sec = lax.axis_index("sec")
    slab = width // secs
    slab_blocks = slab // BLOCK
    base = CAP * BLOCK
    count = drift.shape[2]
    f32 = jnp.float32
    tiny = 1e-5 * 2 * (blocks // seg)
    for k in range(owners):
        source = origin(band, k, owners)
        firsts[source] = messages[k][base : base + blocks, :].astype(f32)
        lasts[source] = messages[k][base + blocks : base + 2 * blocks, :].astype(f32)
        if messages[k].shape[0] > base + 2 * blocks:
            tails[source] = messages[k][base + 2 * blocks : base + 3 * blocks, :].astype(f32)

    def estimate(row, ring, above):
        return -total(above * ring) / (total(row * row + above * above) + tiny)

    for j in range(owners):
        row = firsts[j]
        line, ring = row_differences(row, True)
        if j == 0:
            fixed[j] = row.astype(jnp.bfloat16).astype(f32)
        else:
            half = 0.5 * estimate(row, ring, lasts[j - 1])
            fixed[j] = (row - half * line).astype(jnp.bfloat16).astype(f32)

    row = first[...]
    line, ring = row_differences(row, True)
    upper = jnp.maximum(band - 1, 0)
    own = estimate(row, ring, lasts[upper] + tails[upper])
    own = jnp.where(band == 0, 0.0, own)
    lane_row = lax.broadcasted_iota(jnp.int32, jitter_in.shape, 1)
    jitter_out[...] = jnp.where(lane_row == 0, own, jitter_in[...])

    lane = lax.broadcasted_iota(jnp.int32, (BLOCK, BLOCK), 1)
    top = lax.broadcasted_iota(jnp.int32, (BLOCK, BLOCK), 0) == 0
    lane1 = lax.broadcasted_iota(jnp.int32, (1, BLOCK), 1)

    for k in range(secs):
        n, o = window_place(pcol, target(sec, k, secs), slab)
        turn = (BLOCK - o) & (BLOCK - 1)
        near = jnp.where(top, fixed[band, pl.ds(n, 1), :], strips[k, 0].astype(f32))
        n1 = jnp.minimum(n + 1, blocks - 1)
        far = jnp.where(top, fixed[band, pl.ds(n1, 1), :], strips[k, 1].astype(f32))
        acc[target(sec, k, secs)] = jnp.where(
            lane + o < BLOCK, pltpu.roll(near, turn, 1), pltpu.roll(far, turn, 1)
        )
        den[target(sec, k, secs)] = jnp.ones((1, BLOCK), f32)

    for k in range(owners):
        source = origin(band, k, owners)
        place, found = find_slots(drift, source, band, count)
        for c in range(CAP):
            goal = drift[0, source, place[c], 2]
            q = goal // slab_blocks
            n, o = window_place(pcol, q, slab)

            @pl.when((found > c) & ((goal == n) | (goal == n + 1)))
            def _():
                w = weight[0, source, place[c]]
                turn = (BLOCK - o) & (BLOCK - 1)
                picture = messages[k][c * BLOCK : (c + 1) * BLOCK, :].astype(f32)
                origin_block = drift[0, source, place[c], 0]
                picture = jnp.where(top, fixed[source, pl.ds(origin_block, 1), :], picture)
                inside = (lane1 + o < BLOCK) == (goal == n)
                factor = jnp.where(inside, w, 0.0)
                acc[q] = acc[q] + factor * pltpu.roll(picture, turn, 1)
                den[q] = den[q] + factor

    for k in range(secs):
        q = target(sec, k, secs)
        windows[k][...] = (acc[q] * (1.0 / den[q])).astype(jnp.bfloat16)


def dot(a, b):
    return lax.dot_general(
        a,
        b,
        (((1,), (0,)), ((), ())),
        precision=lax.Precision.HIGHEST,
        preferred_element_type=jnp.float32,
    )


def surface_kernel(secs, tables, *refs):
    arrived = refs[:secs]
    out = refs[secs]
    stack = refs[secs + 1]
    sec = lax.axis_index("sec")
    side = PATCH
    for k in range(secs):
        stack[origin(sec, k, secs)] = arrived[k][...].astype(jnp.float32)
    cosine = tables[:, :side]
    sine = tables[:, side:]
    both = tables[...]
    tall = jnp.concatenate([cosine, sine], 0)
    turn = jnp.concatenate([both, jnp.concatenate([-sine, cosine], 1)], 0)
    close = jnp.concatenate([cosine, -sine], 1) * (1.0 / side)
    last = None
    for s in range(secs):
        first = dot(stack[s], both)
        grid = dot(tall, first)
        real = grid[:side, :side] - grid[side:, side:]
        imag = -(grid[side:, :side] + grid[:side, side:])
        if s > 0:
            last_real, last_imag = last
            cross_real = last_real * real + last_imag * imag
            cross_imag = last_imag * real - last_real * imag
            magnitude = jnp.sqrt(cross_real * cross_real + cross_imag * cross_imag)
            damping = (0.5 / (side * side)) * total(magnitude) + 1e-6
            scaled = 1.0 / (magnitude + damping)
            damped = jnp.concatenate([cross_real * scaled, cross_imag * scaled], 1)
            back = dot(damped, turn)
            back = jnp.concatenate([back[:, :side], back[:, side:]], 0)
            out[s - 1] = dot(close, back)
        last = (real, imag)


def dft_tables(length):
    indices = np.arange(length)
    angles = (indices[:, None] * indices[None, :] % length) * (2.0 * math.pi / length)
    return np.concatenate([np.cos(angles), np.sin(angles)], 1).astype(np.float32)


def per_device(section_pixels, jitter_index, drift_list, blend_weight, patch_col):
    pixels = section_pixels[0]
    rows, width = pixels.shape
    blocks = width // BLOCK
    owners = lax.axis_size(BANDS)
    secs = lax.axis_size("sec")
    chunks = 4
    f32, bf16 = jnp.float32, jnp.bfloat16
    vmem = pl.BlockSpec(memory_space=pltpu.VMEM)
    smem = pl.BlockSpec(memory_space=pltpu.SMEM)
    hbm = pl.BlockSpec(memory_space=pl.ANY)
    shape = jax.ShapeDtypeStruct
    message_rows = [
        CAP * BLOCK + (3 if has_tail(k, owners) else 2) * blocks for k in range(owners)
    ]
    params = pltpu.CompilerParams(vmem_limit_bytes=40 * 1024 * 1024)
    jitter, strips, first, *messages = pl.pallas_call(
        functools.partial(front_kernel, owners, secs, chunks),
        out_shape=[
            shape((1, rows), f32),
            shape((secs, 2, BLOCK, BLOCK), bf16),
            shape((blocks, BLOCK), f32),
        ]
        + [shape((r, BLOCK), bf16) for r in message_rows],
        in_specs=[vmem, smem, smem, hbm],
        out_specs=[vmem] * (3 + owners),
        scratch_shapes=[
            pltpu.VMEM((rows, width), f32),
            pltpu.VMEM((blocks, rows + SUB, BLOCK), f32),
            pltpu.VMEM((blocks, rows, BLOCK), f32),
            pltpu.VMEM((rows, rows), jnp.int32),
            pltpu.VMEM((2, rows + SUB, BLOCK), f32),
            pltpu.SemaphoreType.DMA((chunks,)),
        ],
        compiler_params=params,
        name="front",
    )(jitter_index, drift_list, patch_col, pixels)
    messages = messages[:1] + [
        send(messages[k], BANDS, k, owners) for k in range(1, owners)
    ]
    jitter, *windows = pl.pallas_call(
        functools.partial(blend_kernel, owners, secs),
        out_shape=[shape((1, rows), f32)] + [shape((PATCH, PATCH), bf16)] * secs,
        in_specs=[smem, smem, smem] + [vmem] * (3 + owners),
        out_specs=[vmem] * (1 + secs),
        scratch_shapes=[pltpu.VMEM((owners, blocks, BLOCK), f32)] * 4
        + [pltpu.VMEM((secs, PATCH, PATCH), f32), pltpu.VMEM((secs, 1, PATCH), f32)],
        compiler_params=params,
        name="blend",
    )(drift_list, blend_weight, patch_col, jitter, strips, first, *messages)
    windows = windows[:1] + [send(windows[k], "sec", k, secs) for k in range(1, secs)]
    surfaces = pl.pallas_call(
        functools.partial(surface_kernel, secs),
        out_shape=shape((secs - 1, PATCH, PATCH), f32),
        in_specs=[vmem] * (1 + secs),
        out_specs=vmem,
        scratch_shapes=[pltpu.VMEM((secs, PATCH, PATCH), f32)],
        compiler_params=params,
        name="surface",
    )(jnp.asarray(dft_tables(PATCH)), *windows)
    return (jitter, surfaces[:, None, None])


def solution(mesh):
    in_specs = (
        P(("groups", "sec"), ("tile", "row"), None),
        P(("groups", "sec"), ("tile", "row")),
        P(("groups", "sec"), None, None, None),
        P(("groups", "sec"), None, None),
        P(("tile", "row"), "groups"),
    )
    out_specs = (
        P(("groups", "sec"), ("tile", "row")),
        P("groups", ("tile", "row"), "sec", None, None),
    )
    return jax.shard_map(
        per_device, mesh=mesh, in_specs=in_specs, out_specs=out_specs, check_vma=False
    )
```

time: 105 us -> 34.8 us (0.33)
  local copies, waits for them, and re-layouts: 33.7 us -> 3.7 us
  other arithmetic: 25.4 us -> 0 us
  matrix products: 20.9 us -> 0 us
  Pallas kernels: 0 us -> 12.1 us
  blocking collectives: 11.1 us -> 0 us
  waiting for transfers between devices: 6.03 us -> 10.6 us
  starting transfers between devices: 6.23 us -> 7.56 us
    dot_general x16 -> x0, matrix products: 20.9 us -> none  [the longest x2 10.5 us: row_spectra(): jnp.dot(rows.reshape(row_count * (row_width // SEG), SEG), dft_table, pre...]
    gather x41 -> x0, local copies, waits for them, and re-layouts: 13.2 us -> none
    pallas_call x0 -> x3, Pallas kernels: none -> 12.1 us  [the longest x1 5.01 us: per_device(): pl.pallas_call(functools.partial(surface_kernel, secs), out_shape=shape((...]
    all_to_all x1 -> x0, blocking collectives: 11.1 us -> none  [per_device(): lax.all_to_all(outbound, 'sec', split_axis=3, concat_axis=0, tiled=True)]
    ppermute x1 -> x6, waiting for transfers between devices: 0.01 us -> 10.6 us  [send(): return lax.ppermute(x, axis, [(i, target(i, k, n)) for i in range(n)])]
    add x4 -> x0, other arithmetic: 9.17 us -> none  [the longest x1 9.08 us: align_rows(): aligned + jnp.where(delays[:, None] == shift_by, padded[:, shift_by:shift...]
    slice x5 -> x0, local copies, waits for them, and re-layouts: 7.19 us -> none  [the longest x2 4.19 us: per_device(): above_row = shifted(aligned[row_count - 1:], ('tile', 'row'), 1)]
    all_to_all x1 -> x0, waiting for transfers between devices: 6.03 us -> none  [per_device(): lax.all_to_all(outgoing.reshape(owners, CAP, BLOCK, BLOCK), ('tile', 'row...]
  transfers between devices with their start and end apart: 2 -> 6, of which waited for: 1 -> 3; matrix products, arithmetic and copies ran while one was open for 17% -> 0% of each run, Pallas kernels for 0% -> 0%
where the time goes in v1:
time: 34.8 us; the launch traced here: 34.7 us
  Pallas kernels  12.1 us (35%)
  waiting for transfers between devices  10.6 us (30%)
  starting transfers between devices  7.56 us (22%)
  local copies, waits for them, and re-layouts  3.7 us (11%)
  between operations  0.66 us (2%)
    ppermute x6, waiting for transfers between devices, send(): return lax.ppermute(x, axis, [(i, target(i, k, n)) for i in range(n)])  10.6 us
    ppermute x6, starting transfers between devices, send(): return lax.ppermute(x, axis, [(i, target(i, k, n)) for i in range(n)])  7.56 us
    pallas_call x1, Pallas kernels, per_device(): pl.pallas_call(functools.partial(surface_kernel, secs), out_shape=shape((...  5.01 us
    pallas_call x1, Pallas kernels, per_device(): pl.pallas_call(functools.partial(front_kernel, owners, secs, chunks), out...  4.8 us
    unnamed x11, local copies, waits for them, and re-layouts  3.7 us
    pallas_call x1, Pallas kernels, per_device(): pl.pallas_call(functools.partial(blend_kernel, owners, secs), out_shape=[...  2.34 us
  transfers between devices with their start and end apart: 6, of which 3 were waited for; matrix products, arithmetic and copies ran while one was open for 0% of the time, Pallas kernels for 0%

profile of v1, /device:TPU:0, one launch (start us, length us, event | category | flops | bytes accessed | tf_op | source)
XLA Modules:
  0.0 34.7 jit_solution(11309531914956823735)
XLA Ops:
  0.6 0.0 copy-start.2
  0.6 0.8 %copy.9.drift = s32[1,4,8,3]{3,2,1,0:T(8,128)S(1)} copy(s32[1,4,8,3]{2,1,3,0:T(4,128)} %param.8) | data formatting | bytes 768 | tf_op args[2]
  1.4 0.0 copy-start
  1.4 1.6 %copy-done = f32[1,128,4096]{2,1,0:T(8,128)S(1)} copy-done((f32[1,128,4096]{2,1,0:T(8,128)S(1)}, f32[1,128,4096]{2,1,0:T(8,128)}, u32[]{:S(2)}) %copy-start) | copy-done | bytes 2097176
  3.0 0.0 copy-start.3
  3.0 0.7 %copy-done.3 = s32[1,4]{1,0:T(1,128)S(1)} copy-done((s32[1,4]{1,0:T(1,128)S(1)}, s32[1,4]{1,0:T(1,128)}, u32[]{:S(2)}) %copy-start.3) | copy-done | bytes 40
  3.7 0.0 copy-start.4
  3.7 0.7 %copy-done.4 = s32[1,128]{1,0:T(1,128)S(1)} copy-done((s32[1,128]{1,0:T(1,128)S(1)}, s32[1,128]{1,0:T(1,128)}, u32[]{:S(2)}) %copy-start.4) | copy-done | bytes 536
  4.3 0.0 copy-start.1
  4.3 4.8 %front.1 = (f32[1,128]{1,0:T(1,128)S(1)}, bf16[4,2,128,128]{3,2,1,0:T(8,128)(2,1)S(1)}, f32[32,128]{1,0:T(8,128)S(1)}, bf16[320,128]{1,0:T(8,128)(2,1)S(1)}, bf1...) custom-call(s32[1,128]{1,0:T(1,128)S(1)} %copy-done.4, ...), custom_call_target="tpu_custom_call" | custom-call | tf_op jit(solution)/shard_map/front/pallas_call | solution.py:346
  9.1 0.5 %collective-permute-start = (bf16[352,128]{1,0:T(8,128)(2,1)S(1)}, bf16[352,128]{1,0:T(8,128)(2,1)S(1)}, u32[]{:S(2)}, u32[]{:S(2)}) collective-permute-start(bf16[352,128]{1,0:T(8,128)(2,1)S(1)} %get-tuple-element.18), channel_id=1, source_target_pairs={{0,1},{1,0},{2,3},{3,2},{4,5},{5,4},{6,7},{7,6},{8,9},{9,8},{10,11... | collective-permute-start | bytes 270344 | tf_op jit(solution)/shard_map/ppermute | solution.py:33
  9.7 2.6 %collective-permute-start.2 = (bf16[352,128]{1,0:T(8,128)(2,1)S(1)}, bf16[352,128]{1,0:T(8,128)(2,1)S(1)}, u32[]{:S(2)}, u32[]{:S(2)}) collective-permute-start(bf16[352,128]{1,0:T(8,128)(2,1)S(1)} %get-tuple-element.20), channel_id=1, source_target_pairs={{0,3},{1,2},{2,1},{3,0},{4,7},{5,6},{6,5},{7,4},{8,11},{9,10},{10,... | collective-permute-start | bytes 270344 | tf_op jit(solution)/shard_map/ppermute | solution.py:33
  12.3 0.0 collective-permute-start.1
  12.3 4.9 %collective-permute-done.1.refs_2_ = bf16[320,128]{1,0:T(8,128)(2,1)S(1)} collective-permute-done((bf16[320,128]{1,0:T(8,128)(2,1)S(1)}, bf16[320,128]{1,0:T(8,128)(2,1)S(1)}, u32[]{:S(2)}, u32[]{:S(2)}) %collective-permute-start.1) | collective-permute-done | bytes 81952 | tf_op jit(solution)/shard_map/ppermute | solution.py:33
  17.2 0.0 collective-permute-done.refs_1_
  17.2 0.0 collective-permute-done.2.refs_3_
  17.2 0.0 copy-done.2
  17.2 2.3 %blend.1 = (f32[1,128]{1,0:T(1,128)}, bf16[128,128]{1,0:T(8,128)(2,1)S(1)}, bf16[128,128]{1,0:T(8,128)(2,1)S(1)}, bf16[128,128]{1,0:T(8,128)(2,1)S(1)}, bf16[128,128]{1,0:T(8,128)(2,1)S(1)}) custom-call(s32[1,4,8,3]{3,2,1,0:T(8,128)S(1)} %copy.9.drift, f32[1,4,8]{2,1,0:T(4,128)S(1)} %copy-done.2, s32[1,4]{1,0:T(1,128)S(1)} %copy-done.3, ...), custom_call_target="tpu_custom_call" | custom-call | tf_op jit(solution)/shard_map/blend/pallas_call | solution.py:370
  19.5 1.6 %collective-permute-start.3 = (bf16[128,128]{1,0:T(8,128)(2,1)S(1)}, bf16[128,128]{1,0:T(8,128)(2,1)S(1)}, u32[]{:S(2)}, u32[]{:S(2)}) collective-permute-start(bf16[128,128]{1,0:T(8,128)(2,1)S(1)} %get-tuple-element.23), channel_id=1, source_target_pairs={{0,4},{4,0},{8,12},{12,8},{1,5},{5,1},{9,13},{13,9},{2,6},{6,2},{1... | collective-permute-start | bytes 98312 | tf_op jit(solution)/shard_map/ppermute | solution.py:33
  21.1 2.8 %collective-permute-start.4 = (bf16[128,128]{1,0:T(8,128)(2,1)S(1)}, bf16[128,128]{1,0:T(8,128)(2,1)S(1)}, u32[]{:S(2)}, u32[]{:S(2)}) collective-permute-start(bf16[128,128]{1,0:T(8,128)(2,1)S(1)} %get-tuple-element.24), channel_id=1, source_target_pairs={{0,8},{4,12},{8,0},{12,4},{1,9},{5,13},{9,1},{13,5},{2,10},{6,14},... | collective-permute-start | bytes 98312 | tf_op jit(solution)/shard_map/ppermute | solution.py:33
  23.9 0.0 collective-permute-start.5
  23.9 0.0 collective-permute-done.3.refs_1_
  23.9 2.3 %collective-permute-done.4.refs_2_ = bf16[128,128]{1,0:T(8,128)(2,1)S(1)} collective-permute-done((bf16[128,128]{1,0:T(8,128)(2,1)S(1)}, bf16[128,128]{1,0:T(8,128)(2,1)S(1)}, u32[]{:S(2)}, u32[]{:S(2)}) %collective-permute-start.4) | collective-permute-done | bytes 32800 | tf_op jit(solution)/shard_map/ppermute | solution.py:33
  26.3 3.4 %collective-permute-done.5.refs_3_ = bf16[128,128]{1,0:T(8,128)(2,1)S(1)} collective-permute-done((bf16[128,128]{1,0:T(8,128)(2,1)S(1)}, bf16[128,128]{1,0:T(8,128)(2,1)S(1)}, u32[]{:S(2)}, u32[]{:S(2)}) %collective-permute-start.5) | collective-permute-done | bytes 32800 | tf_op jit(solution)/shard_map/ppermute | solution.py:33
  29.6 0.0 copy-done.1
  29.6 5.0 %surface.1 = f32[3,128,128]{2,1,0:T(8,128)} custom-call(f32[128,256]{1,0:T(8,128)S(1)} %copy-done.1, bf16[128,128]{1,0:T(8,128)(2,1)S(1)} %get-tuple-element.22.refs_0_, bf16[128,128]{1,0:T(8,128)(2,1)S(1)} %collective-permute-done.3.refs_1_, bf16[128,128]{1,0:T(8,128)(2,1)S(1)} %collective-permute-done.4.refs_2_, ...), custom_call_target="tpu_custom_call" | custom-call | tf_op jit(solution)/shard_map/surface/pallas_call | solution.py:381
Async XLA Ops:
  0.6 16.6 %copy-start.2 = (f32[1,4,8]{2,1,0:T(4,128)S(1)}, f32[1,4,8]{2,1,0:T(4,128)}, u32[]{:S(2)}) copy-start(f32[1,4,8]{2,1,0:T(4,128)} %weight.1) | copy-start | bytes 388
  1.4 1.6 %copy-start = (f32[1,128,4096]{2,1,0:T(8,128)S(1)}, f32[1,128,4096]{2,1,0:T(8,128)}, u32[]{:S(2)}) copy-start(f32[1,128,4096]{2,1,0:T(8,128)} %param.6) | copy-start | bytes 6291460
  3.0 0.7 %copy-start.3 = (s32[1,4]{1,0:T(1,128)S(1)}, s32[1,4]{1,0:T(1,128)}, u32[]{:S(2)}) copy-start(s32[1,4]{1,0:T(1,128)} %pcol.3) | copy-start | bytes 52
  3.7 0.7 %copy-start.4 = (s32[1,128]{1,0:T(1,128)S(1)}, s32[1,128]{1,0:T(1,128)}, u32[]{:S(2)}) copy-start(s32[1,128]{1,0:T(1,128)} %delay.1) | copy-start | bytes 1540
  4.3 25.3 %copy-start.1 = (f32[128,256]{1,0:T(8,128)S(1)}, f32[128,256]{1,0:T(8,128)}, u32[]{:S(2)}) copy-start(f32[128,256]{1,0:T(8,128)} %constant.2.clone.tables) | copy-start | bytes 393220
  9.1 8.1 %collective-permute-start = (bf16[352,128]{1,0:T(8,128)(2,1)S(1)}, bf16[352,128]{1,0:T(8,128)(2,1)S(1)}, u32[]{:S(2)}, u32[]{:S(2)}) collective-permute-start(bf16[352,128]{1,0:T(8,128)(2,1)S(1)} %get-tuple-element.18), channel_id=1, source_target_pairs={{0,1},{1,0},{2,3},{3,2},{4,5},{5,4},{6,7},{7,6},{8,9},{9,8},{10,11... | collective-permute-start | bytes 270344 | tf_op jit(solution)/shard_map/ppermute | solution.py:33
  9.7 7.5 %collective-permute-start.2 = (bf16[352,128]{1,0:T(8,128)(2,1)S(1)}, bf16[352,128]{1,0:T(8,128)(2,1)S(1)}, u32[]{:S(2)}, u32[]{:S(2)}) collective-permute-start(bf16[352,128]{1,0:T(8,128)(2,1)S(1)} %get-tuple-element.20), channel_id=1, source_target_pairs={{0,3},{1,2},{2,1},{3,0},{4,7},{5,6},{6,5},{7,4},{8,11},{9,10},{10,... | collective-permute-start | bytes 270344 | tf_op jit(solution)/shard_map/ppermute | solution.py:33
  12.3 4.9 %collective-permute-start.1 = (bf16[320,128]{1,0:T(8,128)(2,1)S(1)}, bf16[320,128]{1,0:T(8,128)(2,1)S(1)}, u32[]{:S(2)}, u32[]{:S(2)}) collective-permute-start(bf16[320,128]{1,0:T(8,128)(2,1)S(1)} %get-tuple-element.19), channel_id=1, source_target_pairs={{0,2},{1,3},{2,0},{3,1},{4,6},{5,7},{6,4},{7,5},{8,10},{9,11},{10,... | collective-permute-start | bytes 245768 | tf_op jit(solution)/shard_map/ppermute | solution.py:33
  19.5 4.4 %collective-permute-start.3 = (bf16[128,128]{1,0:T(8,128)(2,1)S(1)}, bf16[128,128]{1,0:T(8,128)(2,1)S(1)}, u32[]{:S(2)}, u32[]{:S(2)}) collective-permute-start(bf16[128,128]{1,0:T(8,128)(2,1)S(1)} %get-tuple-element.23), channel_id=1, source_target_pairs={{0,4},{4,0},{8,12},{12,8},{1,5},{5,1},{9,13},{13,9},{2,6},{6,2},{1... | collective-permute-start | bytes 98312 | tf_op jit(solution)/shard_map/ppermute | solution.py:33
  21.1 5.1 %collective-permute-start.4 = (bf16[128,128]{1,0:T(8,128)(2,1)S(1)}, bf16[128,128]{1,0:T(8,128)(2,1)S(1)}, u32[]{:S(2)}, u32[]{:S(2)}) collective-permute-start(bf16[128,128]{1,0:T(8,128)(2,1)S(1)} %get-tuple-element.24), channel_id=1, source_target_pairs={{0,8},{4,12},{8,0},{12,4},{1,9},{5,13},{9,1},{13,5},{2,10},{6,14},... | collective-permute-start | bytes 98312 | tf_op jit(solution)/shard_map/ppermute | solution.py:33
  23.9 5.7 %collective-permute-start.5 = (bf16[128,128]{1,0:T(8,128)(2,1)S(1)}, bf16[128,128]{1,0:T(8,128)(2,1)S(1)}, u32[]{:S(2)}, u32[]{:S(2)}) collective-permute-start(bf16[128,128]{1,0:T(8,128)(2,1)S(1)} %get-tuple-element.25), channel_id=1, source_target_pairs={{0,12},{4,8},{8,4},{12,0},{1,13},{5,9},{9,5},{13,1},{2,14},{6,10},... | collective-permute-start | bytes 98312 | tf_op jit(solution)/shard_map/ppermute | solution.py:33

commit v2 on v1

v2 whole, which is shorter than its diff:
```python
import functools
import math

import jax
import jax.numpy as jnp
import numpy as np
from jax import lax
from jax.experimental import pallas as pl
from jax.experimental.pallas import tpu as pltpu
from jax.sharding import PartitionSpec as P

SEG = 512
PATCH = 128
BLOCK = 128
CAP = 2
SUB = 8
BANDS = ("tile", "row")


def is_pow2(n):
    return n & (n - 1) == 0


def target(me, k, n):
    return me ^ k if is_pow2(n) else (me + k) % n


def origin(me, k, n):
    return me ^ k if is_pow2(n) else (me + n - k) % n


def send(x, axis, k, n):
    return lax.ppermute(x, axis, [(i, target(i, k, n)) for i in range(n)])


def has_tail(k, n):
    return any(target(i, k, n) == (i + 1) % n for i in range(n))


def find_slots(drift, band, owner, count):
    place = [jnp.int32(0)] * CAP
    found = jnp.int32(0)
    for p in range(count):
        hit = drift[1, band, p] == owner
        for c in range(CAP):
            place[c] = jnp.where(hit & (found == c), p, place[c])
        found = found + jnp.where(hit, 1, 0)
    return place, found


def window_place(pcol, q, slab):
    start = q * slab + pcol[0, q]
    return start >> 7, start & (BLOCK - 1)


def split(x):
    high = x.astype(jnp.bfloat16)
    return high, (x - high.astype(jnp.float32)).astype(jnp.bfloat16)


def front_kernel(owners, chunks, delay_at, drift_at, pixels, *refs):
    jitter_out, half_out, padded, first_out = refs[:4]
    messages = refs[4 : 3 + owners]
    raw, ring, wide, sums, delay, drift, loaded = refs[3 + owners :]
    rows, width = pixels.shape
    blocks = width // BLOCK
    per = rows // chunks
    band = lax.axis_index(BANDS)

    def load(i):
        at = pl.ds(i * per, per)
        return pltpu.make_async_copy(pixels.at[at, :], raw.at[at, :], loaded.at[i])

    small = [
        pltpu.make_async_copy(a, b, loaded.at[chunks + i])
        for i, (a, b) in enumerate(((delay_at, delay), (drift_at, drift)))
    ]
    small[0].start()
    for i in range(chunks):
        load(i).start()
    small[1].start()
    padded[0] = jnp.zeros(padded.shape[1:], jnp.float32)
    padded[blocks + 1] = jnp.zeros(padded.shape[1:], jnp.float32)
    padded[1 : blocks + 1, 0:SUB, :] = jnp.zeros((blocks, SUB, BLOCK), jnp.float32)
    ring[:, 0:SUB, :] = jnp.zeros((blocks, SUB, BLOCK), jnp.float32)
    small[0].wait()
    wide[...] = jnp.broadcast_to(delay[...], (rows, rows)).T
    lane = lax.broadcasted_iota(jnp.int32, (SUB, BLOCK), 1)
    sub = lax.broadcasted_iota(jnp.int32, (SUB, BLOCK), 0)
    last_lane = lane == BLOCK - 1
    first_sub = sub == 0
    seg = SEG // BLOCK

    def eight_rows(g, _):
        at = pl.multiple_of(g * SUB, SUB)
        delays = wide[pl.ds(at, SUB), :]
        moved = lane + delays
        index = moved & (BLOCK - 1)
        near = moved < BLOCK
        picked = [
            jnp.take_along_axis(
                raw[pl.ds(at, SUB), v * BLOCK : (v + 1) * BLOCK],
                index,
                axis=1,
                mode="promise_in_bounds",
            )
            for v in range(blocks)
        ]
        picked.append(jnp.zeros((SUB, BLOCK), jnp.float32))
        x = [jnp.where(near, picked[v], picked[v + 1]) for v in range(blocks)]
        zero = jnp.zeros((SUB, BLOCK), jnp.float32)
        cross = zero
        power = zero
        for v in range(blocks):
            prv = x[v - 1] if v % seg else x[v + seg - 1]
            behind = pltpu.roll(jnp.where(last_lane, prv, x[v]), 1, 1)
            above = jnp.where(
                first_sub, padded[v + 1, pl.ds(at + SUB - 1, 1), :], pltpu.roll(x[v], 1, 0)
            )
            above_behind = jnp.where(
                first_sub, ring[v, pl.ds(at + SUB - 1, 1), :], pltpu.roll(behind, 1, 0)
            )
            cross = cross + (above * behind - above_behind * x[v])
            power = power + x[v] * x[v]
            padded[v + 1, pl.ds(at + SUB, SUB), :] = x[v]
            ring[v, pl.ds(at + SUB, SUB), :] = behind
        sums[0, pl.ds(at, SUB), :] = cross
        sums[1, pl.ds(at, SUB), :] = power
        return 0

    steps = per // SUB
    for i in range(chunks):
        load(i).wait()
        lax.fori_loop(i * steps, (i + 1) * steps, eight_rows, 0)

    small[1].wait()
    total_cross = jnp.sum(sums[0], axis=1, keepdims=True)
    total_power = jnp.sum(sums[1], axis=1, keepdims=True)
    row_index = lax.broadcasted_iota(jnp.int32, (rows, BLOCK), 0)
    power = jnp.broadcast_to(total_power, (rows, BLOCK))
    power = power + jnp.where(row_index == 0, 0.0, pltpu.roll(power, 1, 0))
    cross = jnp.broadcast_to(total_cross, (rows, BLOCK))
    jitter = cross / (power + 1e-5 * 2 * (blocks // seg))
    half = 0.5 * jitter
    half_out[...] = half
    count = drift.shape[2]
    for k in range(1, owners):
        place, _ = find_slots(drift, band, target(band, k, owners), count)
        for c in range(CAP):
            messages[k - 1][c * BLOCK : (c + 1) * BLOCK, :] = corrected(
                padded, half, drift[0, band, place[c]]
            ).astype(jnp.bfloat16)
    jitter_out[...] = jitter.T[0:1, :]
    for v in range(blocks):
        first_out[0, v : v + 1, :] = padded[v + 1, SUB : SUB + 1, :]
        first_out[1, v : v + 1, :] = padded[v + 1, SUB + rows - 1 : SUB + rows, :]
    first = first_out[0].astype(jnp.bfloat16)
    last, rest = split(first_out[1])
    base = CAP * BLOCK
    for k in range(1, owners):
        message = messages[k - 1]
        message[base : base + blocks, :] = first
        message[base + blocks : base + 2 * blocks, :] = last
        if message.shape[0] > base + 2 * blocks:
            message[base + 2 * blocks : base + 3 * blocks, :] = rest


def corrected(padded, half, n):
    rows = half.shape[0]
    here = padded[n + 1, SUB : SUB + rows, :]
    lane = lax.broadcasted_iota(jnp.int32, here.shape, 1)
    left = jnp.where(lane == BLOCK - 1, padded[n, SUB : SUB + rows, :], here)
    right = jnp.where(lane == 0, padded[n + 2, SUB : SUB + rows, :], here)
    return here - half * (pltpu.roll(right, BLOCK - 1, 1) - pltpu.roll(left, 1, 1))


def plan_kernel(owners, secs, drift, pcol, half_in, padded, acc, own):
    blocks = padded.shape[0] - 2
    slab = blocks * BLOCK // secs
    band = lax.axis_index(BANDS)
    half = half_in[...]
    lane = lax.broadcasted_iota(jnp.int32, half.shape, 1)
    place, _ = find_slots(drift, band, band, drift.shape[2])
    for c in range(CAP):
        own[c * BLOCK : (c + 1) * BLOCK, :] = corrected(
            padded, half, drift[0, band, place[c]]
        ).astype(jnp.bfloat16)
    for q in range(secs):
        n, o = window_place(pcol, q, slab)
        n1 = jnp.minimum(n + 1, blocks - 1)
        near, far = (
            corrected(padded, half, i).astype(jnp.bfloat16).astype(jnp.float32) for i in (n, n1)
        )
        picked = jnp.where(lane >= o, near, far)
        acc[q] = pltpu.roll(picked, (BLOCK - o) & (BLOCK - 1), 1)


def row_differences(x):
    blocks = x.shape[0]
    seg = SEG // BLOCK
    lane = lax.broadcasted_iota(jnp.int32, x.shape, 1)
    block = lax.broadcasted_iota(jnp.int32, x.shape, 0)
    ahead = pltpu.roll(x, BLOCK - 1, 1)
    behind = pltpu.roll(x, 1, 1)
    last_lane = lane == BLOCK - 1
    first_lane = lane == 0
    nxt = pltpu.roll(ahead, blocks - 1, 0)
    prv = pltpu.roll(behind, 1, 0)
    line = jnp.where(last_lane, jnp.where(block == blocks - 1, 0.0, nxt), ahead) - jnp.where(
        first_lane, jnp.where(block == 0, 0.0, prv), behind
    )
    nxt = jnp.where(block % seg == seg - 1, pltpu.roll(ahead, seg - 1, 0), nxt)
    prv = jnp.where(block % seg == 0, pltpu.roll(behind, blocks - seg + 1, 0), prv)
    ring = jnp.where(last_lane, nxt, ahead) - jnp.where(first_lane, prv, behind)
    return line, ring


def total(x):
    return jnp.sum(jnp.sum(x, axis=1, keepdims=True), axis=0, keepdims=True)


def blend_kernel(owners, secs, drift, weight, pcol, jitter_in, edges, begun, *refs):
    messages = refs[:owners]
    jitter_out = refs[owners]
    windows = refs[owners + 1 : owners + 1 + secs]
    firsts, lasts, tails, fixed, acc, den = refs[owners + 1 + secs :]
    blocks = edges.shape[1]
    width = blocks * BLOCK
    seg = SEG // BLOCK
    band = lax.axis_index(BANDS)
    sec = lax.axis_index("sec")
    slab = width // secs
    slab_blocks = slab // BLOCK
    base = CAP * BLOCK
    count = drift.shape[2]
    f32 = jnp.float32
    tiny = 1e-5 * 2 * (blocks // seg)
    firsts[band] = edges[0]
    lasts[band] = edges[1]
    for k in range(1, owners):
        source = origin(band, k, owners)
        firsts[source] = messages[k][base : base + blocks, :].astype(f32)
        lasts[source] = messages[k][base + blocks : base + 2 * blocks, :].astype(f32)
        if messages[k].shape[0] > base + 2 * blocks:
            tails[source] = messages[k][base + 2 * blocks : base + 3 * blocks, :].astype(f32)

    def estimate(row, ring, above):
        return -total(above * ring) / (total(row * row + above * above) + tiny)

    own = jnp.zeros((1, 1), f32)
    for j in range(owners):
        row = firsts[j]
        line, ring = row_differences(row)
        if j == 0:
            fixed[j] = row.astype(jnp.bfloat16).astype(f32)
        else:
            above = lasts[j - 1] + jnp.where(band == j, tails[j - 1], 0.0)
            found = estimate(row, ring, above)
            own = jnp.where(band == j, found, own)
            fixed[j] = (row - 0.5 * found * line).astype(jnp.bfloat16).astype(f32)
    lane_row = lax.broadcasted_iota(jnp.int32, jitter_in.shape, 1)
    jitter_out[...] = jnp.where(lane_row == 0, own, jitter_in[...])

    top = lax.broadcasted_iota(jnp.int32, (BLOCK, BLOCK), 0) == 0
    lane1 = lax.broadcasted_iota(jnp.int32, (1, BLOCK), 1)
    acc[...] = begun[...]
    for q in range(secs):
        n, o = window_place(pcol, q, slab)
        n1 = jnp.minimum(n + 1, blocks - 1)
        picked = jnp.where(lane1 >= o, fixed[band, pl.ds(n, 1), :], fixed[band, pl.ds(n1, 1), :])
        picked = pltpu.roll(jnp.broadcast_to(picked, (SUB, BLOCK)), (BLOCK - o) & (BLOCK - 1), 1)
        acc[q, 0:1, :] = picked[0:1, :]
        den[q] = jnp.ones((1, BLOCK), f32)

    for k in range(owners):
        source = origin(band, k, owners)
        place, found = find_slots(drift, source, band, count)
        for c in range(CAP):
            goal = drift[2, source, place[c]]
            q = goal // slab_blocks
            n, o = window_place(pcol, q, slab)

            @pl.when((found > c) & ((goal == n) | (goal == n + 1)))
            def _():
                w = weight[0, source, place[c]]
                turn = (BLOCK - o) & (BLOCK - 1)
                picture = messages[k][c * BLOCK : (c + 1) * BLOCK, :].astype(f32)
                origin_block = drift[0, source, place[c]]
                picture = jnp.where(top, fixed[source, pl.ds(origin_block, 1), :], picture)
                inside = (lane1 + o < BLOCK) == (goal == n)
                factor = jnp.where(inside, w, 0.0)
                acc[q] = acc[q] + factor * pltpu.roll(picture, turn, 1)
                den[q] = den[q] + factor

    for k in range(secs):
        q = target(sec, k, secs)
        windows[k][...] = (acc[q] * (1.0 / den[q])).astype(jnp.bfloat16)


def dot(a, b):
    return jnp.dot(a, b, preferred_element_type=jnp.float32)


def spectra(patches, left, right):
    side = PATCH
    found = []
    for at in range(0, len(patches), 2):
        pair = patches[at : at + 2]
        beside = jnp.concatenate(pair, 1) if len(pair) > 1 else pair[0]
        columns = dot(left, jnp.concatenate([beside, beside], 0))
        stack = []
        for i in range(len(pair)):
            high, low = split(columns[:, i * side : (i + 1) * side])
            stack.append(jnp.concatenate([high, low, high], 1))
        grid = dot(jnp.concatenate(stack, 0), right)
        for i in range(len(pair)):
            one = grid[2 * side * i : 2 * side * (i + 1)]
            real = one[:side, :side] - one[side:, side:]
            imag = -(one[side:, :side] + one[:side, side:])
            found.append((real, imag))
    return found


def spectrum_kernel(left, right, *refs):
    patches, out = refs[:-1], refs[-1]
    for k, (real, imag) in enumerate(spectra([p[...] for p in patches], left[...], right[...])):
        out[k, 0] = real
        out[k, 1] = imag


def surface_kernel(secs, left, right, turn, close, early, *refs):
    late = refs[: secs - early.shape[0]]
    out, freq, held, sent = refs[len(late) :]
    sec = lax.axis_index("sec")
    side = PATCH
    begun = early.shape[0]
    for k in range(begun):
        freq[origin(sec, k, secs)] = early[k]
    for k, (real, imag) in enumerate(spectra([p[...] for p in late], left[...], right[...])):
        at = origin(sec, begun + k, secs)
        freq[at, 0] = real
        freq[at, 1] = imag
    rows = []
    for s in range(secs - 1):
        real, imag = freq[s, 0], freq[s, 1]
        next_real, next_imag = freq[s + 1, 0], freq[s + 1, 1]
        cross_real = real * next_real + imag * next_imag
        cross_imag = imag * next_real - real * next_imag
        magnitude = jnp.sqrt(cross_real * cross_real + cross_imag * cross_imag)
        damping = (0.5 / (side * side)) * total(magnitude) + 1e-6
        scaled = 1.0 / (magnitude + damping)
        high, low = split(jnp.concatenate([cross_real * scaled, cross_imag * scaled], 1))
        rows.append(jnp.concatenate([high, low, high], 1))
    back = dot(jnp.concatenate(rows, 0), turn[...])
    copies = []
    for s in range(secs - 1):
        one = back[s * side : (s + 1) * side]
        high, low = split(jnp.concatenate([one[:, :side], one[:, side:]], 0))
        held[s] = dot(close[...], jnp.concatenate([high, low, high], 0))
        copies.append(pltpu.make_async_copy(held.at[s], out.at[s], sent.at[s]))
        copies[-1].start()
    for copy in copies:
        copy.wait()


def in_hbm(x):
    return pltpu.with_memory_space_constraint(x, pltpu.HBM)


def halves(x):
    high = x.astype(jnp.bfloat16)
    return high, (x - high.astype(np.float32)).astype(jnp.bfloat16)


def dft_tables(length):
    indices = np.arange(length)
    angles = (indices[:, None] * indices[None, :] % length) * (2.0 * math.pi / length)
    cosine, sine = np.cos(angles).astype(np.float32), np.sin(angles).astype(np.float32)
    left = np.concatenate(halves(np.concatenate([cosine, sine], 0)), 1)
    high, low = halves(np.concatenate([cosine, sine], 1))
    right = np.concatenate([high, high, low], 0)
    high, low = halves(
        np.concatenate(
            [np.concatenate([cosine, sine], 1), np.concatenate([-sine, cosine], 1)], 0
        )
    )
    turn = np.concatenate([high, high, low], 0)
    high, low = halves(np.concatenate([cosine, -sine], 1) / np.float32(length))
    close = np.concatenate([high, high, low], 1)
    return [jnp.asarray(t) for t in (left, right, turn, close)]


def per_device(section_pixels, jitter_index, drift_list, blend_weight, patch_col):
    pixels = section_pixels[0]
    rows, width = pixels.shape
    blocks = width // BLOCK
    owners = lax.axis_size(BANDS)
    secs = lax.axis_size("sec")
    chunks = 8
    drifts = jnp.transpose(drift_list[0], (2, 0, 1))
    f32, bf16 = jnp.float32, jnp.bfloat16
    vmem = pl.BlockSpec(memory_space=pltpu.VMEM)
    smem = pl.BlockSpec(memory_space=pltpu.SMEM)
    hbm = pl.BlockSpec(memory_space=pltpu.HBM)
    shape = jax.ShapeDtypeStruct
    message_rows = [
        CAP * BLOCK + (3 if has_tail(k, owners) else 2) * blocks for k in range(1, owners)
    ]
    params = pltpu.CompilerParams(vmem_limit_bytes=24 * 1024 * 1024)
    jitter, half, padded, edges, *messages = pl.pallas_call(
        functools.partial(front_kernel, owners, chunks),
        out_shape=[
            shape((1, rows), f32),
            shape((rows, BLOCK), f32),
            shape((blocks + 2, rows + SUB, BLOCK), f32),
            shape((2, blocks, BLOCK), f32),
        ]
        + [shape((r, BLOCK), bf16) for r in message_rows],
        in_specs=[hbm] * 3,
        out_specs=[vmem] * (3 + owners),
        scratch_shapes=[
            pltpu.VMEM((rows, width), f32),
            pltpu.VMEM((blocks, rows + SUB, BLOCK), f32),
            pltpu.VMEM((rows, rows), jnp.int32),
            pltpu.VMEM((2, rows, BLOCK), f32),
            pltpu.VMEM((1, rows), jnp.int32),
            pltpu.SMEM(drifts.shape, jnp.int32),
            pltpu.SemaphoreType.DMA((chunks + 2,)),
        ],
        compiler_params=params,
        name="front",
    )(*map(in_hbm, (jitter_index, drifts, pixels)))
    begun, own = pl.pallas_call(
        functools.partial(plan_kernel, owners, secs),
        out_shape=[shape((secs, PATCH, PATCH), f32), shape((CAP * BLOCK, BLOCK), bf16)],
        in_specs=[smem, smem, vmem, vmem],
        out_specs=[vmem] * 2,
        compiler_params=params,
        cost_estimate=pl.CostEstimate(flops=10**8, bytes_accessed=10**6, transcendentals=0),
        name="plan",
    )(drifts, patch_col, half, padded)
    messages = [own] + [send(messages[k - 1], BANDS, k, owners) for k in range(1, owners)]
    jitter, *windows = pl.pallas_call(
        functools.partial(blend_kernel, owners, secs),
        out_shape=[shape((1, rows), f32)] + [shape((PATCH, PATCH), bf16)] * secs,
        in_specs=[smem, smem, smem] + [vmem] * (3 + owners),
        out_specs=[vmem] * (1 + secs),
        scratch_shapes=[pltpu.VMEM((owners, blocks, BLOCK), f32)] * 4
        + [pltpu.VMEM((secs, PATCH, PATCH), f32), pltpu.VMEM((secs, 1, PATCH), f32)],
        compiler_params=params,
        name="blend",
    )(drifts, blend_weight, patch_col, jitter, edges, begun, *messages)
    windows = windows[:1] + [send(windows[k], "sec", k, secs) for k in range(1, secs)]
    left, right, turn, close = dft_tables(PATCH)
    begin = secs // 2
    early = pl.pallas_call(
        spectrum_kernel,
        out_shape=shape((begin, 2, PATCH, PATCH), f32),
        in_specs=[vmem] * (2 + begin),
        out_specs=vmem,
        compiler_params=params,
        cost_estimate=pl.CostEstimate(flops=10**8, bytes_accessed=10**6, transcendentals=0),
        name="spectrum",
    )(left, right, *windows[:begin])
    surfaces = pl.pallas_call(
        functools.partial(surface_kernel, secs),
        out_shape=shape((secs - 1, PATCH, PATCH), f32),
        in_specs=[vmem] * (5 + secs - begin),
        out_specs=hbm,
        scratch_shapes=[
            pltpu.VMEM((secs, 2, PATCH, PATCH), f32),
            pltpu.VMEM((secs - 1, PATCH, PATCH), f32),
            pltpu.SemaphoreType.DMA((secs - 1,)),
        ],
        compiler_params=params,
        name="surface",
    )(left, right, turn, close, early, *windows[begin:])
    return (jitter, surfaces[:, None, None])


def solution(mesh):
    in_specs = (
        P(("groups", "sec"), ("tile", "row"), None),
        P(("groups", "sec"), ("tile", "row")),
        P(("groups", "sec"), None, None, None),
        P(("groups", "sec"), None, None),
        P(("tile", "row"), "groups"),
    )
    out_specs = (
        P(("groups", "sec"), ("tile", "row")),
        P("groups", ("tile", "row"), "sec", None, None),
    )
    return jax.shard_map(
        per_device, mesh=mesh, in_specs=in_specs, out_specs=out_specs, check_vma=False
    )
```

time: 34.8 us -> 27.4 us (0.79)
  waiting for transfers between devices: 10.6 us -> 7.35 us
  local copies, waits for them, and re-layouts: 3.7 us -> 1.38 us
  Pallas kernels: 12.1 us -> 10.1 us
    ppermute x6, waiting for transfers between devices: 10.6 us -> 7.35 us  [send(): return lax.ppermute(x, axis, [(i, target(i, k, n)) for i in range(n)])]
    pallas_call x1, Pallas kernels: 5.01 us -> 2.03 us  [per_device(): pl.pallas_call(functools.partial(surface_kernel, secs), out_shape=shape((...]
    unnamed x11 -> x14, local copies, waits for them, and re-layouts: 3.7 us -> 1.38 us
    pallas_call x1 -> x3, Pallas kernels: 4.8 us -> 6.3 us  [the longest x1 4.44 us: per_device(): pl.pallas_call(functools.partial(front_kernel, owners, chunks), out_shape...]
    pallas_call x1, Pallas kernels: 2.34 us -> 1.76 us  [per_device(): pl.pallas_call(functools.partial(blend_kernel, owners, secs), out_shape=[...]
  transfers between devices with their start and end apart: 6 -> 6, of which waited for: 3 -> 3; matrix products, arithmetic and copies ran while one was open for 0% -> 0% of each run, Pallas kernels for 0% -> 7%
where the time goes in v2:
time: 27.4 us; the launch traced here: 27.2 us
  Pallas kernels  10.1 us (37%)
  starting transfers between devices  7.64 us (28%)
  waiting for transfers between devices  7.35 us (27%)
  local copies, waits for them, and re-layouts  1.38 us (5%)
  between operations  0.71 us (3%)
    ppermute x6, starting transfers between devices, send(): return lax.ppermute(x, axis, [(i, target(i, k, n)) for i in range(n)])  7.64 us
    ppermute x6, waiting for transfers between devices, send(): return lax.ppermute(x, axis, [(i, target(i, k, n)) for i in range(n)])  7.35 us
    pallas_call x1, Pallas kernels, per_device(): pl.pallas_call(functools.partial(front_kernel, owners, chunks), out_shape...  4.44 us
    pallas_call x1, Pallas kernels, per_device(): pl.pallas_call(functools.partial(surface_kernel, secs), out_shape=shape((...  2.03 us
    pallas_call x1, Pallas kernels, per_device(): pl.pallas_call(functools.partial(blend_kernel, owners, secs), out_shape=[...  1.76 us
    unnamed x14, local copies, waits for them, and re-layouts  1.38 us
    pallas_call x1, Pallas kernels, per_device(): pl.pallas_call(functools.partial(plan_kernel, owners, secs), out_shape=[s...  1.38 us
  transfers between devices with their start and end apart: 6, of which 3 were waited for; matrix products, arithmetic and copies ran while one was open for 0% of the time, Pallas kernels for 7%

profile of v2, /device:TPU:0, one launch (start us, length us, event | category | flops | bytes accessed | tf_op | source)
XLA Modules:
  0.0 27.2 jit_solution(8345247700293124379)
XLA Ops:
  0.6 0.0 copy-start.5
  0.6 0.0 copy-start
  0.7 0.0 copy-start.1
  0.7 4.4 %front.1 = (f32[1,128]{1,0:T(1,128)S(1)}, f32[128,128]{1,0:T(8,128)S(1)}, f32[34,136,128]{2,1,0:T(8,128)S(1)}, f32[2,32,128]{2,1,0:T(8,128)S(1)}, bf16[352,128]{...) custom-call(s32[1,128]{1,0:T(1,128)} %delay_at.1, s32[3,4,8]{2,1,0:T(4,128)} %bitcast.7, ...), custom_call_target="tpu_custom_call" | custom-call | tf_op jit(solution)/shard_map/front/pallas_call | solution.py:410
  5.1 0.0 copy-start.2
  5.1 0.0 copy-start.3
  5.1 0.5 %collective-permute-start = (bf16[352,128]{1,0:T(8,128)(2,1)S(1)}, bf16[352,128]{1,0:T(8,128)(2,1)S(1)}, u32[]{:S(2)}, u32[]{:S(2)}) collective-permute-start(bf16[352,128]{1,0:T(8,128)(2,1)S(1)} %get-tuple-element.22), channel_id=1, source_target_pairs={{0,1},{1,0},{2,3},{3,2},{4,5},{5,4},{6,7},{7,6},{8,9},{9,8},{10,11... | collective-permute-start | bytes 270344 | tf_op jit(solution)/shard_map/ppermute | solution.py:33
  5.7 2.6 %collective-permute-start.2 = (bf16[352,128]{1,0:T(8,128)(2,1)S(1)}, bf16[352,128]{1,0:T(8,128)(2,1)S(1)}, u32[]{:S(2)}, u32[]{:S(2)}) collective-permute-start(bf16[352,128]{1,0:T(8,128)(2,1)S(1)} %get-tuple-element.24), channel_id=1, source_target_pairs={{0,3},{1,2},{2,1},{3,0},{4,7},{5,6},{6,5},{7,4},{8,11},{9,10},{10,... | collective-permute-start | bytes 270344 | tf_op jit(solution)/shard_map/ppermute | solution.py:33
  8.3 0.0 collective-permute-start.1
  8.3 0.0 copy-start.4
  8.3 0.7 %copy-done.4 = s32[1,4,8,3]{2,1,3,0:T(4,128)S(1)} copy-done((s32[1,4,8,3]{2,1,3,0:T(4,128)S(1)}, s32[1,4,8,3]{2,1,3,0:T(4,128)}, u32[]{:S(2)}) %copy-start.4) | copy-done | bytes 408
  9.0 0.0 copy-start.6
  9.0 0.7 %copy-done.6 = s32[1,4]{1,0:T(1,128)S(1)} copy-done((s32[1,4]{1,0:T(1,128)S(1)}, s32[1,4]{1,0:T(1,128)}, u32[]{:S(2)}) %copy-start.6) | copy-done | bytes 40
  9.7 1.4 %plan.1 = (f32[4,128,128]{2,1,0:T(8,128)S(1)}, bf16[256,128]{1,0:T(8,128)(2,1)S(1)}) custom-call(s32[3,4,8]{2,1,0:T(4,128)S(1)} %bitcast.8, s32[1,4]{1,0:T(1,128)S(1)} %copy-done.6, f32[128,128]{1,0:T(8,128)S(1)} %get-tuple-element.18.half_in, f32[34,136,128]{2,1,0:T(8,128)S(1)} %get-tuple-element.19.padded), custom_call_target="tpu_custom_call" | custom-call | flops 100000000 | bytes 1000000 | tf_op jit(solution)/shard_map/plan/pallas_call | solution.py:433
  11.0 2.1 %collective-permute-done.1.refs_2_ = bf16[320,128]{1,0:T(8,128)(2,1)S(1)} collective-permute-done((bf16[320,128]{1,0:T(8,128)(2,1)S(1)}, bf16[320,128]{1,0:T(8,128)(2,1)S(1)}, u32[]{:S(2)}, u32[]{:S(2)}) %collective-permute-start.1) | collective-permute-done | bytes 81952 | tf_op jit(solution)/shard_map/ppermute | solution.py:33
  13.2 0.0 collective-permute-done.refs_1_
  13.2 0.0 collective-permute-done.2.refs_3_
  13.2 0.0 copy-done.5
  13.2 1.8 %blend.1 = (f32[1,128]{1,0:T(1,128)}, bf16[128,128]{1,0:T(8,128)(2,1)S(1)}, bf16[128,128]{1,0:T(8,128)(2,1)S(1)}, bf16[128,128]{1,0:T(8,128)(2,1)S(1)}, bf16[128,128]{1,0:T(8,128)(2,1)S(1)}) custom-call(s32[3,4,8]{2,1,0:T(4,128)S(1)} %bitcast.9, f32[1,4,8]{2,1,0:T(4,128)S(1)} %copy-done.5, s32[1,4]{1,0:T(1,128)S(1)} %copy-done.6, ...), custom_call_target="tpu_custom_call" | custom-call | tf_op jit(solution)/shard_map/blend/pallas_call | solution.py:443
  15.0 1.8 %collective-permute-start.3 = (bf16[128,128]{1,0:T(8,128)(2,1)S(1)}, bf16[128,128]{1,0:T(8,128)(2,1)S(1)}, u32[]{:S(2)}, u32[]{:S(2)}) collective-permute-start(bf16[128,128]{1,0:T(8,128)(2,1)S(1)} %get-tuple-element.27), channel_id=1, source_target_pairs={{0,4},{4,0},{8,12},{12,8},{1,5},{5,1},{9,13},{13,9},{2,6},{6,2},{1... | collective-permute-start | bytes 98312 | tf_op jit(solution)/shard_map/ppermute | solution.py:33
  16.8 2.7 %collective-permute-start.4 = (bf16[128,128]{1,0:T(8,128)(2,1)S(1)}, bf16[128,128]{1,0:T(8,128)(2,1)S(1)}, u32[]{:S(2)}, u32[]{:S(2)}) collective-permute-start(bf16[128,128]{1,0:T(8,128)(2,1)S(1)} %get-tuple-element.28), channel_id=1, source_target_pairs={{0,8},{4,12},{8,0},{12,4},{1,9},{5,13},{9,1},{13,5},{2,10},{6,14},... | collective-permute-start | bytes 98312 | tf_op jit(solution)/shard_map/ppermute | solution.py:33
  19.4 0.0 collective-permute-start.5
  19.4 0.0 collective-permute-done.3.refs_1_
  19.4 0.0 copy-done
  19.4 0.0 copy-done.1
  19.4 0.5 %spectrum.1.early = f32[2,2,128,128]{3,2,1,0:T(8,128)S(1)} custom-call(bf16[256,256]{1,0:T(8,128)(2,1)S(1)} %copy-done.1, bf16[384,256]{1,0:T(8,128)(2,1)S(1)} %copy-done, bf16[128,128]{1,0:T(8,128)(2,1)S(1)} %get-tuple-element.26.refs_0_, bf16[128,128]{1,0:T(8,128)(2,1)S(1)} %collective-permute-done.3.refs_1_), custom_call_target="tpu_custom_call" | custom-call | flops 100000000 | bytes 1000000 | tf_op jit(solution)/shard_map/spectrum/pallas_call | solution.py:456
  19.9 2.0 %collective-permute-done.4.refs_0_ = bf16[128,128]{1,0:T(8,128)(2,1)S(1)} collective-permute-done((bf16[128,128]{1,0:T(8,128)(2,1)S(1)}, bf16[128,128]{1,0:T(8,128)(2,1)S(1)}, u32[]{:S(2)}, u32[]{:S(2)}) %collective-permute-start.4) | collective-permute-done | bytes 32800 | tf_op jit(solution)/shard_map/ppermute | solution.py:33
  21.9 3.2 %collective-permute-done.5.refs_1_ = bf16[128,128]{1,0:T(8,128)(2,1)S(1)} collective-permute-done((bf16[128,128]{1,0:T(8,128)(2,1)S(1)}, bf16[128,128]{1,0:T(8,128)(2,1)S(1)}, u32[]{:S(2)}, u32[]{:S(2)}) %collective-permute-start.5) | collective-permute-done | bytes 32800 | tf_op jit(solution)/shard_map/ppermute | solution.py:33
  25.1 0.0 copy-done.2
  25.1 0.0 copy-done.3
  25.1 2.0 %surface.1 = f32[3,128,128]{2,1,0:T(8,128)} custom-call(bf16[256,256]{1,0:T(8,128)(2,1)S(1)} %copy-done.1, bf16[384,256]{1,0:T(8,128)(2,1)S(1)} %copy-done, bf16[768,256]{1,0:T(8,128)(2,1)S(1)} %copy-done.2, bf16[128,768]{1,0:T(8,128)(2,1)S(1)} %copy-done.3, f32[2,2,128,128]{3,2,1,0:T(8,128)S(1)} %spectrum.1.early, ...), custom_call_target="tpu_custom_call" | custom-call | tf_op jit(solution)/shard_map/surface/pallas_call | solution.py:465
Async XLA Ops:
  0.6 12.6 %copy-start.5 = (f32[1,4,8]{2,1,0:T(4,128)S(1)}, f32[1,4,8]{2,1,0:T(4,128)}, u32[]{:S(2)}) copy-start(f32[1,4,8]{2,1,0:T(4,128)} %weight.1) | copy-start | bytes 388
  0.6 18.8 %copy-start = (bf16[384,256]{1,0:T(8,128)(2,1)S(1)}, bf16[384,256]{1,0:T(8,128)(2,1)}, u32[]{:S(2)}) copy-start(bf16[384,256]{1,0:T(8,128)(2,1)} %constant.9.clone.right) | copy-start | bytes 589828
  0.7 18.8 %copy-start.1 = (bf16[256,256]{1,0:T(8,128)(2,1)S(1)}, bf16[256,256]{1,0:T(8,128)(2,1)}, u32[]{:S(2)}) copy-start(bf16[256,256]{1,0:T(8,128)(2,1)} %constant.8.clone.left) | copy-start | bytes 393220
  5.1 20.0 %copy-start.2 = (bf16[768,256]{1,0:T(8,128)(2,1)S(1)}, bf16[768,256]{1,0:T(8,128)(2,1)}, u32[]{:S(2)}) copy-start(bf16[768,256]{1,0:T(8,128)(2,1)} %constant.10.clone.turn) | copy-start | bytes 1179652
  5.1 20.0 %copy-start.3 = (bf16[128,768]{1,0:T(8,128)(2,1)S(1)}, bf16[128,768]{1,0:T(8,128)(2,1)}, u32[]{:S(2)}) copy-start(bf16[128,768]{1,0:T(8,128)(2,1)} %constant.11.clone.close) | copy-start | bytes 589828
  5.1 8.1 %collective-permute-start = (bf16[352,128]{1,0:T(8,128)(2,1)S(1)}, bf16[352,128]{1,0:T(8,128)(2,1)S(1)}, u32[]{:S(2)}, u32[]{:S(2)}) collective-permute-start(bf16[352,128]{1,0:T(8,128)(2,1)S(1)} %get-tuple-element.22), channel_id=1, source_target_pairs={{0,1},{1,0},{2,3},{3,2},{4,5},{5,4},{6,7},{7,6},{8,9},{9,8},{10,11... | collective-permute-start | bytes 270344 | tf_op jit(solution)/shard_map/ppermute | solution.py:33
  5.7 7.5 %collective-permute-start.2 = (bf16[352,128]{1,0:T(8,128)(2,1)S(1)}, bf16[352,128]{1,0:T(8,128)(2,1)S(1)}, u32[]{:S(2)}, u32[]{:S(2)}) collective-permute-start(bf16[352,128]{1,0:T(8,128)(2,1)S(1)} %get-tuple-element.24), channel_id=1, source_target_pairs={{0,3},{1,2},{2,1},{3,0},{4,7},{5,6},{6,5},{7,4},{8,11},{9,10},{10,... | collective-permute-start | bytes 270344 | tf_op jit(solution)/shard_map/ppermute | solution.py:33
  8.3 4.9 %collective-permute-start.1 = (bf16[320,128]{1,0:T(8,128)(2,1)S(1)}, bf16[320,128]{1,0:T(8,128)(2,1)S(1)}, u32[]{:S(2)}, u32[]{:S(2)}) collective-permute-start(bf16[320,128]{1,0:T(8,128)(2,1)S(1)} %get-tuple-element.23), channel_id=1, source_target_pairs={{0,2},{1,3},{2,0},{3,1},{4,6},{5,7},{6,4},{7,5},{8,10},{9,11},{10,... | collective-permute-start | bytes 245768 | tf_op jit(solution)/shard_map/ppermute | solution.py:33
  8.3 0.7 %copy-start.4 = (s32[1,4,8,3]{2,1,3,0:T(4,128)S(1)}, s32[1,4,8,3]{2,1,3,0:T(4,128)}, u32[]{:S(2)}) copy-start(s32[1,4,8,3]{2,1,3,0:T(4,128)} %param.11) | copy-start | bytes 1156
  9.0 0.7 %copy-start.6 = (s32[1,4]{1,0:T(1,128)S(1)}, s32[1,4]{1,0:T(1,128)}, u32[]{:S(2)}) copy-start(s32[1,4]{1,0:T(1,128)} %pcol.3) | copy-start | bytes 52
  15.0 4.5 %collective-permute-start.3 = (bf16[128,128]{1,0:T(8,128)(2,1)S(1)}, bf16[128,128]{1,0:T(8,128)(2,1)S(1)}, u32[]{:S(2)}, u32[]{:S(2)}) collective-permute-start(bf16[128,128]{1,0:T(8,128)(2,1)S(1)} %get-tuple-element.27), channel_id=1, source_target_pairs={{0,4},{4,0},{8,12},{12,8},{1,5},{5,1},{9,13},{13,9},{2,6},{6,2},{1... | collective-permute-start | bytes 98312 | tf_op jit(solution)/shard_map/ppermute | solution.py:33
  16.8 5.1 %collective-permute-start.4 = (bf16[128,128]{1,0:T(8,128)(2,1)S(1)}, bf16[128,128]{1,0:T(8,128)(2,1)S(1)}, u32[]{:S(2)}, u32[]{:S(2)}) collective-permute-start(bf16[128,128]{1,0:T(8,128)(2,1)S(1)} %get-tuple-element.28), channel_id=1, source_target_pairs={{0,8},{4,12},{8,0},{12,4},{1,9},{5,13},{9,1},{13,5},{2,10},{6,14},... | collective-permute-start | bytes 98312 | tf_op jit(solution)/shard_map/ppermute | solution.py:33
  19.4 5.7 %collective-permute-start.5 = (bf16[128,128]{1,0:T(8,128)(2,1)S(1)}, bf16[128,128]{1,0:T(8,128)(2,1)S(1)}, u32[]{:S(2)}, u32[]{:S(2)}) collective-permute-start(bf16[128,128]{1,0:T(8,128)(2,1)S(1)} %get-tuple-element.29), channel_id=1, source_target_pairs={{0,12},{4,8},{8,4},{12,0},{1,13},{5,9},{9,5},{13,1},{2,14},{6,10},... | collective-permute-start | bytes 98312 | tf_op jit(solution)/shard_map/ppermute | solution.py:33

commit v3 on v2

--- a/solution.py
+++ b/solution.py
@@ -14,6 +14,7 @@
 BLOCK = 128
 CAP = 2
 SUB = 8
+PAD = 16
 BANDS = ("tile", "row")
 
 
@@ -35,6 +36,11 @@
 
 def has_tail(k, n):
     return any(target(i, k, n) == (i + 1) % n for i in range(n))
+
+
+def patch_order(n):
+    half = n // 2
+    return [0, half] + [k for k in range(n - 1, 0, -1) if k != half]
 
 
 def find_slots(drift, band, owner, count):
@@ -81,15 +87,23 @@
     small[1].start()
     padded[0] = jnp.zeros(padded.shape[1:], jnp.float32)
     padded[blocks + 1] = jnp.zeros(padded.shape[1:], jnp.float32)
-    padded[1 : blocks + 1, 0:SUB, :] = jnp.zeros((blocks, SUB, BLOCK), jnp.float32)
-    ring[:, 0:SUB, :] = jnp.zeros((blocks, SUB, BLOCK), jnp.float32)
+    padded[1 : blocks + 1, 0:PAD, :] = jnp.zeros((blocks, PAD, BLOCK), jnp.float32)
+    ring[:, 0:PAD, :] = jnp.zeros((blocks, PAD, BLOCK), jnp.float32)
     small[0].wait()
     wide[...] = jnp.broadcast_to(delay[...], (rows, rows)).T
     lane = lax.broadcasted_iota(jnp.int32, (SUB, BLOCK), 1)
-    sub = lax.broadcasted_iota(jnp.int32, (SUB, BLOCK), 0)
     last_lane = lane == BLOCK - 1
-    first_sub = sub == 0
     seg = SEG // BLOCK
+
+    def relate(at):
+        cross = power = jnp.zeros((SUB, BLOCK), jnp.float32)
+        here, over = pl.ds(at + PAD, SUB), pl.ds(at + (PAD - 1), SUB)
+        for v in range(blocks):
+            x, behind = padded[v + 1, here, :], ring[v, here, :]
+            cross = cross + (padded[v + 1, over, :] * behind - ring[v, over, :] * x)
+            power = power + x * x
+        sums[0, pl.ds(at + SUB, SUB), :] = cross
+        sums[1, pl.ds(at + SUB, SUB), :] = power
 
     def eight_rows(g, _):
         at = pl.multiple_of(g * SUB, SUB)
@@ -108,34 +122,25 @@
         ]
         picked.append(jnp.zeros((SUB, BLOCK), jnp.float32))
         x = [jnp.where(near, picked[v], picked[v + 1]) for v in range(blocks)]
-        zero = jnp.zeros((SUB, BLOCK), jnp.float32)
-        cross = zero
-        power = zero
         for v in range(blocks):
             prv = x[v - 1] if v % seg else x[v + seg - 1]
-            behind = pltpu.roll(jnp.where(last_lane, prv, x[v]), 1, 1)
-            above = jnp.where(
-                first_sub, padded[v + 1, pl.ds(at + SUB - 1, 1), :], pltpu.roll(x[v], 1, 0)
-            )
-            above_behind = jnp.where(
-                first_sub, ring[v, pl.ds(at + SUB - 1, 1), :], pltpu.roll(behind, 1, 0)
-            )
-            cross = cross + (above * behind - above_behind * x[v])
-            power = power + x[v] * x[v]
-            padded[v + 1, pl.ds(at + SUB, SUB), :] = x[v]
-            ring[v, pl.ds(at + SUB, SUB), :] = behind
-        sums[0, pl.ds(at, SUB), :] = cross
-        sums[1, pl.ds(at, SUB), :] = power
+            padded[v + 1, pl.ds(at + PAD, SUB), :] = x[v]
+            ring[v, pl.ds(at + PAD, SUB), :] = pltpu.roll(jnp.where(last_lane, prv, x[v]), 1, 1)
+        return 0
+
+    def again(g, _):
+        relate(pl.multiple_of(g * SUB, SUB))
         return 0
 
     steps = per // SUB
     for i in range(chunks):
         load(i).wait()
-        lax.fori_loop(i * steps, (i + 1) * steps, eight_rows, 0)
+        lax.fori_loop(i * steps, (i + 1) * steps, eight_rows, 0, unroll=4)
+        lax.fori_loop(i * steps, (i + 1) * steps, again, 0, unroll=4)
 
     small[1].wait()
-    total_cross = jnp.sum(sums[0], axis=1, keepdims=True)
-    total_power = jnp.sum(sums[1], axis=1, keepdims=True)
+    total_cross = jnp.sum(sums[0, SUB:], axis=1, keepdims=True)
+    total_power = jnp.sum(sums[1, SUB:], axis=1, keepdims=True)
     row_index = lax.broadcasted_iota(jnp.int32, (rows, BLOCK), 0)
     power = jnp.broadcast_to(total_power, (rows, BLOCK))
     power = power + jnp.where(row_index == 0, 0.0, pltpu.roll(power, 1, 0))
@@ -152,8 +157,8 @@
             ).astype(jnp.bfloat16)
     jitter_out[...] = jitter.T[0:1, :]
     for v in range(blocks):
-        first_out[0, v : v + 1, :] = padded[v + 1, SUB : SUB + 1, :]
-        first_out[1, v : v + 1, :] = padded[v + 1, SUB + rows - 1 : SUB + rows, :]
+        first_out[0, v : v + 1, :] = padded[v + 1, PAD : PAD + 1, :]
+        first_out[1, v : v + 1, :] = padded[v + 1, PAD + rows - 1 : PAD + rows, :]
     first = first_out[0].astype(jnp.bfloat16)
     last, rest = split(first_out[1])
     base = CAP * BLOCK
@@ -167,10 +172,10 @@
 
 def corrected(padded, half, n):
     rows = half.shape[0]
-    here = padded[n + 1, SUB : SUB + rows, :]
+    here = padded[n + 1, PAD : PAD + rows, :]
     lane = lax.broadcasted_iota(jnp.int32, here.shape, 1)
-    left = jnp.where(lane == BLOCK - 1, padded[n, SUB : SUB + rows, :], here)
-    right = jnp.where(lane == 0, padded[n + 2, SUB : SUB + rows, :], here)
+    left = jnp.where(lane == BLOCK - 1, padded[n, PAD : PAD + rows, :], here)
+    right = jnp.where(lane == 0, padded[n + 2, PAD : PAD + rows, :], here)
     return here - half * (pltpu.roll(right, BLOCK - 1, 1) - pltpu.roll(left, 1, 1))
 
 
@@ -334,10 +339,11 @@
     sec = lax.axis_index("sec")
     side = PATCH
     begun = early.shape[0]
+    order = patch_order(secs)
     for k in range(begun):
-        freq[origin(sec, k, secs)] = early[k]
+        freq[origin(sec, order[k], secs)] = early[k]
     for k, (real, imag) in enumerate(spectra([p[...] for p in late], left[...], right[...])):
-        at = origin(sec, begun + k, secs)
+        at = origin(sec, order[begun + k], secs)
         freq[at, 0] = real
         freq[at, 1] = imag
     rows = []
@@ -396,7 +402,7 @@
     blocks = width // BLOCK
     owners = lax.axis_size(BANDS)
     secs = lax.axis_size("sec")
-    chunks = 8
+    chunks = 4
     drifts = jnp.transpose(drift_list[0], (2, 0, 1))
     f32, bf16 = jnp.float32, jnp.bfloat16
     vmem = pl.BlockSpec(memory_space=pltpu.VMEM)
@@ -412,7 +418,7 @@
         out_shape=[
             shape((1, rows), f32),
             shape((rows, BLOCK), f32),
-            shape((blocks + 2, rows + SUB, BLOCK), f32),
+            shape((blocks + 2, rows + PAD, BLOCK), f32),
             shape((2, blocks, BLOCK), f32),
         ]
         + [shape((r, BLOCK), bf16) for r in message_rows],
@@ -420,9 +426,9 @@
         out_specs=[vmem] * (3 + owners),
         scratch_shapes=[
             pltpu.VMEM((rows, width), f32),
-            pltpu.VMEM((blocks, rows + SUB, BLOCK), f32),
+            pltpu.VMEM((blocks, rows + PAD, BLOCK), f32),
             pltpu.VMEM((rows, rows), jnp.int32),
-            pltpu.VMEM((2, rows, BLOCK), f32),
+            pltpu.VMEM((2, rows + SUB, BLOCK), f32),
             pltpu.VMEM((1, rows), jnp.int32),
             pltpu.SMEM(drifts.shape, jnp.int32),
             pltpu.SemaphoreType.DMA((chunks + 2,)),
@@ -450,7 +456,8 @@
         compiler_params=params,
         name="blend",
     )(drifts, blend_weight, patch_col, jitter, edges, begun, *messages)
-    windows = windows[:1] + [send(windows[k], "sec", k, secs) for k in range(1, secs)]
+    order = patch_order(secs)
+    windows = windows[:1] + [send(windows[k], "sec", k, secs) for k in order[1:]]
     left, right, turn, close = dft_tables(PATCH)
     begin = secs // 2
     early = pl.pallas_call(

time: 27.4 us -> 25.2 us (0.920)
  waiting for transfers between devices: 7.35 us -> 5.74 us
  Pallas kernels: 10.1 us -> 9.33 us
    ppermute x6, waiting for transfers between devices: 7.35 us -> 5.74 us  [send(): return lax.ppermute(x, axis, [(i, target(i, k, n)) for i in range(n)])]
    pallas_call x1, Pallas kernels: 4.44 us -> 3.74 us  [per_device(): pl.pallas_call(functools.partial(front_kernel, owners, chunks), out_shape...]
where the time goes in v3:
time: 25.2 us; the launch traced here: 25 us
  Pallas kernels  9.33 us (37%)
  starting transfers between devices  7.86 us (31%)
  waiting for transfers between devices  5.74 us (23%)
  local copies, waits for them, and re-layouts  1.38 us (5%)
  between operations  0.71 us (3%)
    ppermute x6, starting transfers between devices, send(): return lax.ppermute(x, axis, [(i, target(i, k, n)) for i in range(n)])  7.86 us
    ppermute x6, waiting for transfers between devices, send(): return lax.ppermute(x, axis, [(i, target(i, k, n)) for i in range(n)])  5.74 us
    pallas_call x1, Pallas kernels, per_device(): pl.pallas_call(functools.partial(front_kernel, owners, chunks), out_shape...  3.74 us
    pallas_call x1, Pallas kernels, per_device(): pl.pallas_call(functools.partial(surface_kernel, secs), out_shape=shape((...  2.04 us
    pallas_call x1, Pallas kernels, per_device(): pl.pallas_call(functools.partial(blend_kernel, owners, secs), out_shape=[...  1.68 us
    unnamed x14, local copies, waits for them, and re-layouts  1.38 us
    pallas_call x1, Pallas kernels, per_device(): pl.pallas_call(functools.partial(plan_kernel, owners, secs), out_shape=[s...  1.38 us
  transfers between devices with their start and end apart: 6, of which 3 were waited for; matrix products, arithmetic and copies ran while one was open for 0% of the time, Pallas kernels for 7%

profile of v3, /device:TPU:0, one launch (start us, length us, event | category | flops | bytes accessed | tf_op | source)
XLA Modules:
  0.0 25.0 jit_solution(8574582605723067610)
XLA Ops:
  0.6 0.0 copy-start.5
  0.6 0.0 copy-start
  0.7 0.0 copy-start.1
  0.7 0.0 copy-start.2
  0.7 0.0 copy-start.3
  0.7 3.7 %front.1 = (f32[1,128]{1,0:T(1,128)S(1)}, f32[128,128]{1,0:T(8,128)S(1)}, f32[34,144,128]{2,1,0:T(8,128)S(1)}, f32[2,32,128]{2,1,0:T(8,128)S(1)}, bf16[352,128]{...) custom-call(s32[1,128]{1,0:T(1,128)} %delay_at.1, s32[3,4,8]{2,1,0:T(4,128)} %bitcast.7, ...), custom_call_target="tpu_custom_call" | custom-call | tf_op jit(solution)/shard_map/front/pallas_call | solution.py:416
  4.4 0.5 %collective-permute-start = (bf16[352,128]{1,0:T(8,128)(2,1)S(1)}, bf16[352,128]{1,0:T(8,128)(2,1)S(1)}, u32[]{:S(2)}, u32[]{:S(2)}) collective-permute-start(bf16[352,128]{1,0:T(8,128)(2,1)S(1)} %get-tuple-element.22), channel_id=1, source_target_pairs={{0,1},{1,0},{2,3},{3,2},{4,5},{5,4},{6,7},{7,6},{8,9},{9,8},{10,11... | collective-permute-start | bytes 270344 | tf_op jit(solution)/shard_map/ppermute | solution.py:34
  5.0 2.6 %collective-permute-start.2 = (bf16[352,128]{1,0:T(8,128)(2,1)S(1)}, bf16[352,128]{1,0:T(8,128)(2,1)S(1)}, u32[]{:S(2)}, u32[]{:S(2)}) collective-permute-start(bf16[352,128]{1,0:T(8,128)(2,1)S(1)} %get-tuple-element.24), channel_id=1, source_target_pairs={{0,3},{1,2},{2,1},{3,0},{4,7},{5,6},{6,5},{7,4},{8,11},{9,10},{10,... | collective-permute-start | bytes 270344 | tf_op jit(solution)/shard_map/ppermute | solution.py:34
  7.6 0.0 collective-permute-start.1
  7.6 0.0 copy-start.4
  7.6 0.7 %copy-done.4 = s32[1,4,8,3]{2,1,3,0:T(4,128)S(1)} copy-done((s32[1,4,8,3]{2,1,3,0:T(4,128)S(1)}, s32[1,4,8,3]{2,1,3,0:T(4,128)}, u32[]{:S(2)}) %copy-start.4) | copy-done | bytes 408
  8.3 0.0 copy-start.6
  8.3 0.7 %copy-done.6 = s32[1,4]{1,0:T(1,128)S(1)} copy-done((s32[1,4]{1,0:T(1,128)S(1)}, s32[1,4]{1,0:T(1,128)}, u32[]{:S(2)}) %copy-start.6) | copy-done | bytes 40
  9.0 1.4 %plan.1 = (f32[4,128,128]{2,1,0:T(8,128)S(1)}, bf16[256,128]{1,0:T(8,128)(2,1)S(1)}) custom-call(s32[3,4,8]{2,1,0:T(4,128)S(1)} %bitcast.8, s32[1,4]{1,0:T(1,128)S(1)} %copy-done.6, f32[128,128]{1,0:T(8,128)S(1)} %get-tuple-element.18.half_in, f32[34,144,128]{2,1,0:T(8,128)S(1)} %get-tuple-element.19.padded), custom_call_target="tpu_custom_call" | custom-call | flops 100000000 | bytes 1000000 | tf_op jit(solution)/shard_map/plan/pallas_call | solution.py:439
  10.3 2.1 %collective-permute-done.1.refs_2_ = bf16[320,128]{1,0:T(8,128)(2,1)S(1)} collective-permute-done((bf16[320,128]{1,0:T(8,128)(2,1)S(1)}, bf16[320,128]{1,0:T(8,128)(2,1)S(1)}, u32[]{:S(2)}, u32[]{:S(2)}) %collective-permute-start.1) | collective-permute-done | bytes 81952 | tf_op jit(solution)/shard_map/ppermute | solution.py:34
  12.5 0.0 collective-permute-done.refs_1_
  12.5 0.0 collective-permute-done.2.refs_3_
  12.5 0.0 copy-done.5
  12.5 1.7 %blend.1 = (f32[1,128]{1,0:T(1,128)}, bf16[128,128]{1,0:T(8,128)(2,1)S(1)}, bf16[128,128]{1,0:T(8,128)(2,1)S(1)}, bf16[128,128]{1,0:T(8,128)(2,1)S(1)}, bf16[128,128]{1,0:T(8,128)(2,1)S(1)}) custom-call(s32[3,4,8]{2,1,0:T(4,128)S(1)} %bitcast.9, f32[1,4,8]{2,1,0:T(4,128)S(1)} %copy-done.5, s32[1,4]{1,0:T(1,128)S(1)} %copy-done.6, ...), custom_call_target="tpu_custom_call" | custom-call | tf_op jit(solution)/shard_map/blend/pallas_call | solution.py:449
  14.2 3.1 %collective-permute-start.3 = (bf16[128,128]{1,0:T(8,128)(2,1)S(1)}, bf16[128,128]{1,0:T(8,128)(2,1)S(1)}, u32[]{:S(2)}, u32[]{:S(2)}) collective-permute-start(bf16[128,128]{1,0:T(8,128)(2,1)S(1)} %get-tuple-element.27), channel_id=1, source_target_pairs={{0,8},{4,12},{8,0},{12,4},{1,9},{5,13},{9,1},{13,5},{2,10},{6,14},... | collective-permute-start | bytes 98312 | tf_op jit(solution)/shard_map/ppermute | solution.py:34
  17.3 1.2 %collective-permute-start.4 = (bf16[128,128]{1,0:T(8,128)(2,1)S(1)}, bf16[128,128]{1,0:T(8,128)(2,1)S(1)}, u32[]{:S(2)}, u32[]{:S(2)}) collective-permute-start(bf16[128,128]{1,0:T(8,128)(2,1)S(1)} %get-tuple-element.28), channel_id=1, source_target_pairs={{0,12},{4,8},{8,4},{12,0},{1,13},{5,9},{9,5},{13,1},{2,14},{6,10},... | collective-permute-start | bytes 98312 | tf_op jit(solution)/shard_map/ppermute | solution.py:34
  18.4 0.5 %collective-permute-start.5 = (bf16[128,128]{1,0:T(8,128)(2,1)S(1)}, bf16[128,128]{1,0:T(8,128)(2,1)S(1)}, u32[]{:S(2)}, u32[]{:S(2)}) collective-permute-start(bf16[128,128]{1,0:T(8,128)(2,1)S(1)} %get-tuple-element.29), channel_id=1, source_target_pairs={{0,4},{4,0},{8,12},{12,8},{1,5},{5,1},{9,13},{13,9},{2,6},{6,2},{1... | collective-permute-start | bytes 98312 | tf_op jit(solution)/shard_map/ppermute | solution.py:34
  18.9 0.4 %collective-permute-done.3.refs_1_ = bf16[128,128]{1,0:T(8,128)(2,1)S(1)} collective-permute-done((bf16[128,128]{1,0:T(8,128)(2,1)S(1)}, bf16[128,128]{1,0:T(8,128)(2,1)S(1)}, u32[]{:S(2)}, u32[]{:S(2)}) %collective-permute-start.3) | collective-permute-done | bytes 32800 | tf_op jit(solution)/shard_map/ppermute | solution.py:34
  19.2 0.0 copy-done
  19.2 0.0 copy-done.1
  19.2 0.5 %spectrum.1.early = f32[2,2,128,128]{3,2,1,0:T(8,128)S(1)} custom-call(bf16[256,256]{1,0:T(8,128)(2,1)S(1)} %copy-done.1, bf16[384,256]{1,0:T(8,128)(2,1)S(1)} %copy-done, bf16[128,128]{1,0:T(8,128)(2,1)S(1)} %get-tuple-element.26.refs_0_, bf16[128,128]{1,0:T(8,128)(2,1)S(1)} %collective-permute-done.3.refs_1_), custom_call_target="tpu_custom_call" | custom-call | flops 100000000 | bytes 1000000 | tf_op jit(solution)/shard_map/spectrum/pallas_call | solution.py:463
  19.7 3.2 %collective-permute-done.4.refs_0_ = bf16[128,128]{1,0:T(8,128)(2,1)S(1)} collective-permute-done((bf16[128,128]{1,0:T(8,128)(2,1)S(1)}, bf16[128,128]{1,0:T(8,128)(2,1)S(1)}, u32[]{:S(2)}, u32[]{:S(2)}) %collective-permute-start.4) | collective-permute-done | bytes 32800 | tf_op jit(solution)/shard_map/ppermute | solution.py:34
  23.0 0.0 collective-permute-done.5.refs_1_
  23.0 0.0 copy-done.2
  23.0 0.0 copy-done.3
  23.0 2.0 %surface.1 = f32[3,128,128]{2,1,0:T(8,128)} custom-call(bf16[256,256]{1,0:T(8,128)(2,1)S(1)} %copy-done.1, bf16[384,256]{1,0:T(8,128)(2,1)S(1)} %copy-done, bf16[768,256]{1,0:T(8,128)(2,1)S(1)} %copy-done.2, bf16[128,768]{1,0:T(8,128)(2,1)S(1)} %copy-done.3, f32[2,2,128,128]{3,2,1,0:T(8,128)S(1)} %spectrum.1.early, ...), custom_call_target="tpu_custom_call" | custom-call | tf_op jit(solution)/shard_map/surface/pallas_call | solution.py:472
Async XLA Ops:
  0.6 11.9 %copy-start.5 = (f32[1,4,8]{2,1,0:T(4,128)S(1)}, f32[1,4,8]{2,1,0:T(4,128)}, u32[]{:S(2)}) copy-start(f32[1,4,8]{2,1,0:T(4,128)} %weight.1) | copy-start | bytes 388
  0.6 18.6 %copy-start = (bf16[384,256]{1,0:T(8,128)(2,1)S(1)}, bf16[384,256]{1,0:T(8,128)(2,1)}, u32[]{:S(2)}) copy-start(bf16[384,256]{1,0:T(8,128)(2,1)} %constant.9.clone.right) | copy-start | bytes 589828
  0.7 18.6 %copy-start.1 = (bf16[256,256]{1,0:T(8,128)(2,1)S(1)}, bf16[256,256]{1,0:T(8,128)(2,1)}, u32[]{:S(2)}) copy-start(bf16[256,256]{1,0:T(8,128)(2,1)} %constant.8.clone.left) | copy-start | bytes 393220
  0.7 22.3 %copy-start.2 = (bf16[768,256]{1,0:T(8,128)(2,1)S(1)}, bf16[768,256]{1,0:T(8,128)(2,1)}, u32[]{:S(2)}) copy-start(bf16[768,256]{1,0:T(8,128)(2,1)} %constant.10.clone.turn) | copy-start | bytes 1179652
  0.7 22.3 %copy-start.3 = (bf16[128,768]{1,0:T(8,128)(2,1)S(1)}, bf16[128,768]{1,0:T(8,128)(2,1)}, u32[]{:S(2)}) copy-start(bf16[128,768]{1,0:T(8,128)(2,1)} %constant.11.clone.close) | copy-start | bytes 589828
  4.4 8.1 %collective-permute-start = (bf16[352,128]{1,0:T(8,128)(2,1)S(1)}, bf16[352,128]{1,0:T(8,128)(2,1)S(1)}, u32[]{:S(2)}, u32[]{:S(2)}) collective-permute-start(bf16[352,128]{1,0:T(8,128)(2,1)S(1)} %get-tuple-element.22), channel_id=1, source_target_pairs={{0,1},{1,0},{2,3},{3,2},{4,5},{5,4},{6,7},{7,6},{8,9},{9,8},{10,11... | collective-permute-start | bytes 270344 | tf_op jit(solution)/shard_map/ppermute | solution.py:34
  5.0 7.5 %collective-permute-start.2 = (bf16[352,128]{1,0:T(8,128)(2,1)S(1)}, bf16[352,128]{1,0:T(8,128)(2,1)S(1)}, u32[]{:S(2)}, u32[]{:S(2)}) collective-permute-start(bf16[352,128]{1,0:T(8,128)(2,1)S(1)} %get-tuple-element.24), channel_id=1, source_target_pairs={{0,3},{1,2},{2,1},{3,0},{4,7},{5,6},{6,5},{7,4},{8,11},{9,10},{10,... | collective-permute-start | bytes 270344 | tf_op jit(solution)/shard_map/ppermute | solution.py:34
  7.6 4.9 %collective-permute-start.1 = (bf16[320,128]{1,0:T(8,128)(2,1)S(1)}, bf16[320,128]{1,0:T(8,128)(2,1)S(1)}, u32[]{:S(2)}, u32[]{:S(2)}) collective-permute-start(bf16[320,128]{1,0:T(8,128)(2,1)S(1)} %get-tuple-element.23), channel_id=1, source_target_pairs={{0,2},{1,3},{2,0},{3,1},{4,6},{5,7},{6,4},{7,5},{8,10},{9,11},{10,... | collective-permute-start | bytes 245768 | tf_op jit(solution)/shard_map/ppermute | solution.py:34
  7.6 0.7 %copy-start.4 = (s32[1,4,8,3]{2,1,3,0:T(4,128)S(1)}, s32[1,4,8,3]{2,1,3,0:T(4,128)}, u32[]{:S(2)}) copy-start(s32[1,4,8,3]{2,1,3,0:T(4,128)} %param.11) | copy-start | bytes 1156
  8.3 0.7 %copy-start.6 = (s32[1,4]{1,0:T(1,128)S(1)}, s32[1,4]{1,0:T(1,128)}, u32[]{:S(2)}) copy-start(s32[1,4]{1,0:T(1,128)} %pcol.3) | copy-start | bytes 52
  14.2 5.0 %collective-permute-start.3 = (bf16[128,128]{1,0:T(8,128)(2,1)S(1)}, bf16[128,128]{1,0:T(8,128)(2,1)S(1)}, u32[]{:S(2)}, u32[]{:S(2)}) collective-permute-start(bf16[128,128]{1,0:T(8,128)(2,1)S(1)} %get-tuple-element.27), channel_id=1, source_target_pairs={{0,8},{4,12},{8,0},{12,4},{1,9},{5,13},{9,1},{13,5},{2,10},{6,14},... | collective-permute-start | bytes 98312 | tf_op jit(solution)/shard_map/ppermute | solution.py:34
  17.3 5.7 %collective-permute-start.4 = (bf16[128,128]{1,0:T(8,128)(2,1)S(1)}, bf16[128,128]{1,0:T(8,128)(2,1)S(1)}, u32[]{:S(2)}, u32[]{:S(2)}) collective-permute-start(bf16[128,128]{1,0:T(8,128)(2,1)S(1)} %get-tuple-element.28), channel_id=1, source_target_pairs={{0,12},{4,8},{8,4},{12,0},{1,13},{5,9},{9,5},{13,1},{2,14},{6,10},... | collective-permute-start | bytes 98312 | tf_op jit(solution)/shard_map/ppermute | solution.py:34
  18.4 4.6 %collective-permute-start.5 = (bf16[128,128]{1,0:T(8,128)(2,1)S(1)}, bf16[128,128]{1,0:T(8,128)(2,1)S(1)}, u32[]{:S(2)}, u32[]{:S(2)}) collective-permute-start(bf16[128,128]{1,0:T(8,128)(2,1)S(1)} %get-tuple-element.29), channel_id=1, source_target_pairs={{0,4},{4,0},{8,12},{12,8},{1,5},{5,1},{9,13},{13,9},{2,6},{6,2},{1... | collective-permute-start | bytes 98312 | tf_op jit(solution)/shard_map/ppermute | solution.py:34

commit v4 on v3

--- a/solution.py
+++ b/solution.py
@@ -14,6 +14,7 @@
 BLOCK = 128
 CAP = 2
 SUB = 8
+NOTE = 5
 PAD = 16
 BANDS = ("tile", "row")
 
@@ -179,7 +180,7 @@
     return here - half * (pltpu.roll(right, BLOCK - 1, 1) - pltpu.roll(left, 1, 1))
 
 
-def plan_kernel(owners, secs, drift, pcol, half_in, padded, acc, own):
+def plan_kernel(owners, secs, drift, weight, pcol, half_in, padded, acc, own, notes, shares):
     blocks = padded.shape[0] - 2
     slab = blocks * BLOCK // secs
     band = lax.axis_index(BANDS)
@@ -198,6 +199,23 @@
         )
         picked = jnp.where(lane >= o, near, far)
         acc[q] = pltpu.roll(picked, (BLOCK - o) & (BLOCK - 1), 1)
+        notes[owners * CAP * NOTE + 2 * q] = n
+        notes[owners * CAP * NOTE + 2 * q + 1] = o
+    for k in range(owners):
+        source = origin(band, k, owners)
+        place, found = find_slots(drift, source, band, drift.shape[2])
+        for c in range(CAP):
+            goal = drift[2, source, place[c]]
+            q = goal // (slab // BLOCK)
+            n, o = window_place(pcol, q, slab)
+            hit = (found > c) & ((goal == n) | (goal == n + 1))
+            at = (k * CAP + c) * NOTE
+            notes[at] = jnp.where(hit, 1, 0)
+            notes[at + 1] = q
+            notes[at + 2] = o
+            notes[at + 3] = jnp.where(goal == n, 1, 0)
+            notes[at + 4] = drift[0, source, place[c]]
+            shares[k * CAP + c] = weight[0, source, place[c]]
 
 
 def row_differences(x):
@@ -224,20 +242,16 @@
     return jnp.sum(jnp.sum(x, axis=1, keepdims=True), axis=0, keepdims=True)
 
 
-def blend_kernel(owners, secs, drift, weight, pcol, jitter_in, edges, begun, *refs):
+def blend_kernel(owners, secs, notes, shares, jitter_in, edges, begun, *refs):
     messages = refs[:owners]
     jitter_out = refs[owners]
     windows = refs[owners + 1 : owners + 1 + secs]
     firsts, lasts, tails, fixed, acc, den = refs[owners + 1 + secs :]
     blocks = edges.shape[1]
-    width = blocks * BLOCK
     seg = SEG // BLOCK
     band = lax.axis_index(BANDS)
     sec = lax.axis_index("sec")
-    slab = width // secs
-    slab_blocks = slab // BLOCK
     base = CAP * BLOCK
-    count = drift.shape[2]
     f32 = jnp.float32
     tiny = 1e-5 * 2 * (blocks // seg)
     firsts[band] = edges[0]
@@ -270,7 +284,8 @@
     lane1 = lax.broadcasted_iota(jnp.int32, (1, BLOCK), 1)
     acc[...] = begun[...]
     for q in range(secs):
-        n, o = window_place(pcol, q, slab)
+        n = notes[owners * CAP * NOTE + 2 * q]
+        o = notes[owners * CAP * NOTE + 2 * q + 1]
         n1 = jnp.minimum(n + 1, blocks - 1)
         picked = jnp.where(lane1 >= o, fixed[band, pl.ds(n, 1), :], fixed[band, pl.ds(n1, 1), :])
         picked = pltpu.roll(jnp.broadcast_to(picked, (SUB, BLOCK)), (BLOCK - o) & (BLOCK - 1), 1)
@@ -279,20 +294,18 @@
 
     for k in range(owners):
         source = origin(band, k, owners)
-        place, found = find_slots(drift, source, band, count)
         for c in range(CAP):
-            goal = drift[2, source, place[c]]
-            q = goal // slab_blocks
-            n, o = window_place(pcol, q, slab)
-
-            @pl.when((found > c) & ((goal == n) | (goal == n + 1)))
+            at = (k * CAP + c) * NOTE
+
+            @pl.when(notes[at] > 0)
             def _():
-                w = weight[0, source, place[c]]
+                q, o = notes[at + 1], notes[at + 2]
+                w = shares[k * CAP + c]
                 turn = (BLOCK - o) & (BLOCK - 1)
                 picture = messages[k][c * BLOCK : (c + 1) * BLOCK, :].astype(f32)
-                origin_block = drift[0, source, place[c]]
+                origin_block = notes[at + 4]
                 picture = jnp.where(top, fixed[source, pl.ds(origin_block, 1), :], picture)
-                inside = (lane1 + o < BLOCK) == (goal == n)
+                inside = (lane1 + o < BLOCK) == (notes[at + 3] > 0)
                 factor = jnp.where(inside, w, 0.0)
                 acc[q] = acc[q] + factor * pltpu.roll(picture, turn, 1)
                 den[q] = den[q] + factor
@@ -371,6 +384,10 @@
 
 def in_hbm(x):
     return pltpu.with_memory_space_constraint(x, pltpu.HBM)
+
+
+def in_smem(x):
+    return pltpu.with_memory_space_constraint(x, pltpu.SMEM)
 
 
 def halves(x):
@@ -436,26 +453,31 @@
         compiler_params=params,
         name="front",
     )(*map(in_hbm, (jitter_index, drifts, pixels)))
-    begun, own = pl.pallas_call(
+    begun, own, notes, shares = pl.pallas_call(
         functools.partial(plan_kernel, owners, secs),
-        out_shape=[shape((secs, PATCH, PATCH), f32), shape((CAP * BLOCK, BLOCK), bf16)],
-        in_specs=[smem, smem, vmem, vmem],
-        out_specs=[vmem] * 2,
+        out_shape=[
+            shape((secs, PATCH, PATCH), f32),
+            shape((CAP * BLOCK, BLOCK), bf16),
+            pltpu.SMEM((owners * CAP * NOTE + 2 * secs,), jnp.int32),
+            pltpu.SMEM((owners * CAP,), f32),
+        ],
+        in_specs=[smem, smem, smem, vmem, vmem],
+        out_specs=[vmem, vmem, smem, smem],
         compiler_params=params,
         cost_estimate=pl.CostEstimate(flops=10**8, bytes_accessed=10**6, transcendentals=0),
         name="plan",
-    )(drifts, patch_col, half, padded)
+    )(drifts, blend_weight, patch_col, half, padded)
     messages = [own] + [send(messages[k - 1], BANDS, k, owners) for k in range(1, owners)]
     jitter, *windows = pl.pallas_call(
         functools.partial(blend_kernel, owners, secs),
         out_shape=[shape((1, rows), f32)] + [shape((PATCH, PATCH), bf16)] * secs,
-        in_specs=[smem, smem, smem] + [vmem] * (3 + owners),
+        in_specs=[smem, smem] + [vmem] * (3 + owners),
         out_specs=[vmem] * (1 + secs),
         scratch_shapes=[pltpu.VMEM((owners, blocks, BLOCK), f32)] * 4
         + [pltpu.VMEM((secs, PATCH, PATCH), f32), pltpu.VMEM((secs, 1, PATCH), f32)],
         compiler_params=params,
         name="blend",
-    )(drifts, blend_weight, patch_col, jitter, edges, begun, *messages)
+    )(in_smem(notes), in_smem(shares), jitter, edges, begun, *messages)
     order = patch_order(secs)
     windows = windows[:1] + [send(windows[k], "sec", k, secs) for k in order[1:]]
     left, right, turn, close = dft_tables(PATCH)

time: 25.2 us -> 24.3 us (0.964)
  waiting for transfers between devices: 5.74 us -> 4.71 us
  local copies, waits for them, and re-layouts: 1.38 us -> 2.05 us
  Pallas kernels: 9.33 us -> 8.77 us
    ppermute x6, waiting for transfers between devices: 5.74 us -> 4.71 us  [send(): return lax.ppermute(x, axis, [(i, target(i, k, n)) for i in range(n)])]
    pallas_call x1, Pallas kernels: 1.68 us -> 1.01 us  [per_device(): pl.pallas_call(functools.partial(blend_kernel, owners, secs), out_shape=[...]
    unnamed x14, local copies, waits for them, and re-layouts: 1.38 us -> 2.05 us
  transfers between devices with their start and end apart: 6 -> 6, of which waited for: 3 -> 3; matrix products, arithmetic and copies ran while one was open for 0% -> 0% of each run, Pallas kernels for 7% -> 8%
where the time goes in v4:
time: 24.3 us; the launch traced here: 24 us
  Pallas kernels  8.77 us (36%)
  starting transfers between devices  7.72 us (32%)
  waiting for transfers between devices  4.71 us (19%)
  local copies, waits for them, and re-layouts  2.05 us (8%)
  between operations  0.7 us (3%)
    ppermute x6, starting transfers between devices, send(): return lax.ppermute(x, axis, [(i, target(i, k, n)) for i in range(n)])  7.72 us
    ppermute x6, waiting for transfers between devices, send(): return lax.ppermute(x, axis, [(i, target(i, k, n)) for i in range(n)])  4.71 us
    pallas_call x1, Pallas kernels, per_device(): pl.pallas_call(functools.partial(front_kernel, owners, chunks), out_shape...  3.75 us
    unnamed x14, local copies, waits for them, and re-layouts  2.05 us
    pallas_call x1, Pallas kernels, per_device(): pl.pallas_call(functools.partial(surface_kernel, secs), out_shape=shape((...  2.04 us
    pallas_call x1, Pallas kernels, per_device(): pl.pallas_call(functools.partial(plan_kernel, owners, secs), out_shape=[s...  1.49 us
    pallas_call x1, Pallas kernels, per_device(): pl.pallas_call(functools.partial(blend_kernel, owners, secs), out_shape=[...  1.01 us
  transfers between devices with their start and end apart: 6, of which 3 were waited for; matrix products, arithmetic and copies ran while one was open for 0% of the time, Pallas kernels for 8%

profile of v4, /device:TPU:0, one launch (start us, length us, event | category | flops | bytes accessed | tf_op | source)
XLA Modules:
  0.0 24.0 jit_solution(16580873427995153198)
XLA Ops:
  0.6 0.0 copy-start
  0.6 0.0 copy-start.1
  0.7 0.0 copy-start.2
  0.7 0.0 copy-start.3
  0.7 3.7 %front.1 = (f32[1,128]{1,0:T(1,128)S(1)}, f32[128,128]{1,0:T(8,128)S(1)}, f32[34,144,128]{2,1,0:T(8,128)S(1)}, f32[2,32,128]{2,1,0:T(8,128)S(1)}, bf16[352,128]{...) custom-call(s32[1,128]{1,0:T(1,128)} %delay_at.1, s32[3,4,8]{2,1,0:T(4,128)} %bitcast.7, ...), custom_call_target="tpu_custom_call" | custom-call | tf_op jit(solution)/shard_map/front/pallas_call | solution.py:433
  4.4 0.5 %collective-permute-start = (bf16[352,128]{1,0:T(8,128)(2,1)S(1)}, bf16[352,128]{1,0:T(8,128)(2,1)S(1)}, u32[]{:S(2)}, u32[]{:S(2)}) collective-permute-start(bf16[352,128]{1,0:T(8,128)(2,1)S(1)} %get-tuple-element.26), channel_id=1, source_target_pairs={{0,1},{1,0},{2,3},{3,2},{4,5},{5,4},{6,7},{7,6},{8,9},{9,8},{10,11... | collective-permute-start | bytes 270344 | tf_op jit(solution)/shard_map/ppermute | solution.py:35
  5.0 2.6 %collective-permute-start.2 = (bf16[352,128]{1,0:T(8,128)(2,1)S(1)}, bf16[352,128]{1,0:T(8,128)(2,1)S(1)}, u32[]{:S(2)}, u32[]{:S(2)}) collective-permute-start(bf16[352,128]{1,0:T(8,128)(2,1)S(1)} %get-tuple-element.28), channel_id=1, source_target_pairs={{0,3},{1,2},{2,1},{3,0},{4,7},{5,6},{6,5},{7,4},{8,11},{9,10},{10,... | collective-permute-start | bytes 270344 | tf_op jit(solution)/shard_map/ppermute | solution.py:35
  7.6 0.0 collective-permute-start.1
  7.6 0.0 copy-start.4
  7.6 0.7 %copy-done.4 = s32[1,4,8,3]{2,1,3,0:T(4,128)S(1)} copy-done((s32[1,4,8,3]{2,1,3,0:T(4,128)S(1)}, s32[1,4,8,3]{2,1,3,0:T(4,128)}, u32[]{:S(2)}) %copy-start.4) | copy-done | bytes 408
  8.3 0.0 copy-start.5
  8.3 0.7 %copy-done.5 = f32[1,4,8]{2,1,0:T(4,128)S(1)} copy-done((f32[1,4,8]{2,1,0:T(4,128)S(1)}, f32[1,4,8]{2,1,0:T(4,128)}, u32[]{:S(2)}) %copy-start.5) | copy-done | bytes 152
  9.0 0.0 copy-start.6
  9.0 0.7 %copy-done.6 = s32[1,4]{1,0:T(1,128)S(1)} copy-done((s32[1,4]{1,0:T(1,128)S(1)}, s32[1,4]{1,0:T(1,128)}, u32[]{:S(2)}) %copy-start.6) | copy-done | bytes 40
  9.6 1.5 %plan.1 = (f32[4,128,128]{2,1,0:T(8,128)S(1)}, bf16[256,128]{1,0:T(8,128)(2,1)S(1)}, s32[48]{0:T(128)S(4)}, f32[8]{0:T(128)S(4)}) custom-call(s32[3,4,8]{2,1,0:T(4,128)S(1)} %bitcast.8, f32[1,4,8]{2,1,0:T(4,128)S(1)} %copy-done.5, s32[1,4]{1,0:T(1,128)S(1)} %copy-done.6, f32[128,128]{1,0:T(8,128)S(1)} %get-tuple-element.18.half_in, ...), custom_call_target="tpu_custom_call" | custom-call | flops 100000000 | bytes 1000000 | tf_op jit(solution)/shard_map/plan/pallas_call | solution.py:456
  11.1 1.3 %collective-permute-done.1.refs_2_ = bf16[320,128]{1,0:T(8,128)(2,1)S(1)} collective-permute-done((bf16[320,128]{1,0:T(8,128)(2,1)S(1)}, bf16[320,128]{1,0:T(8,128)(2,1)S(1)}, u32[]{:S(2)}, u32[]{:S(2)}) %collective-permute-start.1) | collective-permute-done | bytes 81952 | tf_op jit(solution)/shard_map/ppermute | solution.py:35
  12.5 0.0 collective-permute-done.refs_1_
  12.5 0.0 collective-permute-done.2.refs_3_
  12.5 1.0 %blend.1 = (f32[1,128]{1,0:T(1,128)}, bf16[128,128]{1,0:T(8,128)(2,1)S(1)}, bf16[128,128]{1,0:T(8,128)(2,1)S(1)}, bf16[128,128]{1,0:T(8,128)(2,1)S(1)}, bf16[128,128]{1,0:T(8,128)(2,1)S(1)}) custom-call(s32[48]{0:T(128)S(4)} %get-tuple-element.20.notes, f32[8]{0:T(128)S(4)} %get-tuple-element.21.shares, f32[1,128]{1,0:T(1,128)S(1)} %get-tuple-element.22.jitter_in, ...), custom_call_target="tpu_custom_call" | custom-call | tf_op jit(solution)/shard_map/blend/pallas_call | solution.py:471
  13.5 2.7 %collective-permute-start.3 = (bf16[128,128]{1,0:T(8,128)(2,1)S(1)}, bf16[128,128]{1,0:T(8,128)(2,1)S(1)}, u32[]{:S(2)}, u32[]{:S(2)}) collective-permute-start(bf16[128,128]{1,0:T(8,128)(2,1)S(1)} %get-tuple-element.31), channel_id=1, source_target_pairs={{0,8},{4,12},{8,0},{12,4},{1,9},{5,13},{9,1},{13,5},{2,10},{6,14},... | collective-permute-start | bytes 98312 | tf_op jit(solution)/shard_map/ppermute | solution.py:35
  16.2 1.4 %collective-permute-start.4 = (bf16[128,128]{1,0:T(8,128)(2,1)S(1)}, bf16[128,128]{1,0:T(8,128)(2,1)S(1)}, u32[]{:S(2)}, u32[]{:S(2)}) collective-permute-start(bf16[128,128]{1,0:T(8,128)(2,1)S(1)} %get-tuple-element.32), channel_id=1, source_target_pairs={{0,12},{4,8},{8,4},{12,0},{1,13},{5,9},{9,5},{13,1},{2,14},{6,10},... | collective-permute-start | bytes 98312 | tf_op jit(solution)/shard_map/ppermute | solution.py:35
  17.6 0.5 %collective-permute-start.5 = (bf16[128,128]{1,0:T(8,128)(2,1)S(1)}, bf16[128,128]{1,0:T(8,128)(2,1)S(1)}, u32[]{:S(2)}, u32[]{:S(2)}) collective-permute-start(bf16[128,128]{1,0:T(8,128)(2,1)S(1)} %get-tuple-element.33), channel_id=1, source_target_pairs={{0,4},{4,0},{8,12},{12,8},{1,5},{5,1},{9,13},{13,9},{2,6},{6,2},{1... | collective-permute-start | bytes 98312 | tf_op jit(solution)/shard_map/ppermute | solution.py:35
  18.0 0.4 %collective-permute-done.3.refs_1_ = bf16[128,128]{1,0:T(8,128)(2,1)S(1)} collective-permute-done((bf16[128,128]{1,0:T(8,128)(2,1)S(1)}, bf16[128,128]{1,0:T(8,128)(2,1)S(1)}, u32[]{:S(2)}, u32[]{:S(2)}) %collective-permute-start.3) | collective-permute-done | bytes 32800 | tf_op jit(solution)/shard_map/ppermute | solution.py:35
  18.5 0.0 copy-done
  18.5 0.0 copy-done.1
  18.5 0.5 %spectrum.1.early = f32[2,2,128,128]{3,2,1,0:T(8,128)S(1)} custom-call(bf16[256,256]{1,0:T(8,128)(2,1)S(1)} %copy-done.1, bf16[384,256]{1,0:T(8,128)(2,1)S(1)} %copy-done, bf16[128,128]{1,0:T(8,128)(2,1)S(1)} %get-tuple-element.30.refs_0_, bf16[128,128]{1,0:T(8,128)(2,1)S(1)} %collective-permute-done.3.refs_1_), custom_call_target="tpu_custom_call" | custom-call | flops 100000000 | bytes 1000000 | tf_op jit(solution)/shard_map/spectrum/pallas_call | solution.py:485
  19.0 2.9 %collective-permute-done.4.refs_0_ = bf16[128,128]{1,0:T(8,128)(2,1)S(1)} collective-permute-done((bf16[128,128]{1,0:T(8,128)(2,1)S(1)}, bf16[128,128]{1,0:T(8,128)(2,1)S(1)}, u32[]{:S(2)}, u32[]{:S(2)}) %collective-permute-start.4) | collective-permute-done | bytes 32800 | tf_op jit(solution)/shard_map/ppermute | solution.py:35
  21.9 0.0 collective-permute-done.5.refs_1_
  21.9 0.0 copy-done.2
  21.9 0.0 copy-done.3
  21.9 2.0 %surface.1 = f32[3,128,128]{2,1,0:T(8,128)} custom-call(bf16[256,256]{1,0:T(8,128)(2,1)S(1)} %copy-done.1, bf16[384,256]{1,0:T(8,128)(2,1)S(1)} %copy-done, bf16[768,256]{1,0:T(8,128)(2,1)S(1)} %copy-done.2, bf16[128,768]{1,0:T(8,128)(2,1)S(1)} %copy-done.3, f32[2,2,128,128]{3,2,1,0:T(8,128)S(1)} %spectrum.1.early, ...), custom_call_target="tpu_custom_call" | custom-call | tf_op jit(solution)/shard_map/surface/pallas_call | solution.py:494
Async XLA Ops:
  0.6 17.8 %copy-start = (bf16[384,256]{1,0:T(8,128)(2,1)S(1)}, bf16[384,256]{1,0:T(8,128)(2,1)}, u32[]{:S(2)}) copy-start(bf16[384,256]{1,0:T(8,128)(2,1)} %constant.9.clone.right) | copy-start | bytes 589828
  0.6 17.8 %copy-start.1 = (bf16[256,256]{1,0:T(8,128)(2,1)S(1)}, bf16[256,256]{1,0:T(8,128)(2,1)}, u32[]{:S(2)}) copy-start(bf16[256,256]{1,0:T(8,128)(2,1)} %constant.8.clone.left) | copy-start | bytes 393220
  0.7 21.3 %copy-start.2 = (bf16[768,256]{1,0:T(8,128)(2,1)S(1)}, bf16[768,256]{1,0:T(8,128)(2,1)}, u32[]{:S(2)}) copy-start(bf16[768,256]{1,0:T(8,128)(2,1)} %constant.10.clone.turn) | copy-start | bytes 1179652
  0.7 21.2 %copy-start.3 = (bf16[128,768]{1,0:T(8,128)(2,1)S(1)}, bf16[128,768]{1,0:T(8,128)(2,1)}, u32[]{:S(2)}) copy-start(bf16[128,768]{1,0:T(8,128)(2,1)} %constant.11.clone.close) | copy-start | bytes 589828
  4.4 8.1 %collective-permute-start = (bf16[352,128]{1,0:T(8,128)(2,1)S(1)}, bf16[352,128]{1,0:T(8,128)(2,1)S(1)}, u32[]{:S(2)}, u32[]{:S(2)}) collective-permute-start(bf16[352,128]{1,0:T(8,128)(2,1)S(1)} %get-tuple-element.26), channel_id=1, source_target_pairs={{0,1},{1,0},{2,3},{3,2},{4,5},{5,4},{6,7},{7,6},{8,9},{9,8},{10,11... | collective-permute-start | bytes 270344 | tf_op jit(solution)/shard_map/ppermute | solution.py:35
  5.0 7.5 %collective-permute-start.2 = (bf16[352,128]{1,0:T(8,128)(2,1)S(1)}, bf16[352,128]{1,0:T(8,128)(2,1)S(1)}, u32[]{:S(2)}, u32[]{:S(2)}) collective-permute-start(bf16[352,128]{1,0:T(8,128)(2,1)S(1)} %get-tuple-element.28), channel_id=1, source_target_pairs={{0,3},{1,2},{2,1},{3,0},{4,7},{5,6},{6,5},{7,4},{8,11},{9,10},{10,... | collective-permute-start | bytes 270344 | tf_op jit(solution)/shard_map/ppermute | solution.py:35
  7.6 4.9 %collective-permute-start.1 = (bf16[320,128]{1,0:T(8,128)(2,1)S(1)}, bf16[320,128]{1,0:T(8,128)(2,1)S(1)}, u32[]{:S(2)}, u32[]{:S(2)}) collective-permute-start(bf16[320,128]{1,0:T(8,128)(2,1)S(1)} %get-tuple-element.27), channel_id=1, source_target_pairs={{0,2},{1,3},{2,0},{3,1},{4,6},{5,7},{6,4},{7,5},{8,10},{9,11},{10,... | collective-permute-start | bytes 245768 | tf_op jit(solution)/shard_map/ppermute | solution.py:35
  7.6 0.7 %copy-start.4 = (s32[1,4,8,3]{2,1,3,0:T(4,128)S(1)}, s32[1,4,8,3]{2,1,3,0:T(4,128)}, u32[]{:S(2)}) copy-start(s32[1,4,8,3]{2,1,3,0:T(4,128)} %param.11) | copy-start | bytes 1156
  8.3 0.7 %copy-start.5 = (f32[1,4,8]{2,1,0:T(4,128)S(1)}, f32[1,4,8]{2,1,0:T(4,128)}, u32[]{:S(2)}) copy-start(f32[1,4,8]{2,1,0:T(4,128)} %weight.1) | copy-start | bytes 388
  9.0 0.7 %copy-start.6 = (s32[1,4]{1,0:T(1,128)S(1)}, s32[1,4]{1,0:T(1,128)}, u32[]{:S(2)}) copy-start(s32[1,4]{1,0:T(1,128)} %pcol.1) | copy-start | bytes 52
  13.5 5.0 %collective-permute-start.3 = (bf16[128,128]{1,0:T(8,128)(2,1)S(1)}, bf16[128,128]{1,0:T(8,128)(2,1)S(1)}, u32[]{:S(2)}, u32[]{:S(2)}) collective-permute-start(bf16[128,128]{1,0:T(8,128)(2,1)S(1)} %get-tuple-element.31), channel_id=1, source_target_pairs={{0,8},{4,12},{8,0},{12,4},{1,9},{5,13},{9,1},{13,5},{2,10},{6,14},... | collective-permute-start | bytes 98312 | tf_op jit(solution)/shard_map/ppermute | solution.py:35
  16.2 5.7 %collective-permute-start.4 = (bf16[128,128]{1,0:T(8,128)(2,1)S(1)}, bf16[128,128]{1,0:T(8,128)(2,1)S(1)}, u32[]{:S(2)}, u32[]{:S(2)}) collective-permute-start(bf16[128,128]{1,0:T(8,128)(2,1)S(1)} %get-tuple-element.32), channel_id=1, source_target_pairs={{0,12},{4,8},{8,4},{12,0},{1,13},{5,9},{9,5},{13,1},{2,14},{6,10},... | collective-permute-start | bytes 98312 | tf_op jit(solution)/shard_map/ppermute | solution.py:35
  17.6 4.3 %collective-permute-start.5 = (bf16[128,128]{1,0:T(8,128)(2,1)S(1)}, bf16[128,128]{1,0:T(8,128)(2,1)S(1)}, u32[]{:S(2)}, u32[]{:S(2)}) collective-permute-start(bf16[128,128]{1,0:T(8,128)(2,1)S(1)} %get-tuple-element.33), channel_id=1, source_target_pairs={{0,4},{4,0},{8,12},{12,8},{1,5},{5,1},{9,13},{13,9},{2,6},{6,2},{1... | collective-permute-start | bytes 98312 | tf_op jit(solution)/shard_map/ppermute | solution.py:35

commit v5 on v4

--- a/solution.py
+++ b/solution.py
@@ -15,6 +15,7 @@
 CAP = 2
 SUB = 8
 NOTE = 5
+CHUNKS = (0, 2, 6, 11, 16)
 PAD = 16
 BANDS = ("tile", "row")
 
@@ -65,17 +66,18 @@
     return high, (x - high.astype(jnp.float32)).astype(jnp.bfloat16)
 
 
-def front_kernel(owners, chunks, delay_at, drift_at, pixels, *refs):
+def front_kernel(owners, delay_at, drift_at, pixels, *refs):
     jitter_out, half_out, padded, first_out = refs[:4]
     messages = refs[4 : 3 + owners]
     raw, ring, wide, sums, delay, drift, loaded = refs[3 + owners :]
     rows, width = pixels.shape
     blocks = width // BLOCK
-    per = rows // chunks
+    bounds = [rows * part // 16 for part in CHUNKS]
+    chunks = len(CHUNKS) - 1
     band = lax.axis_index(BANDS)
 
     def load(i):
-        at = pl.ds(i * per, per)
+        at = pl.ds(bounds[i], bounds[i + 1] - bounds[i])
         return pltpu.make_async_copy(pixels.at[at, :], raw.at[at, :], loaded.at[i])
 
     small = [
@@ -94,17 +96,20 @@
     wide[...] = jnp.broadcast_to(delay[...], (rows, rows)).T
     lane = lax.broadcasted_iota(jnp.int32, (SUB, BLOCK), 1)
     last_lane = lane == BLOCK - 1
+    first_sub = lax.broadcasted_iota(jnp.int32, (SUB, BLOCK), 0) == 0
     seg = SEG // BLOCK
 
     def relate(at):
-        cross = power = jnp.zeros((SUB, BLOCK), jnp.float32)
         here, over = pl.ds(at + PAD, SUB), pl.ds(at + (PAD - 1), SUB)
+        cross = [jnp.zeros((SUB, BLOCK), jnp.float32)] * seg
         for v in range(blocks):
+            i = v % seg
             x, behind = padded[v + 1, here, :], ring[v, here, :]
-            cross = cross + (padded[v + 1, over, :] * behind - ring[v, over, :] * x)
-            power = power + x * x
-        sums[0, pl.ds(at + SUB, SUB), :] = cross
-        sums[1, pl.ds(at + SUB, SUB), :] = power
+            top = pl.ds(at + (PAD - 1), 1)
+            above = jnp.where(first_sub, padded[v + 1, top, :], pltpu.roll(x, 1, 0))
+            above_behind = jnp.where(first_sub, ring[v, top, :], pltpu.roll(behind, 1, 0))
+            cross[i] = cross[i] + (above * behind - above_behind * x)
+        sums[0, pl.ds(at + SUB, SUB), :] = sum(cross[1:], cross[0])
 
     def eight_rows(g, _):
         at = pl.multiple_of(g * SUB, SUB)
@@ -123,21 +128,24 @@
         ]
         picked.append(jnp.zeros((SUB, BLOCK), jnp.float32))
         x = [jnp.where(near, picked[v], picked[v + 1]) for v in range(blocks)]
+        power = [jnp.zeros((SUB, BLOCK), jnp.float32)] * seg
         for v in range(blocks):
             prv = x[v - 1] if v % seg else x[v + seg - 1]
             padded[v + 1, pl.ds(at + PAD, SUB), :] = x[v]
             ring[v, pl.ds(at + PAD, SUB), :] = pltpu.roll(jnp.where(last_lane, prv, x[v]), 1, 1)
+            power[v % seg] = power[v % seg] + x[v] * x[v]
+        sums[1, pl.ds(at + SUB, SUB), :] = sum(power[1:], power[0])
         return 0
 
     def again(g, _):
         relate(pl.multiple_of(g * SUB, SUB))
         return 0
 
-    steps = per // SUB
     for i in range(chunks):
         load(i).wait()
-        lax.fori_loop(i * steps, (i + 1) * steps, eight_rows, 0, unroll=4)
-        lax.fori_loop(i * steps, (i + 1) * steps, again, 0, unroll=4)
+        groups = bounds[i] // SUB, bounds[i + 1] // SUB
+        lax.fori_loop(*groups, eight_rows, 0, unroll=True)
+        lax.fori_loop(*groups, again, 0, unroll=True)
 
     small[1].wait()
     total_cross = jnp.sum(sums[0, SUB:], axis=1, keepdims=True)
@@ -226,6 +234,7 @@
     ahead = pltpu.roll(x, BLOCK - 1, 1)
     behind = pltpu.roll(x, 1, 1)
     last_lane = lane == BLOCK - 1
+    first_sub = lax.broadcasted_iota(jnp.int32, (SUB, BLOCK), 0) == 0
     first_lane = lane == 0
     nxt = pltpu.roll(ahead, blocks - 1, 0)
     prv = pltpu.roll(behind, 1, 0)
@@ -419,7 +428,7 @@
     blocks = width // BLOCK
     owners = lax.axis_size(BANDS)
     secs = lax.axis_size("sec")
-    chunks = 4
+    chunks = len(CHUNKS) - 1
     drifts = jnp.transpose(drift_list[0], (2, 0, 1))
     f32, bf16 = jnp.float32, jnp.bfloat16
     vmem = pl.BlockSpec(memory_space=pltpu.VMEM)
@@ -431,7 +440,7 @@
     ]
     params = pltpu.CompilerParams(vmem_limit_bytes=24 * 1024 * 1024)
     jitter, half, padded, edges, *messages = pl.pallas_call(
-        functools.partial(front_kernel, owners, chunks),
+        functools.partial(front_kernel, owners),
         out_shape=[
             shape((1, rows), f32),
             shape((rows, BLOCK), f32),

time: 24.3 us -> 23.9 us (0.984)
  Pallas kernels: 8.77 us -> 8.47 us
    pallas_call x1, Pallas kernels: 3.75 us -> 3.45 us  [per_device(): pl.pallas_call(functools.partial(front_kernel, owners), out_shape=[shape(...]
where the time goes in v5:
time: 23.9 us; the launch traced here: 23.7 us
  Pallas kernels  8.47 us (35%)
  starting transfers between devices  7.56 us (32%)
  waiting for transfers between devices  4.88 us (20%)
  local copies, waits for them, and re-layouts  2.05 us (9%)
  between operations  0.7 us (3%)
    ppermute x6, starting transfers between devices, send(): return lax.ppermute(x, axis, [(i, target(i, k, n)) for i in range(n)])  7.56 us
    ppermute x6, waiting for transfers between devices, send(): return lax.ppermute(x, axis, [(i, target(i, k, n)) for i in range(n)])  4.88 us
    pallas_call x1, Pallas kernels, per_device(): pl.pallas_call(functools.partial(front_kernel, owners), out_shape=[shape(...  3.45 us
    unnamed x14, local copies, waits for them, and re-layouts  2.05 us
    pallas_call x1, Pallas kernels, per_device(): pl.pallas_call(functools.partial(surface_kernel, secs), out_shape=shape((...  2.04 us
    pallas_call x1, Pallas kernels, per_device(): pl.pallas_call(functools.partial(plan_kernel, owners, secs), out_shape=[s...  1.49 us
    pallas_call x1, Pallas kernels, per_device(): pl.pallas_call(functools.partial(blend_kernel, owners, secs), out_shape=[...  1.01 us
    pallas_call x1, Pallas kernels, per_device(): pl.pallas_call(spectrum_kernel, out_shape=shape((begin, 2, PATCH, PATCH),...  0.48 us
  transfers between devices with their start and end apart: 6, of which 3 were waited for; matrix products, arithmetic and copies ran while one was open for 0% of the time, Pallas kernels for 8%

profile of v5, /device:TPU:0, one launch (start us, length us, event | category | flops | bytes accessed | tf_op | source)
XLA Modules:
  0.0 23.7 jit_solution(17691240556206012578)
XLA Ops:
  0.6 0.0 copy-start
  0.6 0.0 copy-start.1
  0.7 0.0 copy-start.2
  0.7 0.0 copy-start.3
  0.7 3.5 %front.1 = (f32[1,128]{1,0:T(1,128)S(1)}, f32[128,128]{1,0:T(8,128)S(1)}, f32[34,144,128]{2,1,0:T(8,128)S(1)}, f32[2,32,128]{2,1,0:T(8,128)S(1)}, bf16[352,128]{...) custom-call(s32[1,128]{1,0:T(1,128)} %delay_at.1, s32[3,4,8]{2,1,0:T(4,128)} %bitcast.7, ...), custom_call_target="tpu_custom_call" | custom-call | tf_op jit(solution)/shard_map/front/pallas_call | solution.py:442
  4.1 0.5 %collective-permute-start = (bf16[352,128]{1,0:T(8,128)(2,1)S(1)}, bf16[352,128]{1,0:T(8,128)(2,1)S(1)}, u32[]{:S(2)}, u32[]{:S(2)}) collective-permute-start(bf16[352,128]{1,0:T(8,128)(2,1)S(1)} %get-tuple-element.26), channel_id=1, source_target_pairs={{0,1},{1,0},{2,3},{3,2},{4,5},{5,4},{6,7},{7,6},{8,9},{9,8},{10,11... | collective-permute-start | bytes 270344 | tf_op jit(solution)/shard_map/ppermute | solution.py:36
  4.7 2.6 %collective-permute-start.2 = (bf16[352,128]{1,0:T(8,128)(2,1)S(1)}, bf16[352,128]{1,0:T(8,128)(2,1)S(1)}, u32[]{:S(2)}, u32[]{:S(2)}) collective-permute-start(bf16[352,128]{1,0:T(8,128)(2,1)S(1)} %get-tuple-element.28), channel_id=1, source_target_pairs={{0,3},{1,2},{2,1},{3,0},{4,7},{5,6},{6,5},{7,4},{8,11},{9,10},{10,... | collective-permute-start | bytes 270344 | tf_op jit(solution)/shard_map/ppermute | solution.py:36
  7.3 0.0 collective-permute-start.1
  7.3 0.0 copy-start.4
  7.3 0.7 %copy-done.4 = s32[1,4,8,3]{2,1,3,0:T(4,128)S(1)} copy-done((s32[1,4,8,3]{2,1,3,0:T(4,128)S(1)}, s32[1,4,8,3]{2,1,3,0:T(4,128)}, u32[]{:S(2)}) %copy-start.4) | copy-done | bytes 408
  8.0 0.0 copy-start.5
  8.0 0.7 %copy-done.5 = f32[1,4,8]{2,1,0:T(4,128)S(1)} copy-done((f32[1,4,8]{2,1,0:T(4,128)S(1)}, f32[1,4,8]{2,1,0:T(4,128)}, u32[]{:S(2)}) %copy-start.5) | copy-done | bytes 152
  8.7 0.0 copy-start.6
  8.7 0.7 %copy-done.6 = s32[1,4]{1,0:T(1,128)S(1)} copy-done((s32[1,4]{1,0:T(1,128)S(1)}, s32[1,4]{1,0:T(1,128)}, u32[]{:S(2)}) %copy-start.6) | copy-done | bytes 40
  9.3 1.5 %plan.1 = (f32[4,128,128]{2,1,0:T(8,128)S(1)}, bf16[256,128]{1,0:T(8,128)(2,1)S(1)}, s32[48]{0:T(128)S(4)}, f32[8]{0:T(128)S(4)}) custom-call(s32[3,4,8]{2,1,0:T(4,128)S(1)} %bitcast.8, f32[1,4,8]{2,1,0:T(4,128)S(1)} %copy-done.5, s32[1,4]{1,0:T(1,128)S(1)} %copy-done.6, f32[128,128]{1,0:T(8,128)S(1)} %get-tuple-element.18.half_in, ...), custom_call_target="tpu_custom_call" | custom-call | flops 100000000 | bytes 1000000 | tf_op jit(solution)/shard_map/plan/pallas_call | solution.py:465
  10.8 1.3 %collective-permute-done.1.refs_2_ = bf16[320,128]{1,0:T(8,128)(2,1)S(1)} collective-permute-done((bf16[320,128]{1,0:T(8,128)(2,1)S(1)}, bf16[320,128]{1,0:T(8,128)(2,1)S(1)}, u32[]{:S(2)}, u32[]{:S(2)}) %collective-permute-start.1) | collective-permute-done | bytes 81952 | tf_op jit(solution)/shard_map/ppermute | solution.py:36
  12.2 0.0 collective-permute-done.refs_1_
  12.2 0.0 collective-permute-done.2.refs_3_
  12.2 1.0 %blend.1 = (f32[1,128]{1,0:T(1,128)}, bf16[128,128]{1,0:T(8,128)(2,1)S(1)}, bf16[128,128]{1,0:T(8,128)(2,1)S(1)}, bf16[128,128]{1,0:T(8,128)(2,1)S(1)}, bf16[128,128]{1,0:T(8,128)(2,1)S(1)}) custom-call(s32[48]{0:T(128)S(4)} %get-tuple-element.20.notes, f32[8]{0:T(128)S(4)} %get-tuple-element.21.shares, f32[1,128]{1,0:T(1,128)S(1)} %get-tuple-element.22.jitter_in, ...), custom_call_target="tpu_custom_call" | custom-call | tf_op jit(solution)/shard_map/blend/pallas_call | solution.py:480
  13.2 2.7 %collective-permute-start.3 = (bf16[128,128]{1,0:T(8,128)(2,1)S(1)}, bf16[128,128]{1,0:T(8,128)(2,1)S(1)}, u32[]{:S(2)}, u32[]{:S(2)}) collective-permute-start(bf16[128,128]{1,0:T(8,128)(2,1)S(1)} %get-tuple-element.31), channel_id=1, source_target_pairs={{0,8},{4,12},{8,0},{12,4},{1,9},{5,13},{9,1},{13,5},{2,10},{6,14},... | collective-permute-start | bytes 98312 | tf_op jit(solution)/shard_map/ppermute | solution.py:36
  15.9 1.4 %collective-permute-start.4 = (bf16[128,128]{1,0:T(8,128)(2,1)S(1)}, bf16[128,128]{1,0:T(8,128)(2,1)S(1)}, u32[]{:S(2)}, u32[]{:S(2)}) collective-permute-start(bf16[128,128]{1,0:T(8,128)(2,1)S(1)} %get-tuple-element.32), channel_id=1, source_target_pairs={{0,12},{4,8},{8,4},{12,0},{1,13},{5,9},{9,5},{13,1},{2,14},{6,10},... | collective-permute-start | bytes 98312 | tf_op jit(solution)/shard_map/ppermute | solution.py:36
  17.3 0.3 %collective-permute-start.5 = (bf16[128,128]{1,0:T(8,128)(2,1)S(1)}, bf16[128,128]{1,0:T(8,128)(2,1)S(1)}, u32[]{:S(2)}, u32[]{:S(2)}) collective-permute-start(bf16[128,128]{1,0:T(8,128)(2,1)S(1)} %get-tuple-element.33), channel_id=1, source_target_pairs={{0,4},{4,0},{8,12},{12,8},{1,5},{5,1},{9,13},{13,9},{2,6},{6,2},{1... | collective-permute-start | bytes 98312 | tf_op jit(solution)/shard_map/ppermute | solution.py:36
  17.6 0.6 %collective-permute-done.3.refs_1_ = bf16[128,128]{1,0:T(8,128)(2,1)S(1)} collective-permute-done((bf16[128,128]{1,0:T(8,128)(2,1)S(1)}, bf16[128,128]{1,0:T(8,128)(2,1)S(1)}, u32[]{:S(2)}, u32[]{:S(2)}) %collective-permute-start.3) | collective-permute-done | bytes 32800 | tf_op jit(solution)/shard_map/ppermute | solution.py:36
  18.2 0.0 copy-done
  18.2 0.0 copy-done.1
  18.2 0.5 %spectrum.1.early = f32[2,2,128,128]{3,2,1,0:T(8,128)S(1)} custom-call(bf16[256,256]{1,0:T(8,128)(2,1)S(1)} %copy-done.1, bf16[384,256]{1,0:T(8,128)(2,1)S(1)} %copy-done, bf16[128,128]{1,0:T(8,128)(2,1)S(1)} %get-tuple-element.30.refs_0_, bf16[128,128]{1,0:T(8,128)(2,1)S(1)} %collective-permute-done.3.refs_1_), custom_call_target="tpu_custom_call" | custom-call | flops 100000000 | bytes 1000000 | tf_op jit(solution)/shard_map/spectrum/pallas_call | solution.py:494
  18.7 2.9 %collective-permute-done.4.refs_0_ = bf16[128,128]{1,0:T(8,128)(2,1)S(1)} collective-permute-done((bf16[128,128]{1,0:T(8,128)(2,1)S(1)}, bf16[128,128]{1,0:T(8,128)(2,1)S(1)}, u32[]{:S(2)}, u32[]{:S(2)}) %collective-permute-start.4) | collective-permute-done | bytes 32800 | tf_op jit(solution)/shard_map/ppermute | solution.py:36
  21.6 0.0 collective-permute-done.5.refs_1_
  21.6 0.0 copy-done.2
  21.6 0.0 copy-done.3
  21.6 2.0 %surface.1 = f32[3,128,128]{2,1,0:T(8,128)} custom-call(bf16[256,256]{1,0:T(8,128)(2,1)S(1)} %copy-done.1, bf16[384,256]{1,0:T(8,128)(2,1)S(1)} %copy-done, bf16[768,256]{1,0:T(8,128)(2,1)S(1)} %copy-done.2, bf16[128,768]{1,0:T(8,128)(2,1)S(1)} %copy-done.3, f32[2,2,128,128]{3,2,1,0:T(8,128)S(1)} %spectrum.1.early, ...), custom_call_target="tpu_custom_call" | custom-call | tf_op jit(solution)/shard_map/surface/pallas_call | solution.py:503
Async XLA Ops:
  0.6 17.5 %copy-start = (bf16[384,256]{1,0:T(8,128)(2,1)S(1)}, bf16[384,256]{1,0:T(8,128)(2,1)}, u32[]{:S(2)}) copy-start(bf16[384,256]{1,0:T(8,128)(2,1)} %constant.9.clone.right) | copy-start | bytes 589828
  0.6 17.5 %copy-start.1 = (bf16[256,256]{1,0:T(8,128)(2,1)S(1)}, bf16[256,256]{1,0:T(8,128)(2,1)}, u32[]{:S(2)}) copy-start(bf16[256,256]{1,0:T(8,128)(2,1)} %constant.8.clone.left) | copy-start | bytes 393220
  0.7 21.0 %copy-start.2 = (bf16[768,256]{1,0:T(8,128)(2,1)S(1)}, bf16[768,256]{1,0:T(8,128)(2,1)}, u32[]{:S(2)}) copy-start(bf16[768,256]{1,0:T(8,128)(2,1)} %constant.10.clone.turn) | copy-start | bytes 1179652
  0.7 21.0 %copy-start.3 = (bf16[128,768]{1,0:T(8,128)(2,1)S(1)}, bf16[128,768]{1,0:T(8,128)(2,1)}, u32[]{:S(2)}) copy-start(bf16[128,768]{1,0:T(8,128)(2,1)} %constant.11.clone.close) | copy-start | bytes 589828
  4.1 8.1 %collective-permute-start = (bf16[352,128]{1,0:T(8,128)(2,1)S(1)}, bf16[352,128]{1,0:T(8,128)(2,1)S(1)}, u32[]{:S(2)}, u32[]{:S(2)}) collective-permute-start(bf16[352,128]{1,0:T(8,128)(2,1)S(1)} %get-tuple-element.26), channel_id=1, source_target_pairs={{0,1},{1,0},{2,3},{3,2},{4,5},{5,4},{6,7},{7,6},{8,9},{9,8},{10,11... | collective-permute-start | bytes 270344 | tf_op jit(solution)/shard_map/ppermute | solution.py:36
  4.7 7.5 %collective-permute-start.2 = (bf16[352,128]{1,0:T(8,128)(2,1)S(1)}, bf16[352,128]{1,0:T(8,128)(2,1)S(1)}, u32[]{:S(2)}, u32[]{:S(2)}) collective-permute-start(bf16[352,128]{1,0:T(8,128)(2,1)S(1)} %get-tuple-element.28), channel_id=1, source_target_pairs={{0,3},{1,2},{2,1},{3,0},{4,7},{5,6},{6,5},{7,4},{8,11},{9,10},{10,... | collective-permute-start | bytes 270344 | tf_op jit(solution)/shard_map/ppermute | solution.py:36
  7.3 4.9 %collective-permute-start.1 = (bf16[320,128]{1,0:T(8,128)(2,1)S(1)}, bf16[320,128]{1,0:T(8,128)(2,1)S(1)}, u32[]{:S(2)}, u32[]{:S(2)}) collective-permute-start(bf16[320,128]{1,0:T(8,128)(2,1)S(1)} %get-tuple-element.27), channel_id=1, source_target_pairs={{0,2},{1,3},{2,0},{3,1},{4,6},{5,7},{6,4},{7,5},{8,10},{9,11},{10,... | collective-permute-start | bytes 245768 | tf_op jit(solution)/shard_map/ppermute | solution.py:36
  7.3 0.7 %copy-start.4 = (s32[1,4,8,3]{2,1,3,0:T(4,128)S(1)}, s32[1,4,8,3]{2,1,3,0:T(4,128)}, u32[]{:S(2)}) copy-start(s32[1,4,8,3]{2,1,3,0:T(4,128)} %param.11) | copy-start | bytes 1156
  8.0 0.7 %copy-start.5 = (f32[1,4,8]{2,1,0:T(4,128)S(1)}, f32[1,4,8]{2,1,0:T(4,128)}, u32[]{:S(2)}) copy-start(f32[1,4,8]{2,1,0:T(4,128)} %weight.1) | copy-start | bytes 388
  8.7 0.7 %copy-start.6 = (s32[1,4]{1,0:T(1,128)S(1)}, s32[1,4]{1,0:T(1,128)}, u32[]{:S(2)}) copy-start(s32[1,4]{1,0:T(1,128)} %pcol.1) | copy-start | bytes 52
  13.2 5.0 %collective-permute-start.3 = (bf16[128,128]{1,0:T(8,128)(2,1)S(1)}, bf16[128,128]{1,0:T(8,128)(2,1)S(1)}, u32[]{:S(2)}, u32[]{:S(2)}) collective-permute-start(bf16[128,128]{1,0:T(8,128)(2,1)S(1)} %get-tuple-element.31), channel_id=1, source_target_pairs={{0,8},{4,12},{8,0},{12,4},{1,9},{5,13},{9,1},{13,5},{2,10},{6,14},... | collective-permute-start | bytes 98312 | tf_op jit(solution)/shard_map/ppermute | solution.py:36
  15.9 5.7 %collective-permute-start.4 = (bf16[128,128]{1,0:T(8,128)(2,1)S(1)}, bf16[128,128]{1,0:T(8,128)(2,1)S(1)}, u32[]{:S(2)}, u32[]{:S(2)}) collective-permute-start(bf16[128,128]{1,0:T(8,128)(2,1)S(1)} %get-tuple-element.32), channel_id=1, source_target_pairs={{0,12},{4,8},{8,4},{12,0},{1,13},{5,9},{9,5},{13,1},{2,14},{6,10},... | collective-permute-start | bytes 98312 | tf_op jit(solution)/shard_map/ppermute | solution.py:36
  17.3 4.3 %collective-permute-start.5 = (bf16[128,128]{1,0:T(8,128)(2,1)S(1)}, bf16[128,128]{1,0:T(8,128)(2,1)S(1)}, u32[]{:S(2)}, u32[]{:S(2)}) collective-permute-start(bf16[128,128]{1,0:T(8,128)(2,1)S(1)} %get-tuple-element.33), channel_id=1, source_target_pairs={{0,4},{4,0},{8,12},{12,8},{1,5},{5,1},{9,13},{13,9},{2,6},{6,2},{1... | collective-permute-start | bytes 98312 | tf_op jit(solution)/shard_map/ppermute | solution.py:36

commit v6 on v5

--- a/solution.py
+++ b/solution.py
@@ -188,7 +188,20 @@
     return here - half * (pltpu.roll(right, BLOCK - 1, 1) - pltpu.roll(left, 1, 1))
 
 
-def plan_kernel(owners, secs, drift, weight, pcol, half_in, padded, acc, own, notes, shares):
+def plan_kernel(owners, secs, drift_at, weight_at, pcol_at, tables_at, half_in, padded, *refs):
+    acc, own, notes, shares = refs[:4]
+    drift, weight, pcol, tables, loaded = refs[8:]
+    copies = [
+        pltpu.make_async_copy(a, b, loaded.at[i])
+        for i, (a, b) in enumerate(
+            ((drift_at, drift), (weight_at, weight), (pcol_at, pcol), (tables_at, tables))
+        )
+    ]
+    for copy in copies:
+        copy.start()
+    for copy in copies:
+        copy.wait()
+    fill_tables(tables, *refs[4:8])
     blocks = padded.shape[0] - 2
     slab = blocks * BLOCK // secs
     band = lax.axis_index(BANDS)
@@ -407,19 +420,26 @@
 def dft_tables(length):
     indices = np.arange(length)
     angles = (indices[:, None] * indices[None, :] % length) * (2.0 * math.pi / length)
-    cosine, sine = np.cos(angles).astype(np.float32), np.sin(angles).astype(np.float32)
-    left = np.concatenate(halves(np.concatenate([cosine, sine], 0)), 1)
-    high, low = halves(np.concatenate([cosine, sine], 1))
-    right = np.concatenate([high, high, low], 0)
-    high, low = halves(
-        np.concatenate(
-            [np.concatenate([cosine, sine], 1), np.concatenate([-sine, cosine], 1)], 0
-        )
-    )
-    turn = np.concatenate([high, high, low], 0)
-    high, low = halves(np.concatenate([cosine, -sine], 1) / np.float32(length))
-    close = np.concatenate([high, high, low], 1)
-    return [jnp.asarray(t) for t in (left, right, turn, close)]
+    tables = np.concatenate([np.cos(angles), np.sin(angles)], 1).astype(np.float32)
+    return jnp.asarray(np.concatenate(halves(tables), 1))
+
+
+def fill_tables(tables, left, right, turn, close):
+    side = PATCH
+    parts = [tables[:, i * side : (i + 1) * side] for i in range(4)]
+    for part, (cosine, sine) in enumerate((parts[:2], parts[2:])):
+        left[:side, part * side : (part + 1) * side] = cosine
+        left[side:, part * side : (part + 1) * side] = sine
+        for at in (0, 1) if part == 0 else (2,):
+            right[at * side : (at + 1) * side, :side] = cosine
+            right[at * side : (at + 1) * side, side:] = sine
+            rows = 2 * side * at
+            turn[rows : rows + side, :side] = cosine
+            turn[rows : rows + side, side:] = sine
+            turn[rows + side : rows + 2 * side, :side] = -sine
+            turn[rows + side : rows + 2 * side, side:] = cosine
+            close[:, rows : rows + side] = cosine * (1.0 / side)
+            close[:, rows + side : rows + 2 * side] = -sine * (1.0 / side)
 
 
 def per_device(section_pixels, jitter_index, drift_list, blend_weight, patch_col):
@@ -462,20 +482,31 @@
         compiler_params=params,
         name="front",
     )(*map(in_hbm, (jitter_index, drifts, pixels)))
-    begun, own, notes, shares = pl.pallas_call(
+    begun, own, notes, shares, left, right, turn, close = pl.pallas_call(
         functools.partial(plan_kernel, owners, secs),
         out_shape=[
             shape((secs, PATCH, PATCH), f32),
             shape((CAP * BLOCK, BLOCK), bf16),
             pltpu.SMEM((owners * CAP * NOTE + 2 * secs,), jnp.int32),
             pltpu.SMEM((owners * CAP,), f32),
+            shape((2 * PATCH, 2 * PATCH), bf16),
+            shape((3 * PATCH, 2 * PATCH), bf16),
+            shape((6 * PATCH, 2 * PATCH), bf16),
+            shape((PATCH, 6 * PATCH), bf16),
         ],
-        in_specs=[smem, smem, smem, vmem, vmem],
-        out_specs=[vmem, vmem, smem, smem],
+        in_specs=[hbm] * 4 + [vmem] * 2,
+        out_specs=[vmem, vmem, smem, smem] + [vmem] * 4,
+        scratch_shapes=[
+            pltpu.SMEM(drifts.shape, jnp.int32),
+            pltpu.SMEM(blend_weight.shape, f32),
+            pltpu.SMEM(patch_col.shape, jnp.int32),
+            pltpu.VMEM((PATCH, 4 * PATCH), bf16),
+            pltpu.SemaphoreType.DMA((4,)),
+        ],
         compiler_params=params,
         cost_estimate=pl.CostEstimate(flops=10**8, bytes_accessed=10**6, transcendentals=0),
         name="plan",
-    )(drifts, blend_weight, patch_col, half, padded)
+    )(*map(in_hbm, (drifts, blend_weight, patch_col, dft_tables(PATCH))), half, padded)
     messages = [own] + [send(messages[k - 1], BANDS, k, owners) for k in range(1, owners)]
     jitter, *windows = pl.pallas_call(
         functools.partial(blend_kernel, owners, secs),
@@ -489,7 +520,6 @@
     )(in_smem(notes), in_smem(shares), jitter, edges, begun, *messages)
     order = patch_order(secs)
     windows = windows[:1] + [send(windows[k], "sec", k, secs) for k in order[1:]]
-    left, right, turn, close = dft_tables(PATCH)
     begin = secs // 2
     early = pl.pallas_call(
         spectrum_kernel,

time: 23.9 us -> 23.9 us (level)
  local copies, waits for them, and re-layouts: 2.05 us -> 0 us
  waiting for transfers between devices: 4.88 us -> 6.6 us
  Pallas kernels: 8.47 us -> 8.78 us
    unnamed x14 -> x0, local copies, waits for them, and re-layouts: 2.05 us -> none
    ppermute x6, waiting for transfers between devices: 4.88 us -> 6.6 us  [send(): return lax.ppermute(x, axis, [(i, target(i, k, n)) for i in range(n)])]
    pallas_call x1, Pallas kernels: 1.49 us -> 1.97 us  [per_device(): pl.pallas_call(functools.partial(plan_kernel, owners, secs), out_shape=[s...]
  transfers between devices with their start and end apart: 6 -> 6, of which waited for: 3 -> 3; matrix products, arithmetic and copies ran while one was open for 0% -> 0% of each run, Pallas kernels for 8% -> 10%
where the time goes in v6:
time: 23.9 us; the launch traced here: 23.6 us
  Pallas kernels  8.78 us (37%)
  starting transfers between devices  7.6 us (32%)
  waiting for transfers between devices  6.6 us (28%)
  between operations  0.66 us (3%)
    ppermute x6, starting transfers between devices, send(): return lax.ppermute(x, axis, [(i, target(i, k, n)) for i in range(n)])  7.6 us
    ppermute x6, waiting for transfers between devices, send(): return lax.ppermute(x, axis, [(i, target(i, k, n)) for i in range(n)])  6.6 us
    pallas_call x1, Pallas kernels, per_device(): pl.pallas_call(functools.partial(front_kernel, owners), out_shape=[shape(...  3.38 us
    pallas_call x1, Pallas kernels, per_device(): pl.pallas_call(functools.partial(surface_kernel, secs), out_shape=shape((...  2.03 us
    pallas_call x1, Pallas kernels, per_device(): pl.pallas_call(functools.partial(plan_kernel, owners, secs), out_shape=[s...  1.97 us
    pallas_call x1, Pallas kernels, per_device(): pl.pallas_call(functools.partial(blend_kernel, owners, secs), out_shape=[...  0.91 us
    pallas_call x1, Pallas kernels, per_device(): pl.pallas_call(spectrum_kernel, out_shape=shape((begin, 2, PATCH, PATCH),...  0.48 us
  transfers between devices with their start and end apart: 6, of which 3 were waited for; matrix products, arithmetic and copies ran while one was open for 0% of the time, Pallas kernels for 10%

profile of v6, /device:TPU:0, one launch (start us, length us, event | category | flops | bytes accessed | tf_op | source)
XLA Modules:
  0.0 23.6 jit_solution(3222613895729382637)
XLA Ops:
  0.6 3.4 %front.1 = (f32[1,128]{1,0:T(1,128)S(1)}, f32[128,128]{1,0:T(8,128)S(1)}, f32[34,144,128]{2,1,0:T(8,128)S(1)}, f32[2,32,128]{2,1,0:T(8,128)S(1)}, bf16[352,128]{...) custom-call(s32[1,128]{1,0:T(1,128)} %delay_at.1, s32[3,4,8]{2,1,0:T(4,128)} %bitcast.9, ...), custom_call_target="tpu_custom_call" | custom-call | tf_op jit(solution)/shard_map/front/pallas_call | solution.py:462
  4.0 0.5 %collective-permute-start = (bf16[352,128]{1,0:T(8,128)(2,1)S(1)}, bf16[352,128]{1,0:T(8,128)(2,1)S(1)}, u32[]{:S(2)}, u32[]{:S(2)}) collective-permute-start(bf16[352,128]{1,0:T(8,128)(2,1)S(1)} %get-tuple-element.30), channel_id=1, source_target_pairs={{0,1},{1,0},{2,3},{3,2},{4,5},{5,4},{6,7},{7,6},{8,9},{9,8},{10,11... | collective-permute-start | bytes 270344 | tf_op jit(solution)/shard_map/ppermute | solution.py:36
  4.5 2.6 %collective-permute-start.2 = (bf16[352,128]{1,0:T(8,128)(2,1)S(1)}, bf16[352,128]{1,0:T(8,128)(2,1)S(1)}, u32[]{:S(2)}, u32[]{:S(2)}) collective-permute-start(bf16[352,128]{1,0:T(8,128)(2,1)S(1)} %get-tuple-element.32), channel_id=1, source_target_pairs={{0,3},{1,2},{2,1},{3,0},{4,7},{5,6},{6,5},{7,4},{8,11},{9,10},{10,... | collective-permute-start | bytes 270344 | tf_op jit(solution)/shard_map/ppermute | solution.py:36
  7.2 0.0 collective-permute-start.1
  7.2 2.0 %plan.1 = (f32[4,128,128]{2,1,0:T(8,128)S(1)}, bf16[256,128]{1,0:T(8,128)(2,1)S(1)}, s32[48]{0:T(128)S(4)}, f32[8]{0:T(128)S(4)}, bf16[256,256]{1,0:T(8,128)(2,1...) custom-call(s32[3,4,8]{2,1,0:T(4,128)} %bitcast.10, ...), custom_call_target="tpu_custom_call" | custom-call | flops 100000000 | bytes 1000000 | tf_op jit(solution)/shard_map/plan/pallas_call | solution.py:485
  9.2 2.9 %collective-permute-done.1.refs_2_ = bf16[320,128]{1,0:T(8,128)(2,1)S(1)} collective-permute-done((bf16[320,128]{1,0:T(8,128)(2,1)S(1)}, bf16[320,128]{1,0:T(8,128)(2,1)S(1)}, u32[]{:S(2)}, u32[]{:S(2)}) %collective-permute-start.1) | collective-permute-done | bytes 81952 | tf_op jit(solution)/shard_map/ppermute | solution.py:36
  12.1 0.0 collective-permute-done.refs_1_
  12.1 0.0 collective-permute-done.2.refs_3_
  12.1 0.9 %blend.1 = (f32[1,128]{1,0:T(1,128)}, bf16[128,128]{1,0:T(8,128)(2,1)S(1)}, bf16[128,128]{1,0:T(8,128)(2,1)S(1)}, bf16[128,128]{1,0:T(8,128)(2,1)S(1)}, bf16[128,128]{1,0:T(8,128)(2,1)S(1)}) custom-call(s32[48]{0:T(128)S(4)} %get-tuple-element.24.notes, f32[8]{0:T(128)S(4)} %get-tuple-element.25.shares, f32[1,128]{1,0:T(1,128)S(1)} %get-tuple-element.26.jitter_in, ...), custom_call_target="tpu_custom_call" | custom-call | tf_op jit(solution)/shard_map/blend/pallas_call | solution.py:511
  13.0 2.9 %collective-permute-start.3 = (bf16[128,128]{1,0:T(8,128)(2,1)S(1)}, bf16[128,128]{1,0:T(8,128)(2,1)S(1)}, u32[]{:S(2)}, u32[]{:S(2)}) collective-permute-start(bf16[128,128]{1,0:T(8,128)(2,1)S(1)} %get-tuple-element.39), channel_id=1, source_target_pairs={{0,8},{4,12},{8,0},{12,4},{1,9},{5,13},{9,1},{13,5},{2,10},{6,14},... | collective-permute-start | bytes 98312 | tf_op jit(solution)/shard_map/ppermute | solution.py:36
  15.9 1.4 %collective-permute-start.4 = (bf16[128,128]{1,0:T(8,128)(2,1)S(1)}, bf16[128,128]{1,0:T(8,128)(2,1)S(1)}, u32[]{:S(2)}, u32[]{:S(2)}) collective-permute-start(bf16[128,128]{1,0:T(8,128)(2,1)S(1)} %get-tuple-element.40), channel_id=1, source_target_pairs={{0,12},{4,8},{8,4},{12,0},{1,13},{5,9},{9,5},{13,1},{2,14},{6,10},... | collective-permute-start | bytes 98312 | tf_op jit(solution)/shard_map/ppermute | solution.py:36
  17.3 0.1 collective-permute-start.5
  17.4 0.7 %collective-permute-done.3.refs_1_ = bf16[128,128]{1,0:T(8,128)(2,1)S(1)} collective-permute-done((bf16[128,128]{1,0:T(8,128)(2,1)S(1)}, bf16[128,128]{1,0:T(8,128)(2,1)S(1)}, u32[]{:S(2)}, u32[]{:S(2)}) %collective-permute-start.3) | collective-permute-done | bytes 32800 | tf_op jit(solution)/shard_map/ppermute | solution.py:36
  18.1 0.5 %spectrum.1.early = f32[2,2,128,128]{3,2,1,0:T(8,128)S(1)} custom-call(bf16[256,256]{1,0:T(8,128)(2,1)S(1)} %get-tuple-element.34.left, bf16[384,256]{1,0:T(8,128)(2,1)S(1)} %get-tuple-element.35.right, bf16[128,128]{1,0:T(8,128)(2,1)S(1)} %get-tuple-element.38.refs_0_, bf16[128,128]{1,0:T(8,128)(2,1)S(1)} %collective-permute-done.3.refs_1_), custom_call_target="tpu_custom_call" | custom-call | flops 100000000 | bytes 1000000 | tf_op jit(solution)/shard_map/spectrum/pallas_call | solution.py:524
  18.6 3.0 %collective-permute-done.4.refs_0_ = bf16[128,128]{1,0:T(8,128)(2,1)S(1)} collective-permute-done((bf16[128,128]{1,0:T(8,128)(2,1)S(1)}, bf16[128,128]{1,0:T(8,128)(2,1)S(1)}, u32[]{:S(2)}, u32[]{:S(2)}) %collective-permute-start.4) | collective-permute-done | bytes 32800 | tf_op jit(solution)/shard_map/ppermute | solution.py:36
  21.6 0.0 collective-permute-done.5.refs_1_
  21.6 2.0 %surface.1 = f32[3,128,128]{2,1,0:T(8,128)} custom-call(bf16[256,256]{1,0:T(8,128)(2,1)S(1)} %get-tuple-element.34.left, bf16[384,256]{1,0:T(8,128)(2,1)S(1)} %get-tuple-element.35.right, bf16[768,256]{1,0:T(8,128)(2,1)S(1)} %get-tuple-element.36.turn, bf16[128,768]{1,0:T(8,128)(2,1)S(1)} %get-tuple-element.37.close, f32[2,2,128,128]{3,2,1,0:T(8,128)S(1)} %spectrum.1.early, ...), custom_call_target="tpu_custom_call" | custom-call | tf_op jit(solution)/shard_map/surface/pallas_call | solution.py:533
Async XLA Ops:
  4.0 8.1 %collective-permute-start = (bf16[352,128]{1,0:T(8,128)(2,1)S(1)}, bf16[352,128]{1,0:T(8,128)(2,1)S(1)}, u32[]{:S(2)}, u32[]{:S(2)}) collective-permute-start(bf16[352,128]{1,0:T(8,128)(2,1)S(1)} %get-tuple-element.30), channel_id=1, source_target_pairs={{0,1},{1,0},{2,3},{3,2},{4,5},{5,4},{6,7},{7,6},{8,9},{9,8},{10,11... | collective-permute-start | bytes 270344 | tf_op jit(solution)/shard_map/ppermute | solution.py:36
  4.5 7.5 %collective-permute-start.2 = (bf16[352,128]{1,0:T(8,128)(2,1)S(1)}, bf16[352,128]{1,0:T(8,128)(2,1)S(1)}, u32[]{:S(2)}, u32[]{:S(2)}) collective-permute-start(bf16[352,128]{1,0:T(8,128)(2,1)S(1)} %get-tuple-element.32), channel_id=1, source_target_pairs={{0,3},{1,2},{2,1},{3,0},{4,7},{5,6},{6,5},{7,4},{8,11},{9,10},{10,... | collective-permute-start | bytes 270344 | tf_op jit(solution)/shard_map/ppermute | solution.py:36
  7.2 4.9 %collective-permute-start.1 = (bf16[320,128]{1,0:T(8,128)(2,1)S(1)}, bf16[320,128]{1,0:T(8,128)(2,1)S(1)}, u32[]{:S(2)}, u32[]{:S(2)}) collective-permute-start(bf16[320,128]{1,0:T(8,128)(2,1)S(1)} %get-tuple-element.31), channel_id=1, source_target_pairs={{0,2},{1,3},{2,0},{3,1},{4,6},{5,7},{6,4},{7,5},{8,10},{9,11},{10,... | collective-permute-start | bytes 245768 | tf_op jit(solution)/shard_map/ppermute | solution.py:36
  13.0 5.1 %collective-permute-start.3 = (bf16[128,128]{1,0:T(8,128)(2,1)S(1)}, bf16[128,128]{1,0:T(8,128)(2,1)S(1)}, u32[]{:S(2)}, u32[]{:S(2)}) collective-permute-start(bf16[128,128]{1,0:T(8,128)(2,1)S(1)} %get-tuple-element.39), channel_id=1, source_target_pairs={{0,8},{4,12},{8,0},{12,4},{1,9},{5,13},{9,1},{13,5},{2,10},{6,14},... | collective-permute-start | bytes 98312 | tf_op jit(solution)/shard_map/ppermute | solution.py:36
  15.9 5.7 %collective-permute-start.4 = (bf16[128,128]{1,0:T(8,128)(2,1)S(1)}, bf16[128,128]{1,0:T(8,128)(2,1)S(1)}, u32[]{:S(2)}, u32[]{:S(2)}) collective-permute-start(bf16[128,128]{1,0:T(8,128)(2,1)S(1)} %get-tuple-element.40), channel_id=1, source_target_pairs={{0,12},{4,8},{8,4},{12,0},{1,13},{5,9},{9,5},{13,1},{2,14},{6,10},... | collective-permute-start | bytes 98312 | tf_op jit(solution)/shard_map/ppermute | solution.py:36
  17.3 4.3 %collective-permute-start.5 = (bf16[128,128]{1,0:T(8,128)(2,1)S(1)}, bf16[128,128]{1,0:T(8,128)(2,1)S(1)}, u32[]{:S(2)}, u32[]{:S(2)}) collective-permute-start(bf16[128,128]{1,0:T(8,128)(2,1)S(1)} %get-tuple-element.41), channel_id=1, source_target_pairs={{0,4},{4,0},{8,12},{12,8},{1,5},{5,1},{9,13},{13,9},{2,6},{6,2},{1... | collective-permute-start | bytes 98312 | tf_op jit(solution)/shard_map/ppermute | solution.py:36

commit v7 on v6

--- a/solution.py
+++ b/solution.py
@@ -67,9 +67,9 @@
 
 
 def front_kernel(owners, delay_at, drift_at, pixels, *refs):
-    jitter_out, half_out, padded, first_out = refs[:4]
-    messages = refs[4 : 3 + owners]
-    raw, ring, wide, sums, delay, drift, loaded = refs[3 + owners :]
+    half_out, padded, first_out = refs[:3]
+    messages = refs[3 : 2 + owners]
+    raw, ring, wide, sums, delay, drift, loaded = refs[2 + owners :]
     rows, width = pixels.shape
     blocks = width // BLOCK
     bounds = [rows * part // 16 for part in CHUNKS]
@@ -164,7 +164,6 @@
             messages[k - 1][c * BLOCK : (c + 1) * BLOCK, :] = corrected(
                 padded, half, drift[0, band, place[c]]
             ).astype(jnp.bfloat16)
-    jitter_out[...] = jitter.T[0:1, :]
     for v in range(blocks):
         first_out[0, v : v + 1, :] = padded[v + 1, PAD : PAD + 1, :]
         first_out[1, v : v + 1, :] = padded[v + 1, PAD + rows - 1 : PAD + rows, :]
@@ -190,7 +189,7 @@
 
 def plan_kernel(owners, secs, drift_at, weight_at, pcol_at, tables_at, half_in, padded, *refs):
     acc, own, notes, shares = refs[:4]
-    drift, weight, pcol, tables, loaded = refs[8:]
+    jitter_out, drift, weight, pcol, tables, loaded = refs[8:]
     copies = [
         pltpu.make_async_copy(a, b, loaded.at[i])
         for i, (a, b) in enumerate(
@@ -206,6 +205,7 @@
     slab = blocks * BLOCK // secs
     band = lax.axis_index(BANDS)
     half = half_in[...]
+    jitter_out[...] = (2.0 * half).T[0:1, :]
     lane = lax.broadcasted_iota(jnp.int32, half.shape, 1)
     place, _ = find_slots(drift, band, band, drift.shape[2])
     for c in range(CAP):
@@ -459,17 +459,16 @@
         CAP * BLOCK + (3 if has_tail(k, owners) else 2) * blocks for k in range(1, owners)
     ]
     params = pltpu.CompilerParams(vmem_limit_bytes=24 * 1024 * 1024)
-    jitter, half, padded, edges, *messages = pl.pallas_call(
+    half, padded, edges, *messages = pl.pallas_call(
         functools.partial(front_kernel, owners),
         out_shape=[
-            shape((1, rows), f32),
             shape((rows, BLOCK), f32),
             shape((blocks + 2, rows + PAD, BLOCK), f32),
             shape((2, blocks, BLOCK), f32),
         ]
         + [shape((r, BLOCK), bf16) for r in message_rows],
         in_specs=[hbm] * 3,
-        out_specs=[vmem] * (3 + owners),
+        out_specs=[vmem] * (2 + owners),
         scratch_shapes=[
             pltpu.VMEM((rows, width), f32),
             pltpu.VMEM((blocks, rows + PAD, BLOCK), f32),
@@ -482,7 +481,7 @@
         compiler_params=params,
         name="front",
     )(*map(in_hbm, (jitter_index, drifts, pixels)))
-    begun, own, notes, shares, left, right, turn, close = pl.pallas_call(
+    begun, own, notes, shares, left, right, turn, close, jitter = pl.pallas_call(
         functools.partial(plan_kernel, owners, secs),
         out_shape=[
             shape((secs, PATCH, PATCH), f32),
@@ -493,9 +492,10 @@
             shape((3 * PATCH, 2 * PATCH), bf16),
             shape((6 * PATCH, 2 * PATCH), bf16),
             shape((PATCH, 6 * PATCH), bf16),
+            shape((1, rows), f32),
         ],
         in_specs=[hbm] * 4 + [vmem] * 2,
-        out_specs=[vmem, vmem, smem, smem] + [vmem] * 4,
+        out_specs=[vmem, vmem, smem, smem] + [vmem] * 5,
         scratch_shapes=[
             pltpu.SMEM(drifts.shape, jnp.int32),
             pltpu.SMEM(blend_weight.shape, f32),

time: 23.9 us -> 23.8 us (level)
  no operation moved by 1% of the time
where the time goes in v7:
time: 23.8 us; the launch traced here: 23.6 us
  Pallas kernels  8.67 us (36%)
  starting transfers between devices  7.74 us (33%)
  waiting for transfers between devices  6.56 us (28%)
  between operations  0.66 us (3%)
    ppermute x6, starting transfers between devices, send(): return lax.ppermute(x, axis, [(i, target(i, k, n)) for i in range(n)])  7.74 us
    ppermute x6, waiting for transfers between devices, send(): return lax.ppermute(x, axis, [(i, target(i, k, n)) for i in range(n)])  6.56 us
    pallas_call x1, Pallas kernels, per_device(): pl.pallas_call(functools.partial(front_kernel, owners), out_shape=[shape(...  3.37 us
    pallas_call x1, Pallas kernels, per_device(): pl.pallas_call(functools.partial(surface_kernel, secs), out_shape=shape((...  2.03 us
    pallas_call x1, Pallas kernels, per_device(): pl.pallas_call(functools.partial(plan_kernel, owners, secs), out_shape=[s...  1.97 us
    pallas_call x1, Pallas kernels, per_device(): pl.pallas_call(functools.partial(blend_kernel, owners, secs), out_shape=[...  0.81 us
    pallas_call x1, Pallas kernels, per_device(): pl.pallas_call(spectrum_kernel, out_shape=shape((begin, 2, PATCH, PATCH),...  0.48 us
  transfers between devices with their start and end apart: 6, of which 3 were waited for; matrix products, arithmetic and copies ran while one was open for 0% of the time, Pallas kernels for 10%

profile of v7, /device:TPU:0, one launch (start us, length us, event | category | flops | bytes accessed | tf_op | source)
XLA Modules:
  0.0 23.6 jit_solution(10578532296057880169)
XLA Ops:
  0.6 3.4 %front.1 = (f32[128,128]{1,0:T(8,128)S(1)}, f32[34,144,128]{2,1,0:T(8,128)S(1)}, f32[2,32,128]{2,1,0:T(8,128)S(1)}, bf16[352,128]{1,0:T(8,128)(2,1)S(1)}, bf16[3...) custom-call(s32[1,128]{1,0:T(1,128)} %delay_at.1, s32[3,4,8]{2,1,0:T(4,128)} %bitcast.9, f32[128,4096]{1,0:T(8,128)} %bitcast.7), custom_call_target="tpu_custom_call" | custom-call | tf_op jit(solution)/shard_map/front/pallas_call | solution.py:462
  4.0 0.5 %collective-permute-start = (bf16[352,128]{1,0:T(8,128)(2,1)S(1)}, bf16[352,128]{1,0:T(8,128)(2,1)S(1)}, u32[]{:S(2)}, u32[]{:S(2)}) collective-permute-start(bf16[352,128]{1,0:T(8,128)(2,1)S(1)} %get-tuple-element.30), channel_id=1, source_target_pairs={{0,1},{1,0},{2,3},{3,2},{4,5},{5,4},{6,7},{7,6},{8,9},{9,8},{10,11... | collective-permute-start | bytes 270344 | tf_op jit(solution)/shard_map/ppermute | solution.py:36
  4.5 2.6 %collective-permute-start.2 = (bf16[352,128]{1,0:T(8,128)(2,1)S(1)}, bf16[352,128]{1,0:T(8,128)(2,1)S(1)}, u32[]{:S(2)}, u32[]{:S(2)}) collective-permute-start(bf16[352,128]{1,0:T(8,128)(2,1)S(1)} %get-tuple-element.32), channel_id=1, source_target_pairs={{0,3},{1,2},{2,1},{3,0},{4,7},{5,6},{6,5},{7,4},{8,11},{9,10},{10,... | collective-permute-start | bytes 270344 | tf_op jit(solution)/shard_map/ppermute | solution.py:36
  7.1 0.0 collective-permute-start.1
  7.2 2.0 %plan.1 = (f32[4,128,128]{2,1,0:T(8,128)S(1)}, bf16[256,128]{1,0:T(8,128)(2,1)S(1)}, s32[48]{0:T(128)S(4)}, f32[8]{0:T(128)S(4)}, bf16[256,256]{1,0:T(8,128)(2,1...) custom-call(s32[3,4,8]{2,1,0:T(4,128)} %bitcast.10, ...), custom_call_target="tpu_custom_call" | custom-call | flops 100000000 | bytes 1000000 | tf_op jit(solution)/shard_map/plan/pallas_call | solution.py:484
  9.2 2.9 %collective-permute-done.1.refs_2_ = bf16[320,128]{1,0:T(8,128)(2,1)S(1)} collective-permute-done((bf16[320,128]{1,0:T(8,128)(2,1)S(1)}, bf16[320,128]{1,0:T(8,128)(2,1)S(1)}, u32[]{:S(2)}, u32[]{:S(2)}) %collective-permute-start.1) | collective-permute-done | bytes 81952 | tf_op jit(solution)/shard_map/ppermute | solution.py:36
  12.1 0.0 collective-permute-done.refs_1_
  12.1 0.0 collective-permute-done.2.refs_3_
  12.1 0.8 %blend.1 = (f32[1,128]{1,0:T(1,128)}, bf16[128,128]{1,0:T(8,128)(2,1)S(1)}, bf16[128,128]{1,0:T(8,128)(2,1)S(1)}, bf16[128,128]{1,0:T(8,128)(2,1)S(1)}, bf16[128,128]{1,0:T(8,128)(2,1)S(1)}) custom-call(s32[48]{0:T(128)S(4)} %get-tuple-element.24.notes, f32[8]{0:T(128)S(4)} %get-tuple-element.25.shares, f32[1,128]{1,0:T(1,128)S(1)} %get-tuple-element.26.jitter_in, ...), custom_call_target="tpu_custom_call" | custom-call | tf_op jit(solution)/shard_map/blend/pallas_call | solution.py:511
  12.9 3.0 %collective-permute-start.3 = (bf16[128,128]{1,0:T(8,128)(2,1)S(1)}, bf16[128,128]{1,0:T(8,128)(2,1)S(1)}, u32[]{:S(2)}, u32[]{:S(2)}) collective-permute-start(bf16[128,128]{1,0:T(8,128)(2,1)S(1)} %get-tuple-element.39), channel_id=1, source_target_pairs={{0,8},{4,12},{8,0},{12,4},{1,9},{5,13},{9,1},{13,5},{2,10},{6,14},... | collective-permute-start | bytes 98312 | tf_op jit(solution)/shard_map/ppermute | solution.py:36
  15.9 1.5 %collective-permute-start.4 = (bf16[128,128]{1,0:T(8,128)(2,1)S(1)}, bf16[128,128]{1,0:T(8,128)(2,1)S(1)}, u32[]{:S(2)}, u32[]{:S(2)}) collective-permute-start(bf16[128,128]{1,0:T(8,128)(2,1)S(1)} %get-tuple-element.40), channel_id=1, source_target_pairs={{0,12},{4,8},{8,4},{12,0},{1,13},{5,9},{9,5},{13,1},{2,14},{6,10},... | collective-permute-start | bytes 98312 | tf_op jit(solution)/shard_map/ppermute | solution.py:36
  17.3 0.1 collective-permute-start.5
  17.4 0.6 %collective-permute-done.3.refs_1_ = bf16[128,128]{1,0:T(8,128)(2,1)S(1)} collective-permute-done((bf16[128,128]{1,0:T(8,128)(2,1)S(1)}, bf16[128,128]{1,0:T(8,128)(2,1)S(1)}, u32[]{:S(2)}, u32[]{:S(2)}) %collective-permute-start.3) | collective-permute-done | bytes 32800 | tf_op jit(solution)/shard_map/ppermute | solution.py:36
  18.0 0.5 %spectrum.1.early = f32[2,2,128,128]{3,2,1,0:T(8,128)S(1)} custom-call(bf16[256,256]{1,0:T(8,128)(2,1)S(1)} %get-tuple-element.34.left, bf16[384,256]{1,0:T(8,128)(2,1)S(1)} %get-tuple-element.35.right, bf16[128,128]{1,0:T(8,128)(2,1)S(1)} %get-tuple-element.38.refs_0_, bf16[128,128]{1,0:T(8,128)(2,1)S(1)} %collective-permute-done.3.refs_1_), custom_call_target="tpu_custom_call" | custom-call | flops 100000000 | bytes 1000000 | tf_op jit(solution)/shard_map/spectrum/pallas_call | solution.py:524
  18.5 3.1 %collective-permute-done.4.refs_0_ = bf16[128,128]{1,0:T(8,128)(2,1)S(1)} collective-permute-done((bf16[128,128]{1,0:T(8,128)(2,1)S(1)}, bf16[128,128]{1,0:T(8,128)(2,1)S(1)}, u32[]{:S(2)}, u32[]{:S(2)}) %collective-permute-start.4) | collective-permute-done | bytes 32800 | tf_op jit(solution)/shard_map/ppermute | solution.py:36
  21.6 0.0 collective-permute-done.5.refs_1_
  21.6 2.0 %surface.1 = f32[3,128,128]{2,1,0:T(8,128)} custom-call(bf16[256,256]{1,0:T(8,128)(2,1)S(1)} %get-tuple-element.34.left, bf16[384,256]{1,0:T(8,128)(2,1)S(1)} %get-tuple-element.35.right, bf16[768,256]{1,0:T(8,128)(2,1)S(1)} %get-tuple-element.36.turn, bf16[128,768]{1,0:T(8,128)(2,1)S(1)} %get-tuple-element.37.close, f32[2,2,128,128]{3,2,1,0:T(8,128)S(1)} %spectrum.1.early, ...), custom_call_target="tpu_custom_call" | custom-call | tf_op jit(solution)/shard_map/surface/pallas_call | solution.py:533
Async XLA Ops:
  4.0 8.1 %collective-permute-start = (bf16[352,128]{1,0:T(8,128)(2,1)S(1)}, bf16[352,128]{1,0:T(8,128)(2,1)S(1)}, u32[]{:S(2)}, u32[]{:S(2)}) collective-permute-start(bf16[352,128]{1,0:T(8,128)(2,1)S(1)} %get-tuple-element.30), channel_id=1, source_target_pairs={{0,1},{1,0},{2,3},{3,2},{4,5},{5,4},{6,7},{7,6},{8,9},{9,8},{10,11... | collective-permute-start | bytes 270344 | tf_op jit(solution)/shard_map/ppermute | solution.py:36
  4.5 7.5 %collective-permute-start.2 = (bf16[352,128]{1,0:T(8,128)(2,1)S(1)}, bf16[352,128]{1,0:T(8,128)(2,1)S(1)}, u32[]{:S(2)}, u32[]{:S(2)}) collective-permute-start(bf16[352,128]{1,0:T(8,128)(2,1)S(1)} %get-tuple-element.32), channel_id=1, source_target_pairs={{0,3},{1,2},{2,1},{3,0},{4,7},{5,6},{6,5},{7,4},{8,11},{9,10},{10,... | collective-permute-start | bytes 270344 | tf_op jit(solution)/shard_map/ppermute | solution.py:36
  7.1 4.9 %collective-permute-start.1 = (bf16[320,128]{1,0:T(8,128)(2,1)S(1)}, bf16[320,128]{1,0:T(8,128)(2,1)S(1)}, u32[]{:S(2)}, u32[]{:S(2)}) collective-permute-start(bf16[320,128]{1,0:T(8,128)(2,1)S(1)} %get-tuple-element.31), channel_id=1, source_target_pairs={{0,2},{1,3},{2,0},{3,1},{4,6},{5,7},{6,4},{7,5},{8,10},{9,11},{10,... | collective-permute-start | bytes 245768 | tf_op jit(solution)/shard_map/ppermute | solution.py:36
  12.9 5.2 %collective-permute-start.3 = (bf16[128,128]{1,0:T(8,128)(2,1)S(1)}, bf16[128,128]{1,0:T(8,128)(2,1)S(1)}, u32[]{:S(2)}, u32[]{:S(2)}) collective-permute-start(bf16[128,128]{1,0:T(8,128)(2,1)S(1)} %get-tuple-element.39), channel_id=1, source_target_pairs={{0,8},{4,12},{8,0},{12,4},{1,9},{5,13},{9,1},{13,5},{2,10},{6,14},... | collective-permute-start | bytes 98312 | tf_op jit(solution)/shard_map/ppermute | solution.py:36
  15.9 5.7 %collective-permute-start.4 = (bf16[128,128]{1,0:T(8,128)(2,1)S(1)}, bf16[128,128]{1,0:T(8,128)(2,1)S(1)}, u32[]{:S(2)}, u32[]{:S(2)}) collective-permute-start(bf16[128,128]{1,0:T(8,128)(2,1)S(1)} %get-tuple-element.40), channel_id=1, source_target_pairs={{0,12},{4,8},{8,4},{12,0},{1,13},{5,9},{9,5},{13,1},{2,14},{6,10},... | collective-permute-start | bytes 98312 | tf_op jit(solution)/shard_map/ppermute | solution.py:36
  17.3 4.3 %collective-permute-start.5 = (bf16[128,128]{1,0:T(8,128)(2,1)S(1)}, bf16[128,128]{1,0:T(8,128)(2,1)S(1)}, u32[]{:S(2)}, u32[]{:S(2)}) collective-permute-start(bf16[128,128]{1,0:T(8,128)(2,1)S(1)} %get-tuple-element.41), channel_id=1, source_target_pairs={{0,4},{4,0},{8,12},{12,8},{1,5},{5,1},{9,13},{13,9},{2,6},{6,2},{1... | collective-permute-start | bytes 98312 | tf_op jit(solution)/shard_map/ppermute | solution.py:36
